TPU v7x, 32 devices: a whole 2x2x4 slice. The times are simulated.
32 devices in a mesh: col: 4 (over x, core), row: 8 (over z, y).
Axes of the slice: x: 2, y: 2, z: 4, core: 2. Of those that a mesh axis runs over, the one named last changes fastest.
Arguments:
- drive: float32 [8192], P(('col', 'row')), may hold values from -6 to 6
- resist: float32 [8192], P(('col', 'row')), may hold values from 1 to 4
- centers: float32 [3, 8192], P(None, 'col'), may hold values from 0 to 1
- tangents: float32 [3, 8192], P(None, 'col'), may hold values from -5 to 5
- iron_points: float32 [3, 65536], P(None, ('col', 'row')), may hold values from 0 to 1
- owner: int32 [65536, 1], P(('col', 'row')), may hold values from 0 to 7; in each aligned block of 2048 rows (0 to 2047, 2048 to 4095, ...) at most 512 rows name the same one
- range_len: int32 [8], replicated, may hold values from 256 to 1024, as said below
Outputs:
- currents: float32 [8192], P(('col', 'row'))
- iron_field: float32 [3, 65536], P(None, ('col', 'row'))
Inputs may be any that keep to these rules, and one draw needn't show every extreme that they name: `owner`: the 2048 points of one device name each block at most 512 times, and in every draw some device names some block exactly 512 times. `range_len`: some block has all 1024 segments active.
All inputs are finite; a program needn't handle non-finite values.
Results may differ from a plain program's by a relative error of at most 0.0003.
Values sent between devices are 32-bit elements; how exact they have to be, the bound alone decides.
No kernel may reach another device: no remote copies, remote signals or barrier semaphores. Data moves between devices by JAX's collectives and lax.ppermute only.
A program may use at most 64 MiB of HBM per device.

v0:
```python
import functools
import math

import jax
import jax.numpy as jnp
from jax import lax
from jax.experimental import pallas as pl
from jax.experimental.pallas import tpu as pltpu
from jax.sharding import PartitionSpec as P

EPS_SEG = 0.0004
EPS_FIELD = 0.0025
AXES = ("col", "row")
CHUNK = 128
GROUP = 4
TILE = 512
KEEP_BYTES = 16 * 1024 * 1024
VMEM_LIMIT = 32 * 1024 * 1024
STREAM_LIMIT = 44 * 1024 * 1024
STREAM_BYTES = 20 * 1024 * 1024
ENTRY_LIMIT = 60 * 1024 * 1024


def split3(x):
    high = x.astype(jnp.bfloat16).astype(jnp.float32)
    rest = x - high
    middle = rest.astype(jnp.bfloat16).astype(jnp.float32)
    low = (rest - middle).astype(jnp.bfloat16).astype(jnp.float32)
    return high, middle, low


def left_parts(x):
    high, middle, low = split3(x)
    return jnp.concatenate([high, high, middle, middle, high, low], axis=0)


def right_parts(x):
    high, middle, low = split3(x)
    return jnp.concatenate([high, middle, high, middle, low, high], axis=0).astype(jnp.bfloat16)


def rows8(*rows):
    width = rows[0].shape[1]
    count = sum(r.shape[0] for r in rows)
    if count < 8:
        rows = rows + (jnp.zeros((8 - count, width), jnp.float32),)
    return jnp.concatenate(rows, axis=0)


def left_center(c, eps):
    square = jnp.sum(c * c, axis=0, keepdims=True)
    return rows8(-2.0 * c, jnp.ones_like(square), square + eps)


def right_center(c):
    square = jnp.sum(c * c, axis=0, keepdims=True)
    return rows8(c, square, jnp.ones_like(square))


def dot(a, b):
    return jnp.dot(a, b, preferred_element_type=jnp.float32)


def dot_nt(a, b):
    return lax.dot_general(a, b, (((1,), (1,)), ((), ())), preferred_element_type=jnp.float32)


def transposed(x):
    return x.T.astype(jnp.bfloat16)


def fold_lanes(x):
    total = x[:, 0:128]
    for piece in range(1, x.shape[1] // 128):
        total = total + x[:, piece * 128:(piece + 1) * 128]
    return total


def iota(shape, axis):
    return lax.broadcasted_iota(jnp.int32, shape, axis)


def aligned(start, size):
    return pl.ds(pl.multiple_of(start, size), size)


def piece_column(shift, n_col):
    return lax.rem(lax.axis_index("col") + n_col - shift, n_col)


def couple(pieces, vec_ref, acc_ref, kept=None, right_ref=None, moment_ref=None):
    seg_dev = acc_ref.shape[0]
    n_col = len(pieces)
    length = pieces[0].shape[1]
    own = pieces[0][:, aligned(lax.axis_index("row") * seg_dev, seg_dev)]
    lc = transposed(left_parts(left_center(own[0:3] - 0.5, EPS_SEG)))
    lt = transposed(left_parts(rows8(own[3:6])))
    acc_ref[...] = jnp.zeros_like(acc_ref)
    count = length // TILE
    for shift, piece in enumerate(pieces):
        col = piece_column(shift, n_col)

        def step(k, carry):
            geo = piece[:, aligned(k * TILE, TILE)]
            vec_at = pl.ds(pl.multiple_of(col * length + k * TILE, TILE), TILE)
            center, tangent = geo[0:3] - 0.5, geo[3:6]
            rc = right_parts(right_center(center))
            rt = right_parts(rows8(tangent))
            pair = dot(lt, rt) * lax.rsqrt(dot(lc, rc))
            if kept is not None:
                kept[0][shift * count + k] = pair
                kept_copy(kept, shift * count + k, out=True).start()
            if right_ref is not None:
                cross = jnp.concatenate([
                    tangent[1:2] * center[2:3] - tangent[2:3] * center[1:2],
                    tangent[2:3] * center[0:1] - tangent[0:1] * center[2:3],
                    tangent[0:1] * center[1:2] - tangent[1:2] * center[0:1],
                ], axis=0)
                both = rows8(tangent, cross)
                for part in range(TILE // seg_dev):
                    row = k * (TILE // seg_dev) + part
                    block_at = aligned((row * n_col + col) * seg_dev, seg_dev)
                    right_ref[:, block_at] = rc[:, part * seg_dev:(part + 1) * seg_dev]
                    moment_ref[:, block_at] = both[:, part * seg_dev:(part + 1) * seg_dev]
            acc_ref[...] += fold_lanes(pair * vec_ref[:, vec_at])
            return carry

        lax.fori_loop(0, count, step, 0, unroll=4)
    return jnp.sum(acc_ref[...].T, axis=0, keepdims=True)


def kept_copy(kept, index, out):
    local, remote, sems = kept
    if out:
        return pltpu.make_async_copy(local.at[index], remote.at[index], sems.at[index])
    return pltpu.make_async_copy(remote.at[index], local.at[index], sems.at[index])


def couple_kept(kept, vec_ref, acc_ref, n_col):
    acc_ref[...] = jnp.zeros_like(acc_ref)
    length = vec_ref.shape[1] // n_col
    count = length // TILE
    for shift in range(n_col):
        col = piece_column(shift, n_col)

        def step(k, carry):
            kept_copy(kept, shift * count + k, out=False).wait()
            vec_at = pl.ds(pl.multiple_of(col * length + k * TILE, TILE), TILE)
            acc_ref[...] += fold_lanes(kept[0][shift * count + k] * vec_ref[:, vec_at])
            return carry

        lax.fori_loop(0, count, step, 0, unroll=2)
    return jnp.sum(acc_ref[...].T, axis=0, keepdims=True)


def spread_rows(ref, row):
    for k in range(ref.shape[0]):
        ref[k] = row


def entry_kernel(drive_hbm, centers_hbm, tangents_hbm, spread_ref, geo_ref, drive_ref, centers, tangents, sems):
    pairs = ((drive_hbm, drive_ref), (centers_hbm, centers), (tangents_hbm, tangents))
    copies = [pltpu.make_async_copy(source, target, sems.at[k]) for k, (source, target) in enumerate(pairs)]
    for copy in copies:
        copy.start()
    for copy in copies:
        copy.wait()
    spread_rows(spread_ref, drive_ref[...])
    geo_ref[0:3] = centers[...]
    geo_ref[3:6] = tangents[...]


def first_kernel(coupling, n_col, keep, drive_ref, drive_own_ref, resist_ref, after_ref, *refs):
    pieces, refs = refs[:n_col], refs[n_col:]
    image_ref, spread_ref, right_ref, moment_ref = refs[0:4]
    kept = None
    if keep:
        kept_hbm = refs[4]
        vec_ref, acc_ref, kept_ref, sems = refs[5:]
        kept = (kept_ref, kept_hbm, sems)
    else:
        vec_ref, acc_ref = refs[4:]
    drive = drive_ref[...]
    scale = 1.0 / jnp.sqrt(jnp.sum(drive * drive, keepdims=True))
    vec_ref[...] = drive * scale
    product = couple(pieces, vec_ref, acc_ref, kept, right_ref, moment_ref)
    image = resist_ref[...] * (drive_own_ref[...] * scale) + coupling * product
    image_ref[...] = image
    spread_rows(spread_ref, image)
    if keep:
        for index in range(kept_ref.shape[0]):
            kept_copy(kept, index, out=True).wait()


def second_kernel(coupling, n_col, keep, drive_ref, image_ref, drive_own_ref, image_own_ref, resist_ref, after_ref, *refs):
    if keep:
        kept_hbm, refs = refs[0], refs[1:]
        vec_ref, acc_ref, kept_ref, sems = refs[4:]
        kept = (kept_ref, kept_hbm, sems)
        for index in range(kept_ref.shape[0]):
            kept_copy(kept, index, out=False).start()
    else:
        pieces, refs = refs[:n_col], refs[n_col:]
        vec_ref, acc_ref = refs[4:]
    basis_ref, basis_own_ref, stats_ref, known_ref = refs[0:4]
    drive = drive_ref[...]
    norm = jnp.sqrt(jnp.sum(drive * drive, keepdims=True))
    scale = 1.0 / norm
    basis_a = drive * scale
    image = image_ref[...]
    hessen_a = jnp.sum(image * basis_a, keepdims=True)
    rest = image - hessen_a * basis_a
    hessen_b = jnp.sqrt(jnp.sum(rest * rest, keepdims=True))
    inverse = 1.0 / hessen_b
    basis_b = rest * inverse
    vec_ref[...] = basis_b
    basis_ref[0:1, :] = basis_a
    basis_ref[1:2, :] = basis_b
    own_a = drive_own_ref[...] * scale
    own_b = (image_own_ref[...] - hessen_a * own_a) * inverse
    basis_own_ref[0:1, :] = own_a
    basis_own_ref[1:2, :] = own_b
    if keep:
        product = couple_kept(kept, vec_ref, acc_ref, n_col)
    else:
        product = couple(pieces, vec_ref, acc_ref)
    second = resist_ref[...] * own_b + coupling * product
    lane = iota((1, 128), 1)

    def three(a, b, c):
        return jnp.where(lane == 0, a, jnp.where(lane == 1, b, jnp.where(lane == 2, c, 0.0)))

    spread_rows(stats_ref, three(
        jnp.sum(second * own_a, keepdims=True),
        jnp.sum(second * own_b, keepdims=True),
        jnp.sum(second * second, keepdims=True),
    ))
    known_ref[...] = three(norm, hessen_a, hessen_b)


def group_kernel(owner_ref, points_ref, drive_in_ref, resist_in_ref, centers_in_ref, tangents_in_ref,
                 slot_ref, table_ref, left_ref, drive_ref, resist_ref, geo_ref, planes_ref, *, n_row):
    drive_ref[...] = drive_in_ref[...]
    resist_ref[...] = resist_in_ref[...]
    geo_ref[0:3] = centers_in_ref[...]
    geo_ref[3:6] = tangents_in_ref[...]
    points = owner_ref.shape[1]
    chunk_count = left_ref.shape[0] // CHUNK
    owner = owner_ref[...]
    rows = max(8, n_row)
    marks = jnp.where(iota((rows, points), 0) == owner, 1.0, 0.0)
    tile = 256
    upper = jnp.where(iota((tile, tile), 0) <= iota((tile, tile), 1), 1.0, 0.0).astype(jnp.bfloat16)
    before = jnp.zeros((rows, 1), jnp.float32)
    ranks = []
    for piece in range(points // tile):
        part = dot(marks[:, piece * tile:(piece + 1) * tile].astype(jnp.bfloat16), upper)
        ranks.append(part + before - 1.0)
        before = before + part[:, tile - 1:tile]
    ranks = jnp.concatenate(ranks, axis=1)
    chunks = jnp.floor((before + (CHUNK - 1)) * (1.0 / CHUNK))
    start = jnp.zeros((1, 1), jnp.float32)
    starts = []
    for name in range(rows):
        starts.append(start)
        start = start + chunks[name:name + 1]
    starts = jnp.concatenate(starts, axis=0)
    slot = jnp.sum(marks * (ranks + starts * CHUNK), axis=0, keepdims=True).astype(jnp.int32)
    slot_ref[...] = slot
    lane = iota((rows, 128), 1)
    ended = jnp.sum(jnp.where(starts + chunks <= lane.astype(jnp.float32), 1.0, 0.0), axis=0, keepdims=True)
    block = jnp.minimum(ended, n_row - 1.0)
    place = iota((8, 128), 0)
    table_ref[...] = jnp.where(place == 0, block, start).astype(jnp.int32)
    high = jnp.where(iota((chunk_count, points), 0) == slot // CHUNK, 1.0, 0.0)
    low = jnp.where(iota((CHUNK, points), 0) == slot % CHUNK, 1.0, 0.0).astype(jnp.bfloat16)
    parts = split3(points_ref[...] - 0.5)
    spread = jnp.concatenate([high * part[k:k + 1] for k in range(3) for part in parts], axis=0).astype(jnp.bfloat16)
    placed = dot_nt(spread, low)
    planes = [placed[k * chunk_count:(k + 1) * chunk_count] for k in range(9)]
    x, y, z = (planes[3 * k] + planes[3 * k + 1] + planes[3 * k + 2] for k in range(3))
    sides = [-2.0 * x, -2.0 * y, -2.0 * z, jnp.ones_like(x), x * x + y * y + z * z + EPS_FIELD]
    sides = [split3(side) for side in sides]
    empty = jnp.zeros_like(x)
    for group, part in enumerate([0, 0, 1, 1, 0, 2]):
        for k in range(8):
            to = pl.ds((group * 8 + k) * chunk_count, chunk_count)
            planes_ref[to, :] = sides[k][part] if k < 5 else empty
    for chunk in range(chunk_count):
        left_ref[chunk * CHUNK:(chunk + 1) * CHUNK, :] = transposed(planes_ref[pl.ds(chunk, 48, stride=chunk_count), :])


def cube_halves(left, right):
    inverse = lax.rsqrt(dot(left, right))
    cube = inverse * inverse * inverse
    high = cube.astype(jnp.bfloat16)
    return high, (cube - high.astype(jnp.float32)).astype(jnp.bfloat16)


def weigh_kernel(group_ref, left_ref, right_ref, cubes_hbm, done_ref, cubes_ref, sems, *, n_row):
    width = right_ref.shape[1] // n_row
    done_ref[...] = jnp.zeros_like(done_ref)
    kept = (cubes_ref, cubes_hbm, sems)
    steps = (group_ref[1, 0] + GROUP - 1) // GROUP

    def step(k, carry):
        for part in range(GROUP):
            chunk = k * GROUP + part
            block_at = aligned(group_ref[0, chunk] * width, width)
            high, low = cube_halves(left_ref[aligned(chunk * CHUNK, CHUNK), :], right_ref[:, block_at])
            cubes_ref[chunk, 0:CHUNK] = high
            cubes_ref[chunk, CHUNK:2 * CHUNK] = low
            kept_copy(kept, chunk, out=True).start()
        return carry

    def finish(k, carry):
        for part in range(GROUP):
            kept_copy(kept, k * GROUP + part, out=True).wait()
        return carry

    lax.fori_loop(0, steps, step, 0)
    lax.fori_loop(0, steps, finish, 0)


def field_kernel(group_ref, length_ref, slot_ref, moment_ref, basis_ref, *refs, n_row, n_col, keep):
    chunk_count = refs[-1].shape[0] // 16 if not keep else refs[-3].shape[0] // 16
    steps = (group_ref[1, 0] + GROUP - 1) // GROUP
    if keep:
        cubes_hbm, out_ref, table_ref, sums_ref, cubes_ref, sems = refs
        kept = (cubes_ref, cubes_hbm, sems)

        def begin(k, carry):
            for part in range(GROUP):
                kept_copy(kept, k * GROUP + part, out=False).start()
            return carry

        lax.fori_loop(0, steps, begin, 0)
    else:
        left_ref, right_ref, out_ref, table_ref, sums_ref = refs
    segments = moment_ref.shape[1]
    width = segments // n_row
    seg_dev = width // n_col
    scale = 1.0 / math.sqrt(width)
    lane = iota((1, seg_dev), 1)
    sums_ref[...] = jnp.zeros_like(sums_ref)

    def table_step(block, carry):
        length = length_ref[block]
        for col in range(n_col):
            vec_at = aligned((col * n_row + block) * seg_dev, seg_dev)
            block_at = aligned((block * n_col + col) * seg_dev, seg_dev)
            both = moment_ref[:, block_at]
            active = jnp.where(lane + col * seg_dev < length, scale, 0.0)
            first = both * (basis_ref[0:1, vec_at] * active)
            second = both * (basis_ref[1:2, vec_at] * active)
            parts = jnp.concatenate([first, second], axis=0)
            high = parts.astype(jnp.bfloat16).astype(jnp.float32)
            table_ref[:, block_at] = jnp.concatenate([high, parts - high], axis=0).astype(jnp.bfloat16)
        return carry

    lax.fori_loop(0, n_row, table_step, 0, unroll=2)

    def step(k, carry):
        for part in range(GROUP):
            chunk = k * GROUP + part
            block_at = aligned(group_ref[0, chunk] * width, width)
            if keep:
                kept_copy(kept, chunk, out=False).wait()
                cubes = cubes_ref[chunk]
            else:
                high, low = cube_halves(left_ref[aligned(chunk * CHUNK, CHUNK), :], right_ref[:, block_at])
                cubes = jnp.concatenate([high, low], axis=0)
            both = dot_nt(cubes, table_ref[:, block_at])
            total = (both[0:CHUNK] + both[CHUNK:2 * CHUNK]).T
            sums_ref[pl.ds(chunk, 16, stride=chunk_count), :] = total[0:16] + total[16:32]
        return carry

    lax.fori_loop(0, steps, step, 0)
    sums = jnp.concatenate([sums_ref[0:6 * chunk_count], sums_ref[8 * chunk_count:14 * chunk_count]], axis=0)
    sums = jnp.concatenate(split3(sums), axis=1).astype(jnp.bfloat16)
    for tile in range(slot_ref.shape[1] // TILE):
        at = pl.ds(tile * TILE, TILE)
        slot = slot_ref[:, at]
        low = jnp.where(iota((CHUNK, TILE), 0) == slot % CHUNK, 1.0, 0.0).astype(jnp.bfloat16)
        high = jnp.where(iota((chunk_count, TILE), 0) == slot // CHUNK, 1.0, 0.0)
        found = dot(sums, jnp.concatenate([low, low, low], axis=0))
        for row in range(12):
            picked = found[row * chunk_count:(row + 1) * chunk_count] * high
            out_ref[row:row + 1, at] = jnp.sum(picked, axis=0, keepdims=True)


def final_kernel(stats_ref, known_ref, basis_own_ref, field_ref, points_ref, currents_ref, iron_ref):
    stats = jnp.sum(stats_ref[...], axis=0)
    known = known_ref[...]
    initial_norm, hessen_a, hessen_b = known[:, 0:1], known[:, 1:2], known[:, 2:3]
    hessen_c, hessen_d, normal_second = stats[:, 0:1], stats[:, 1:2], stats[:, 2:3]
    normal_first = hessen_a * hessen_a + hessen_b * hessen_b
    normal_cross = hessen_a * hessen_c + hessen_b * hessen_d
    target_first = initial_norm * hessen_a
    target_second = initial_norm * hessen_c
    determinant = normal_first * normal_second - normal_cross * normal_cross
    weight_first = (normal_second * target_first - normal_cross * target_second) / determinant
    weight_second = (normal_first * target_second - normal_cross * target_first) / determinant
    currents_ref[...] = weight_first * basis_own_ref[0:1, :] + weight_second * basis_own_ref[1:2, :]
    moments = weight_first * field_ref[0:6, :] + weight_second * field_ref[6:12, :]
    points = points_ref[...] - 0.5
    px, py, pz = points[0:1], points[1:2], points[2:3]
    iron_ref[0:1, :] = pz * moments[1:2] - py * moments[2:3] - moments[3:4]
    iron_ref[1:2, :] = px * moments[2:3] - pz * moments[0:1] - moments[4:5]
    iron_ref[2:3, :] = py * moments[0:1] - px * moments[1:2] - moments[5:6]


def shape(*sizes, dtype=jnp.float32):
    return jax.ShapeDtypeStruct(sizes, dtype)


def shards(drive, resist, centers, tangents, iron_points, owner, range_len):
    seg_dev = drive.shape[0]
    col_len = centers.shape[1]
    n_col = lax.axis_size("col")
    n_row = lax.axis_size("row")
    n_dev = n_col * n_row
    segments = seg_dev * n_dev
    width = n_col * seg_dev
    points_count = iron_points.shape[1]
    coupling = 0.5 / math.sqrt(segments)
    keep = seg_dev * segments * 4 <= KEEP_BYTES
    tiles = segments // TILE
    call = functools.partial(pl.pallas_call, compiler_params=pltpu.CompilerParams(vmem_limit_bytes=VMEM_LIMIT))
    scratch = [pltpu.VMEM((1, segments), jnp.float32), pltpu.VMEM((seg_dev, 128), jnp.float32)]
    if keep:
        scratch += [pltpu.VMEM((tiles, seg_dev, TILE), jnp.float32), pltpu.SemaphoreType.DMA((tiles,))]
    hbm = pl.BlockSpec(memory_space=pltpu.HBM)
    smem = pl.BlockSpec(memory_space=pltpu.SMEM)
    vmem = pl.BlockSpec(memory_space=pltpu.VMEM)

    def work(microseconds):
        return pl.CostEstimate(flops=int(microseconds * 1e9), bytes_accessed=0, transcendentals=0)

    def roomy(row_bytes):
        return STREAM_BYTES // row_bytes

    def exchange(x):
        return lax.all_to_all(x, AXES, 0, 0, tiled=True)

    spread, geometry = pl.pallas_call(
        entry_kernel,
        out_shape=(shape(n_dev, 1, seg_dev), shape(6, col_len)),
        in_specs=[hbm] * 3,
        scratch_shapes=[
            pltpu.VMEM((1, seg_dev), jnp.float32),
            pltpu.VMEM((3, col_len), jnp.float32),
            pltpu.VMEM((3, col_len), jnp.float32),
            pltpu.SemaphoreType.DMA((3,)),
        ],
        compiler_params=pltpu.CompilerParams(vmem_limit_bytes=ENTRY_LIMIT),
        name="entry",
    )(drive[None, :], centers, tangents)
    drive_all = exchange(spread).reshape(1, segments)
    pieces = [
        lax.ppermute(geometry, "col", [(k, (k + shift) % n_col) for k in range(n_col)]) for shift in range(1, n_col)
    ]

    chunk_count = points_count // CHUNK + n_row * (CHUNK - 1) // CHUNK
    chunk_count = -(-chunk_count // 8) * 8
    slot, group_table, left, drive_own, resist_own, own_geometry = call(
        functools.partial(group_kernel, n_row=n_row),
        out_shape=(
            shape(1, points_count, dtype=jnp.int32),
            shape(8, 128, dtype=jnp.int32),
            shape(chunk_count * CHUNK, 48, dtype=jnp.bfloat16),
            shape(1, seg_dev),
            shape(1, seg_dev),
            shape(6, col_len),
        ),
        scratch_shapes=[pltpu.VMEM((48 * chunk_count, CHUNK), jnp.float32)],
        cost_estimate=work(3),
        name="group_points",
    )(owner.reshape(1, points_count), iron_points, drive[None, :], resist[None, :], centers, tangents)
    pieces = [own_geometry] + pieces

    stream = functools.partial(
        pl.pallas_call, compiler_params=pltpu.CompilerParams(vmem_limit_bytes=STREAM_LIMIT if keep else VMEM_LIMIT)
    )
    first = stream(
        functools.partial(first_kernel, coupling, n_col, keep),
        out_shape=(
            shape(1, seg_dev), shape(n_dev, 1, seg_dev), shape(48, segments, dtype=jnp.bfloat16), shape(8, segments),
        ) + ((shape(roomy(seg_dev * TILE * 4), seg_dev, TILE),) if keep else ()),
        out_specs=(vmem,) * 4 + ((hbm,) if keep else ()),
        scratch_shapes=scratch,
        cost_estimate=work(5),
        name="first_image",
    )(drive_all, drive_own, resist_own, group_table, *pieces)
    image_own, image_spread, right, moment = first[0:4]
    image_all = exchange(image_spread).reshape(1, segments)
    cube_shape = (chunk_count, 2 * CHUNK, width)
    cube_scratch = [pltpu.VMEM(cube_shape, jnp.bfloat16), pltpu.SemaphoreType.DMA((chunk_count,))]
    if keep:
        cubes, after = stream(
            functools.partial(weigh_kernel, n_row=n_row),
            out_shape=(shape(roomy(4 * CHUNK * width), *cube_shape[1:], dtype=jnp.bfloat16), shape(8, 128)),
            in_specs=[smem, vmem, vmem],
            out_specs=(hbm, vmem),
            scratch_shapes=cube_scratch,
            cost_estimate=work(5),
            name="weigh",
        )(group_table, left, right)
    else:
        after = group_table
    basis, basis_own, stats, known = stream(
        functools.partial(second_kernel, coupling, n_col, keep),
        out_shape=(shape(2, segments), shape(2, seg_dev), shape(n_dev, 1, 128), shape(1, 128)),
        in_specs=[vmem] * 6 + ([hbm] if keep else [vmem] * n_col),
        scratch_shapes=scratch,
        cost_estimate=work(2),
        name="second_image",
    )(drive_all, image_all, drive_own, image_own, resist_own, after, *(first[4:5] if keep else pieces))
    stats_all = exchange(stats)

    field = stream(
        functools.partial(field_kernel, n_row=n_row, n_col=n_col, keep=keep),
        out_shape=shape(12, points_count),
        in_specs=[smem, smem, vmem, vmem, vmem] + ([hbm] if keep else [vmem, vmem]),
        scratch_shapes=[
            pltpu.VMEM((32, segments), jnp.bfloat16),
            pltpu.VMEM((16 * chunk_count, CHUNK), jnp.float32),
        ] + (cube_scratch if keep else []),
        cost_estimate=work(6),
        name="block_field",
    )(group_table, range_len, slot, moment, basis, *([cubes] if keep else [left, right]))
    currents, iron_field = stream(
        final_kernel,
        out_shape=(shape(1, seg_dev), shape(3, points_count)),
        name="combine",
    )(stats_all, known, basis_own, field, iron_points)
    return (currents[0], iron_field)


def solution(mesh):
    return jax.shard_map(
        shards,
        mesh=mesh,
        in_specs=(
            P(AXES),
            P(AXES),
            P(None, "col"),
            P(None, "col"),
            P(None, AXES),
            P(AXES, None),
            P(),
        ),
        out_specs=(P(AXES), P(None, AXES)),
        check_vma=False,
    )
```

profile of v0, /device:TPU:0, one launch (start us, length us, event | category | flops | bytes accessed | tf_op | source)
XLA Modules:
  0.0 55.4 jit_solution(6534713111601330133)
XLA Ops:
  0.6 1.5 %entry.1 = (f32[32,1,256]{2,1,0:T(1,128)}, f32[6,2048]{1,0:T(8,128)}) custom-call(f32[1,256]{1,0:T(1,128)} %bitcast.9, f32[3,2048]{1,0:T(4,128)} %centers_in_ref.1, f32[3,2048]{1,0:T(4,128)} %tangents_in_ref.1), custom_call_target="tpu_custom_call" | custom-call | tf_op jit(solution)/shard_map/entry/pallas_call | solution.py:446
  2.1 2.4 %collective-permute-start.2 = (f32[6,2048]{1,0:T(8,128)}, f32[6,2048]{1,0:T(8,128)S(1)}, u32[]{:S(2)}, u32[]{:S(2)}) collective-permute-start(f32[6,2048]{1,0:T(8,128)} %get-tuple-element.28), channel_id=1, source_target_pairs={{0,24},{8,0},{16,8},{24,16},{1,25},{9,1},{17,9},{25,17},{2,26},{10... | collective-permute-start | bytes 147464 | tf_op jit(solution)/shard_map/ppermute | solution.py:461
  4.5 0.6 %collective-permute-start.1 = (f32[6,2048]{1,0:T(8,128)}, f32[6,2048]{1,0:T(8,128)S(1)}, u32[]{:S(2)}, u32[]{:S(2)}) collective-permute-start(f32[6,2048]{1,0:T(8,128)} %get-tuple-element.28), channel_id=1, source_target_pairs={{0,16},{8,24},{16,0},{24,8},{1,17},{9,25},{17,1},{25,9},{2,18},{10... | collective-permute-start | bytes 147464 | tf_op jit(solution)/shard_map/ppermute | solution.py:461
  5.2 0.2 collective-permute-start
  5.3 5.9 %all-to-all-start = ((f32[32,1,256]{2,1,0:T(1,128)}), f32[32,1,256]{2,1,0:T(1,128)S(1)}, u32[]{:S(2)}, u32[]{:S(2)}) async-start(f32[32,1,256]{2,1,0:T(1,128)} %get-tuple-element.23), calls=%async_computation | async-start | bytes 65536 | tf_op jit(solution)/shard_map/all_to_all | solution.py:444
  11.3 0.0 copy-start
  11.3 0.7 %copy-done = f32[3,2048]{1,0:T(4,128)S(1)} copy-done((f32[3,2048]{1,0:T(4,128)S(1)}, f32[3,2048]{1,0:T(4,128)}, u32[]{:S(2)}) %copy-start) | copy-done | bytes 24600
  12.0 0.8 %copy-done.1 = f32[3,2048]{1,0:T(4,128)S(1)} copy-done((f32[3,2048]{1,0:T(4,128)S(1)}, f32[3,2048]{1,0:T(4,128)}, u32[]{:S(2)}) %copy-start.1) | copy-done | bytes 24600
  12.8 0.8 %copy-done.2 = f32[3,2048]{1,0:T(4,128)S(1)} copy-done((f32[3,2048]{1,0:T(4,128)S(1)}, f32[3,2048]{1,0:T(4,128)}, u32[]{:S(2)}) %copy-start.2) | copy-done | bytes 24600
  13.6 0.7 %copy-done.4 = f32[256]{0:T(256)S(1)} copy-done((f32[256]{0:T(256)S(1)}, f32[256]{0:T(256)}, u32[]{:S(2)}) %copy-start.4) | copy-done | bytes 1048
  14.2 0.7 %copy-done.5 = s32[2048,1]{0,1:T(1,128)S(1)} copy-done((s32[2048,1]{0,1:T(1,128)S(1)}, s32[2048,1]{0,1:T(1,128)}, u32[]{:S(2)}) %copy-start.5) | copy-done | bytes 8216
  14.9 0.7 %copy-done.6 = f32[256]{0:T(256)S(1)} copy-done((f32[256]{0:T(256)S(1)}, f32[256]{0:T(256)}, u32[]{:S(2)}) %copy-start.6) | copy-done | bytes 1048
  15.6 1.2 %group_points.1 = (s32[1,2048]{1,0:T(1,128)S(1)}, s32[8,128]{1,0:T(8,128)S(1)}, bf16[3072,48]{1,0:T(8,128)(2,1)S(1)}, f32[1,256]{1,0:T(1,128)S(1)}, f32[1,256]{1,0:T(1,128)S(1)}, /*index=5*/f32[6,2048]{1,0:T(8,128)S(1)}) custom-call(s32[1,2048]{1,0:T(1,128)S(1)} %bitcast.11, f32[3,2048]{1,0:T(4,128)S(1)} %copy-done.2, f32[1,256]{1,0:T(1,128)S(1)} %bitcast.10, ...), custom_call_target="tpu_custom_call" | custom-call | flops 3000000000 | tf_op jit(solution)/shard_map/group_points/pallas_call | solution.py:466
  16.8 0.0 collective-permute-done.2.refs_3_
  16.9 1.6 %all-to-all-done = f32[32,1,256]{2,1,0:T(1,128)S(1)} async-done(((f32[32,1,256]{2,1,0:T(1,128)}), f32[32,1,256]{2,1,0:T(1,128)S(1)}, u32[]{:S(2)}, u32[]{:S(2)}) %all-to-all-start) | async-done | bytes 32800 | tf_op jit(solution)/shard_map/all_to_all | solution.py:444
  18.5 4.4 %first_image.1 = (f32[1,256]{1,0:T(1,128)S(1)}, f32[32,1,256]{2,1,0:T(1,128)}, bf16[48,8192]{1,0:T(8,128)(2,1)S(1)}, f32[8,8192]{1,0:T(8,128)S(1)}, f32[40,256,512]{2,1,0:T(8,128)}) custom-call(f32[1,8192]{1,0:T(1,128)S(1)} %bitcast.6, f32[1,256]{1,0:T(1,128)S(1)} %get-tuple-element.24.drive_own_ref, f32[1,256]{1,0:T(1,128)S(1)} %get-tuple-element.25.resist_ref, ...), custom_call_target="tpu_custom_call" | custom-call | flops 5000000000 | tf_op jit(solution)/shard_map/first_image/pallas_call | solution.py:485
  22.9 0.0 copy-start.7
  22.9 4.3 %all-to-all-start.1 = ((f32[32,1,256]{2,1,0:T(1,128)}), f32[32,1,256]{2,1,0:T(1,128)S(1)}, u32[]{:S(2)}, u32[]{:S(2)}) async-start(f32[32,1,256]{2,1,0:T(1,128)} %get-tuple-element.29), calls=%async_computation.1 | async-start | bytes 65536 | tf_op jit(solution)/shard_map/all_to_all | solution.py:444
  27.2 5.3 %weigh.1 = (bf16[40,256,1024]{2,1,0:T(8,128)(2,1)}, f32[8,128]{1,0:T(8,128)S(1)}) custom-call(s32[8,128]{1,0:T(8,128)S(1)} %get-tuple-element.26.after_ref.group_ref, bf16[3072,48]{1,0:T(8,128)(2,1)S(1)} %get-tuple-element.31.left_ref, bf16[48,8192]{1,0:T(8,128)(2,1)S(1)} %get-tuple-element.32.right_ref), custom_call_target="tpu_custom_call" | custom-call | flops 5000000000 | tf_op jit(solution)/shard_map/weigh/pallas_call | solution.py:500
  32.5 1.9 %all-to-all-done.1 = f32[32,1,256]{2,1,0:T(1,128)S(1)} async-done(((f32[32,1,256]{2,1,0:T(1,128)}), f32[32,1,256]{2,1,0:T(1,128)S(1)}, u32[]{:S(2)}, u32[]{:S(2)}) %all-to-all-start.1) | async-done | bytes 32800 | tf_op jit(solution)/shard_map/all_to_all | solution.py:444
  34.4 4.5 %second_image.1 = (f32[2,8192]{1,0:T(2,128)S(1)}, f32[2,256]{1,0:T(2,128)S(1)}, f32[32,1,128]{2,1,0:T(1,128)}, f32[1,128]{1,0:T(1,128)S(1)}) custom-call(f32[1,8192]{1,0:T(1,128)S(1)} %bitcast.7, f32[1,8192]{1,0:T(1,128)S(1)} %bitcast.8, f32[1,256]{1,0:T(1,128)S(1)} %get-tuple-element.24.drive_own_ref, f32[1,256]{1,0:T(1,128)S(1)} %get-tuple-element.30.image_own_ref, ...), custom_call_target="tpu_custom_call" | custom-call | flops 2000000000 | tf_op jit(solution)/shard_map/second_image/pallas_call | solution.py:511
  38.9 4.0 %all-to-all-start.2 = ((f32[32,1,128]{2,1,0:T(1,128)}), f32[32,1,128]{2,1,0:T(1,128)S(1)}, u32[]{:S(2)}, u32[]{:S(2)}) async-start(f32[32,1,128]{2,1,0:T(1,128)} %get-tuple-element.35), calls=%async_computation.2 | async-start | bytes 32768 | tf_op jit(solution)/shard_map/all_to_all | solution.py:444
  42.9 11.5 %block_field.1.field_ref = f32[12,2048]{1,0:T(8,128)S(1)} custom-call(s32[8,128]{1,0:T(8,128)S(1)} %get-tuple-element.26.after_ref.group_ref, s32[8]{0:T(128)S(1)} %copy-done.7, s32[1,2048]{1,0:T(1,128)S(1)} %get-tuple-element.38.slot_ref, f32[8,8192]{1,0:T(8,128)S(1)} %get-tuple-element.39.moment_ref, f32[2,8192]{1,0:T(2,128)S(1)} %get-tuple-element.40.basis_ref, ...), custom_call_target="tpu_custom_call" | custom-call | flops 6000000000 | tf_op jit(solution)/shard_map/block_field/pallas_call | solution.py:521
  54.4 1.0 %combine.1 = (f32[1,256]{1,0:T(1,128)}, f32[3,2048]{1,0:T(4,128)}) custom-call(f32[32,1,128]{2,1,0:T(1,128)S(1)} %all-to-all-done.2.stats_ref, f32[1,128]{1,0:T(1,128)S(1)} %get-tuple-element.36.known_ref, f32[2,256]{1,0:T(2,128)S(1)} %get-tuple-element.37.basis_own_ref, f32[12,2048]{1,0:T(8,128)S(1)} %block_field.1.field_ref, f32[3,2048]{1,0:T(4,128)S(1)} %copy-done.3), custom_call_target="tpu_custom_call" | custom-call | tf_op jit(solution)/shard_map/combine/pallas_call | solution.py:532
  (11 shorter events, 0.0 us)
Async XLA Ops:
  2.1 14.7 %collective-permute-start.2 = (f32[6,2048]{1,0:T(8,128)}, f32[6,2048]{1,0:T(8,128)S(1)}, u32[]{:S(2)}, u32[]{:S(2)}) collective-permute-start(f32[6,2048]{1,0:T(8,128)} %get-tuple-element.28), channel_id=1, source_target_pairs={{0,24},{8,0},{16,8},{24,16},{1,25},{9,1},{17,9},{25,17},{2,26},{10... | collective-permute-start | bytes 147464 | tf_op jit(solution)/shard_map/ppermute | solution.py:461
  4.5 12.3 %collective-permute-start.1 = (f32[6,2048]{1,0:T(8,128)}, f32[6,2048]{1,0:T(8,128)S(1)}, u32[]{:S(2)}, u32[]{:S(2)}) collective-permute-start(f32[6,2048]{1,0:T(8,128)} %get-tuple-element.28), channel_id=1, source_target_pairs={{0,16},{8,24},{16,0},{24,8},{1,17},{9,25},{17,1},{25,9},{2,18},{10... | collective-permute-start | bytes 147464 | tf_op jit(solution)/shard_map/ppermute | solution.py:461
  5.2 11.7 %collective-permute-start = (f32[6,2048]{1,0:T(8,128)}, f32[6,2048]{1,0:T(8,128)S(1)}, u32[]{:S(2)}, u32[]{:S(2)}) collective-permute-start(f32[6,2048]{1,0:T(8,128)} %get-tuple-element.28), channel_id=1, source_target_pairs={{0,8},{8,16},{16,24},{24,0},{1,9},{9,17},{17,25},{25,1},{2,10},{10... | collective-permute-start | bytes 147464 | tf_op jit(solution)/shard_map/ppermute | solution.py:461
  5.3 13.1 %all-to-all-start = ((f32[32,1,256]{2,1,0:T(1,128)}), f32[32,1,256]{2,1,0:T(1,128)S(1)}, u32[]{:S(2)}, u32[]{:S(2)}) async-start(f32[32,1,256]{2,1,0:T(1,128)} %get-tuple-element.23), calls=%async_computation | async-start | bytes 65536 | tf_op jit(solution)/shard_map/all_to_all | solution.py:444
  11.3 0.8 %copy-start = (f32[3,2048]{1,0:T(4,128)S(1)}, f32[3,2048]{1,0:T(4,128)}, u32[]{:S(2)}) copy-start(f32[3,2048]{1,0:T(4,128)} %centers_in_ref.1) | copy-start | bytes 73732
  12.0 0.8 %copy-start.1 = (f32[3,2048]{1,0:T(4,128)S(1)}, f32[3,2048]{1,0:T(4,128)}, u32[]{:S(2)}) copy-start(f32[3,2048]{1,0:T(4,128)} %tangents_in_ref.1) | copy-start | bytes 73732
  12.8 0.8 %copy-start.2 = (f32[3,2048]{1,0:T(4,128)S(1)}, f32[3,2048]{1,0:T(4,128)}, u32[]{:S(2)}) copy-start(f32[3,2048]{1,0:T(4,128)} %points_ref.3) | copy-start | bytes 73732
  13.6 0.7 %copy-start.4 = (f32[256]{0:T(256)S(1)}, f32[256]{0:T(256)}, u32[]{:S(2)}) copy-start(f32[256]{0:T(256)} %param.7) | copy-start | bytes 3076
  14.2 0.7 %copy-start.5 = (s32[2048,1]{0,1:T(1,128)S(1)}, s32[2048,1]{0,1:T(1,128)}, u32[]{:S(2)}) copy-start(s32[2048,1]{0,1:T(1,128)} %param.12) | copy-start | bytes 24580
  14.9 0.7 %copy-start.6 = (f32[256]{0:T(256)S(1)}, f32[256]{0:T(256)}, u32[]{:S(2)}) copy-start(f32[256]{0:T(256)} %param.8) | copy-start | bytes 3076
  22.9 20.0 %copy-start.7 = (s32[8]{0:T(128)S(1)}, s32[8]{0:T(128)}, u32[]{:S(2)}) copy-start(s32[8]{0:T(128)} %length_ref.1) | copy-start | bytes 100
  22.9 11.5 %all-to-all-start.1 = ((f32[32,1,256]{2,1,0:T(1,128)}), f32[32,1,256]{2,1,0:T(1,128)S(1)}, u32[]{:S(2)}, u32[]{:S(2)}) async-start(f32[32,1,256]{2,1,0:T(1,128)} %get-tuple-element.29), calls=%async_computation.1 | async-start | bytes 65536 | tf_op jit(solution)/shard_map/all_to_all | solution.py:444
  34.4 20.0 %copy-start.3 = (f32[3,2048]{1,0:T(4,128)S(1)}, f32[3,2048]{1,0:T(4,128)}, u32[]{:S(2)}) copy-start(f32[3,2048]{1,0:T(4,128)} %points_ref.3) | copy-start | bytes 73732
  38.9 15.5 %all-to-all-start.2 = ((f32[32,1,128]{2,1,0:T(1,128)}), f32[32,1,128]{2,1,0:T(1,128)S(1)}, u32[]{:S(2)}, u32[]{:S(2)}) async-start(f32[32,1,128]{2,1,0:T(1,128)} %get-tuple-element.35), calls=%async_computation.2 | async-start | bytes 32768 | tf_op jit(solution)/shard_map/all_to_all | solution.py:444
where the time goes:
time: 56.3 us; the launch traced here: 55.4 us
  Pallas kernels  29.4 us (52%)
  starting transfers between devices  17.5 us (31%)
  local copies, waits for them, and re-layouts  4.33 us (8%)
  waiting for transfers between devices  3.45 us (6%)
  between operations  0.77 us (1%)
    all_to_all x3, starting transfers between devices, exchange(): return lax.all_to_all(x, AXES, 0, 0, tiled=True)  14.2 us
    pallas_call x1, Pallas kernels, shards(): stream(functools.partial(field_kernel, n_row=n_row, n_col=n_col, keep=kee...  11.5 us
    pallas_call x1, Pallas kernels, shards(): stream(functools.partial(weigh_kernel, n_row=n_row), out_shape=(shape(roo...  5.32 us
    pallas_call x1, Pallas kernels, shards(): stream(functools.partial(second_kernel, coupling, n_col, keep), out_shape...  4.5 us
    pallas_call x1, Pallas kernels, shards(): stream(functools.partial(first_kernel, coupling, n_col, keep), out_shape=...  4.4 us
    unnamed x16, local copies, waits for them, and re-layouts  4.33 us
    all_to_all x3, waiting for transfers between devices, exchange(): return lax.all_to_all(x, AXES, 0, 0, tiled=True)  3.44 us
    ppermute x3, starting transfers between devices, shards(): lax.ppermute(geometry, 'col', [(k, (k + shift) % n_col) for k in range(n_...  3.23 us
  transfers between devices with their start and end apart: 6, of which 2 were waited for; matrix products, arithmetic and copies ran while one was open for 0% of the time, Pallas kernels for 33%

commit v1 on v0

--- a/solution.py
+++ b/solution.py
@@ -14,6 +14,8 @@
 CHUNK = 128
 GROUP = 4
 TILE = 512
+COLUMNS = 256
+ROWS = 64
 KEEP_BYTES = 16 * 1024 * 1024
 VMEM_LIMIT = 32 * 1024 * 1024
 STREAM_LIMIT = 44 * 1024 * 1024
@@ -88,17 +90,34 @@
     return lax.rem(lax.axis_index("col") + n_col - shift, n_col)
 
 
-def couple(pieces, vec_ref, acc_ref, kept=None, right_ref=None, moment_ref=None):
+def own_sides(own_ref, left_ref):
+    seg_dev = left_ref.shape[1]
+    own = own_ref[:, aligned(lax.axis_index("row") * seg_dev, seg_dev)]
+    left_ref[0] = transposed(left_parts(left_center(own[0:3] - 0.5, EPS_SEG)))
+    left_ref[1] = transposed(left_parts(rows8(own[3:6])))
+
+
+def couple_tile(left_ref, rc, rt, vec, acc_ref, kept_ref=None, index=0):
+    for part in range(TILE // COLUMNS):
+        columns = slice(part * COLUMNS, (part + 1) * COLUMNS)
+        for row in range(0, acc_ref.shape[0], ROWS):
+            rows = slice(row, row + ROWS)
+            pair = dot(left_ref[1, rows], rt[:, columns]) * lax.rsqrt(dot(left_ref[0, rows], rc[:, columns]))
+            if kept_ref is not None:
+                kept_ref[index, rows, columns] = pair
+            acc_ref[rows] += fold_lanes(pair * vec[:, columns])
+
+
+def couple(pieces, vec_ref, acc_ref, left_ref, kept=None, right_ref=None, along_ref=None, moment_ref=None):
     seg_dev = acc_ref.shape[0]
     n_col = len(pieces)
     length = pieces[0].shape[1]
-    own = pieces[0][:, aligned(lax.axis_index("row") * seg_dev, seg_dev)]
-    lc = transposed(left_parts(left_center(own[0:3] - 0.5, EPS_SEG)))
-    lt = transposed(left_parts(rows8(own[3:6])))
+    own_sides(pieces[0], left_ref)
     acc_ref[...] = jnp.zeros_like(acc_ref)
     count = length // TILE
     for shift, piece in enumerate(pieces):
         col = piece_column(shift, n_col)
+        keeps = kept is not None and (shift + 1) * count <= kept[0].shape[0]
 
         def step(k, carry):
             geo = piece[:, aligned(k * TILE, TILE)]
@@ -106,10 +125,10 @@
             center, tangent = geo[0:3] - 0.5, geo[3:6]
             rc = right_parts(right_center(center))
             rt = right_parts(rows8(tangent))
-            pair = dot(lt, rt) * lax.rsqrt(dot(lc, rc))
-            if kept is not None:
-                kept[0][shift * count + k] = pair
-                kept_copy(kept, shift * count + k, out=True).start()
+            index = shift * count + k
+            couple_tile(left_ref, rc, rt, vec_ref[:, vec_at], acc_ref, kept[0] if keeps else None, index)
+            if keeps:
+                kept_copy(kept, index, out=True).start()
             if right_ref is not None:
                 cross = jnp.concatenate([
                     tangent[1:2] * center[2:3] - tangent[2:3] * center[1:2],
@@ -117,12 +136,39 @@
                     tangent[0:1] * center[1:2] - tangent[1:2] * center[0:1],
                 ], axis=0)
                 both = rows8(tangent, cross)
+                along_ref[:, vec_at] = rt
                 for part in range(TILE // seg_dev):
                     row = k * (TILE // seg_dev) + part
                     block_at = aligned((row * n_col + col) * seg_dev, seg_dev)
                     right_ref[:, block_at] = rc[:, part * seg_dev:(part + 1) * seg_dev]
                     moment_ref[:, block_at] = both[:, part * seg_dev:(part + 1) * seg_dev]
-            acc_ref[...] += fold_lanes(pair * vec_ref[:, vec_at])
+            return carry
+
+        lax.fori_loop(0, count, step, 0, unroll=4)
+    return jnp.sum(acc_ref[...].T, axis=0, keepdims=True)
+
+
+def couple_again(kept, own_ref, right_ref, along_ref, vec_ref, acc_ref, left_ref, n_col):
+    own_sides(own_ref, left_ref)
+    seg_dev = acc_ref.shape[0]
+    acc_ref[...] = jnp.zeros_like(acc_ref)
+    length = vec_ref.shape[1] // n_col
+    count = length // TILE
+    stored = kept[0].shape[0] // count
+    for shift in list(range(stored, n_col)) + list(range(stored)):
+        col = piece_column(shift, n_col)
+
+        def step(k, carry):
+            vec_at = pl.ds(pl.multiple_of(col * length + k * TILE, TILE), TILE)
+            if shift < stored:
+                kept_copy(kept, shift * count + k, out=False).wait()
+                acc_ref[...] += fold_lanes(kept[0][shift * count + k] * vec_ref[:, vec_at])
+            else:
+                rc = jnp.concatenate([
+                    right_ref[:, aligned(((k * (TILE // seg_dev) + part) * n_col + col) * seg_dev, seg_dev)]
+                    for part in range(TILE // seg_dev)
+                ], axis=1)
+                couple_tile(left_ref, rc, along_ref[:, vec_at], vec_ref[:, vec_at], acc_ref)
             return carry
 
         lax.fori_loop(0, count, step, 0, unroll=4)
@@ -134,23 +180,6 @@
     if out:
         return pltpu.make_async_copy(local.at[index], remote.at[index], sems.at[index])
     return pltpu.make_async_copy(remote.at[index], local.at[index], sems.at[index])
-
-
-def couple_kept(kept, vec_ref, acc_ref, n_col):
-    acc_ref[...] = jnp.zeros_like(acc_ref)
-    length = vec_ref.shape[1] // n_col
-    count = length // TILE
-    for shift in range(n_col):
-        col = piece_column(shift, n_col)
-
-        def step(k, carry):
-            kept_copy(kept, shift * count + k, out=False).wait()
-            vec_at = pl.ds(pl.multiple_of(col * length + k * TILE, TILE), TILE)
-            acc_ref[...] += fold_lanes(kept[0][shift * count + k] * vec_ref[:, vec_at])
-            return carry
-
-        lax.fori_loop(0, count, step, 0, unroll=2)
-    return jnp.sum(acc_ref[...].T, axis=0, keepdims=True)
 
 
 def spread_rows(ref, row):
@@ -172,18 +201,18 @@
 
 def first_kernel(coupling, n_col, keep, drive_ref, drive_own_ref, resist_ref, after_ref, *refs):
     pieces, refs = refs[:n_col], refs[n_col:]
-    image_ref, spread_ref, right_ref, moment_ref = refs[0:4]
+    image_ref, spread_ref, right_ref, along_ref, moment_ref = refs[0:5]
     kept = None
     if keep:
-        kept_hbm = refs[4]
-        vec_ref, acc_ref, kept_ref, sems = refs[5:]
+        kept_hbm = refs[5]
+        vec_ref, acc_ref, left_ref, kept_ref, sems = refs[6:]
         kept = (kept_ref, kept_hbm, sems)
     else:
-        vec_ref, acc_ref = refs[4:]
+        vec_ref, acc_ref, left_ref = refs[5:]
     drive = drive_ref[...]
     scale = 1.0 / jnp.sqrt(jnp.sum(drive * drive, keepdims=True))
     vec_ref[...] = drive * scale
-    product = couple(pieces, vec_ref, acc_ref, kept, right_ref, moment_ref)
+    product = couple(pieces, vec_ref, acc_ref, left_ref, kept, right_ref, along_ref, moment_ref)
     image = resist_ref[...] * (drive_own_ref[...] * scale) + coupling * product
     image_ref[...] = image
     spread_rows(spread_ref, image)
@@ -194,14 +223,15 @@
 
 def second_kernel(coupling, n_col, keep, drive_ref, image_ref, drive_own_ref, image_own_ref, resist_ref, after_ref, *refs):
     if keep:
-        kept_hbm, refs = refs[0], refs[1:]
-        vec_ref, acc_ref, kept_ref, sems = refs[4:]
+        kept_hbm, own_ref, right_ref, along_ref = refs[0:4]
+        refs = refs[4:]
+        vec_ref, acc_ref, left_ref, kept_ref, sems = refs[4:]
         kept = (kept_ref, kept_hbm, sems)
         for index in range(kept_ref.shape[0]):
             kept_copy(kept, index, out=False).start()
     else:
         pieces, refs = refs[:n_col], refs[n_col:]
-        vec_ref, acc_ref = refs[4:]
+        vec_ref, acc_ref, left_ref = refs[4:]
     basis_ref, basis_own_ref, stats_ref, known_ref = refs[0:4]
     drive = drive_ref[...]
     norm = jnp.sqrt(jnp.sum(drive * drive, keepdims=True))
@@ -221,9 +251,9 @@
     basis_own_ref[0:1, :] = own_a
     basis_own_ref[1:2, :] = own_b
     if keep:
-        product = couple_kept(kept, vec_ref, acc_ref, n_col)
+        product = couple_again(kept, own_ref, right_ref, along_ref, vec_ref, acc_ref, left_ref, n_col)
     else:
-        product = couple(pieces, vec_ref, acc_ref)
+        product = couple(pieces, vec_ref, acc_ref, left_ref)
     second = resist_ref[...] * own_b + coupling * product
     lane = iota((1, 128), 1)
 
@@ -358,7 +388,7 @@
             table_ref[:, block_at] = jnp.concatenate([high, parts - high], axis=0).astype(jnp.bfloat16)
         return carry
 
-    lax.fori_loop(0, n_row, table_step, 0, unroll=2)
+    lax.fori_loop(0, n_row, table_step, 0, unroll=min(n_row, 8))
 
     def step(k, carry):
         for part in range(GROUP):
@@ -370,8 +400,8 @@
             else:
                 high, low = cube_halves(left_ref[aligned(chunk * CHUNK, CHUNK), :], right_ref[:, block_at])
                 cubes = jnp.concatenate([high, low], axis=0)
-            both = dot_nt(cubes, table_ref[:, block_at])
-            total = (both[0:CHUNK] + both[CHUNK:2 * CHUNK]).T
+            both = dot_nt(table_ref[:, block_at], cubes)
+            total = both[:, 0:CHUNK] + both[:, CHUNK:2 * CHUNK]
             sums_ref[pl.ds(chunk, 16, stride=chunk_count), :] = total[0:16] + total[16:32]
         return carry
 
@@ -425,9 +455,13 @@
     points_count = iron_points.shape[1]
     coupling = 0.5 / math.sqrt(segments)
     keep = seg_dev * segments * 4 <= KEEP_BYTES
-    tiles = segments // TILE
     call = functools.partial(pl.pallas_call, compiler_params=pltpu.CompilerParams(vmem_limit_bytes=VMEM_LIMIT))
-    scratch = [pltpu.VMEM((1, segments), jnp.float32), pltpu.VMEM((seg_dev, 128), jnp.float32)]
+    scratch = [
+        pltpu.VMEM((1, segments), jnp.float32),
+        pltpu.VMEM((seg_dev, 128), jnp.float32),
+        pltpu.VMEM((2, seg_dev, 48), jnp.bfloat16),
+    ]
+    tiles = (n_col // 2) * (col_len // TILE)
     if keep:
         scratch += [pltpu.VMEM((tiles, seg_dev, TILE), jnp.float32), pltpu.SemaphoreType.DMA((tiles,))]
     hbm = pl.BlockSpec(memory_space=pltpu.HBM)
@@ -485,14 +519,15 @@
     first = stream(
         functools.partial(first_kernel, coupling, n_col, keep),
         out_shape=(
-            shape(1, seg_dev), shape(n_dev, 1, seg_dev), shape(48, segments, dtype=jnp.bfloat16), shape(8, segments),
+            shape(1, seg_dev), shape(n_dev, 1, seg_dev), shape(48, segments, dtype=jnp.bfloat16),
+            shape(48, segments, dtype=jnp.bfloat16), shape(8, segments),
         ) + ((shape(roomy(seg_dev * TILE * 4), seg_dev, TILE),) if keep else ()),
-        out_specs=(vmem,) * 4 + ((hbm,) if keep else ()),
+        out_specs=(vmem,) * 5 + ((hbm,) if keep else ()),
         scratch_shapes=scratch,
         cost_estimate=work(5),
         name="first_image",
     )(drive_all, drive_own, resist_own, group_table, *pieces)
-    image_own, image_spread, right, moment = first[0:4]
+    image_own, image_spread, right, along, moment = first[0:5]
     image_all = exchange(image_spread).reshape(1, segments)
     cube_shape = (chunk_count, 2 * CHUNK, width)
     cube_scratch = [pltpu.VMEM(cube_shape, jnp.bfloat16), pltpu.SemaphoreType.DMA((chunk_count,))]
@@ -511,11 +546,11 @@
     basis, basis_own, stats, known = stream(
         functools.partial(second_kernel, coupling, n_col, keep),
         out_shape=(shape(2, segments), shape(2, seg_dev), shape(n_dev, 1, 128), shape(1, 128)),
-        in_specs=[vmem] * 6 + ([hbm] if keep else [vmem] * n_col),
+        in_specs=[vmem] * 6 + ([hbm] + [vmem] * 3 if keep else [vmem] * n_col),
         scratch_shapes=scratch,
         cost_estimate=work(2),
         name="second_image",
-    )(drive_all, image_all, drive_own, image_own, resist_own, after, *(first[4:5] if keep else pieces))
+    )(drive_all, image_all, drive_own, image_own, resist_own, after, *([first[5], own_geometry, right, along] if keep else pieces))
     stats_all = exchange(stats)
 
     field = stream(

time: 56.3 us -> 54.3 us (0.964)
  Pallas kernels: 29.4 us -> 27.4 us
    pallas_call x1, Pallas kernels: 11.5 us -> 10.6 us  [shards(): stream(functools.partial(field_kernel, n_row=n_row, n_col=n_col, keep=kee...]
    pallas_call x1, Pallas kernels: 4.4 us -> 3.64 us  [shards(): stream(functools.partial(first_kernel, coupling, n_col, keep), out_shape=...]
  transfers between devices with their start and end apart: 6 -> 6, of which waited for: 2 -> 2; matrix products, arithmetic and copies ran while one was open for 0% -> 0% of each run, Pallas kernels for 33% -> 32%
where the time goes in v1:
time: 54.3 us; the launch traced here: 53.4 us
  Pallas kernels  27.4 us (50%)
  starting transfers between devices  17.4 us (32%)
  local copies, waits for them, and re-layouts  4.33 us (8%)
  waiting for transfers between devices  3.47 us (6%)
  between operations  0.77 us (1%)
    all_to_all x3, starting transfers between devices, exchange(): return lax.all_to_all(x, AXES, 0, 0, tiled=True)  14.2 us
    pallas_call x1, Pallas kernels, shards(): stream(functools.partial(field_kernel, n_row=n_row, n_col=n_col, keep=kee...  10.6 us
    pallas_call x1, Pallas kernels, shards(): stream(functools.partial(weigh_kernel, n_row=n_row), out_shape=(shape(roo...  5.3 us
    unnamed x16, local copies, waits for them, and re-layouts  4.33 us
    pallas_call x1, Pallas kernels, shards(): stream(functools.partial(second_kernel, coupling, n_col, keep), out_shape...  4.19 us
    pallas_call x1, Pallas kernels, shards(): stream(functools.partial(first_kernel, coupling, n_col, keep), out_shape=...  3.64 us
    all_to_all x3, waiting for transfers between devices, exchange(): return lax.all_to_all(x, AXES, 0, 0, tiled=True)  3.46 us
    ppermute x3, starting transfers between devices, shards(): lax.ppermute(geometry, 'col', [(k, (k + shift) % n_col) for k in range(n_...  3.23 us
  transfers between devices with their start and end apart: 6, of which 2 were waited for; matrix products, arithmetic and copies ran while one was open for 0% of the time, Pallas kernels for 32%

profile of v1, /device:TPU:0, one launch (start us, length us, event | category | flops | bytes accessed | tf_op | source)
XLA Modules:
  0.0 53.4 jit_solution(384502899110743956)
XLA Ops:
  0.6 1.5 %entry.1 = (f32[32,1,256]{2,1,0:T(1,128)}, f32[6,2048]{1,0:T(8,128)}) custom-call(f32[1,256]{1,0:T(1,128)} %bitcast.9, f32[3,2048]{1,0:T(4,128)} %centers_in_ref.1, f32[3,2048]{1,0:T(4,128)} %tangents_in_ref.1), custom_call_target="tpu_custom_call" | custom-call | tf_op jit(solution)/shard_map/entry/pallas_call | solution.py:480
  2.1 2.4 %collective-permute-start.2 = (f32[6,2048]{1,0:T(8,128)}, f32[6,2048]{1,0:T(8,128)S(1)}, u32[]{:S(2)}, u32[]{:S(2)}) collective-permute-start(f32[6,2048]{1,0:T(8,128)} %get-tuple-element.29), channel_id=1, source_target_pairs={{0,24},{8,0},{16,8},{24,16},{1,25},{9,1},{17,9},{25,17},{2,26},{10... | collective-permute-start | bytes 147464 | tf_op jit(solution)/shard_map/ppermute | solution.py:495
  4.5 0.6 %collective-permute-start.1 = (f32[6,2048]{1,0:T(8,128)}, f32[6,2048]{1,0:T(8,128)S(1)}, u32[]{:S(2)}, u32[]{:S(2)}) collective-permute-start(f32[6,2048]{1,0:T(8,128)} %get-tuple-element.29), channel_id=1, source_target_pairs={{0,16},{8,24},{16,0},{24,8},{1,17},{9,25},{17,1},{25,9},{2,18},{10... | collective-permute-start | bytes 147464 | tf_op jit(solution)/shard_map/ppermute | solution.py:495
  5.2 0.2 collective-permute-start
  5.3 5.9 %all-to-all-start = ((f32[32,1,256]{2,1,0:T(1,128)}), f32[32,1,256]{2,1,0:T(1,128)S(1)}, u32[]{:S(2)}, u32[]{:S(2)}) async-start(f32[32,1,256]{2,1,0:T(1,128)} %get-tuple-element.24), calls=%async_computation | async-start | bytes 65536 | tf_op jit(solution)/shard_map/all_to_all | solution.py:478
  11.3 0.0 copy-start
  11.3 0.7 %copy-done = f32[3,2048]{1,0:T(4,128)S(1)} copy-done((f32[3,2048]{1,0:T(4,128)S(1)}, f32[3,2048]{1,0:T(4,128)}, u32[]{:S(2)}) %copy-start) | copy-done | bytes 24600
  12.0 0.8 %copy-done.1 = f32[3,2048]{1,0:T(4,128)S(1)} copy-done((f32[3,2048]{1,0:T(4,128)S(1)}, f32[3,2048]{1,0:T(4,128)}, u32[]{:S(2)}) %copy-start.1) | copy-done | bytes 24600
  12.8 0.8 %copy-done.2 = f32[3,2048]{1,0:T(4,128)S(1)} copy-done((f32[3,2048]{1,0:T(4,128)S(1)}, f32[3,2048]{1,0:T(4,128)}, u32[]{:S(2)}) %copy-start.2) | copy-done | bytes 24600
  13.6 0.7 %copy-done.4 = f32[256]{0:T(256)S(1)} copy-done((f32[256]{0:T(256)S(1)}, f32[256]{0:T(256)}, u32[]{:S(2)}) %copy-start.4) | copy-done | bytes 1048
  14.2 0.7 %copy-done.5 = s32[2048,1]{0,1:T(1,128)S(1)} copy-done((s32[2048,1]{0,1:T(1,128)S(1)}, s32[2048,1]{0,1:T(1,128)}, u32[]{:S(2)}) %copy-start.5) | copy-done | bytes 8216
  14.9 0.7 %copy-done.6 = f32[256]{0:T(256)S(1)} copy-done((f32[256]{0:T(256)S(1)}, f32[256]{0:T(256)}, u32[]{:S(2)}) %copy-start.6) | copy-done | bytes 1048
  15.6 1.2 %group_points.1 = (s32[1,2048]{1,0:T(1,128)S(1)}, s32[8,128]{1,0:T(8,128)S(1)}, bf16[3072,48]{1,0:T(8,128)(2,1)S(1)}, f32[1,256]{1,0:T(1,128)S(1)}, f32[1,256]{1,0:T(1,128)S(1)}, /*index=5*/f32[6,2048]{1,0:T(8,128)S(1)}) custom-call(s32[1,2048]{1,0:T(1,128)S(1)} %bitcast.11, f32[3,2048]{1,0:T(4,128)S(1)} %copy-done.2, f32[1,256]{1,0:T(1,128)S(1)} %bitcast.10, ...), custom_call_target="tpu_custom_call" | custom-call | flops 3000000000 | tf_op jit(solution)/shard_map/group_points/pallas_call | solution.py:500
  16.8 0.0 collective-permute-done.2.refs_3_
  16.9 1.6 %all-to-all-done = f32[32,1,256]{2,1,0:T(1,128)S(1)} async-done(((f32[32,1,256]{2,1,0:T(1,128)}), f32[32,1,256]{2,1,0:T(1,128)S(1)}, u32[]{:S(2)}, u32[]{:S(2)}) %all-to-all-start) | async-done | bytes 32800 | tf_op jit(solution)/shard_map/all_to_all | solution.py:478
  18.5 3.6 %first_image.1 = (f32[1,256]{1,0:T(1,128)S(1)}, f32[32,1,256]{2,1,0:T(1,128)}, bf16[48,8192]{1,0:T(8,128)(2,1)S(1)}, bf16[48,8192]{1,0:T(8,128)(2,1)S(1)}, f32[8...) custom-call(f32[1,8192]{1,0:T(1,128)S(1)} %bitcast.6, f32[1,256]{1,0:T(1,128)S(1)} %get-tuple-element.25.drive_own_ref, ...), custom_call_target="tpu_custom_call" | custom-call | flops 5000000000 | tf_op jit(solution)/shard_map/first_image/pallas_call | solution.py:519
  22.1 0.0 copy-start.7
  22.1 4.3 %all-to-all-start.1 = ((f32[32,1,256]{2,1,0:T(1,128)}), f32[32,1,256]{2,1,0:T(1,128)S(1)}, u32[]{:S(2)}, u32[]{:S(2)}) async-start(f32[32,1,256]{2,1,0:T(1,128)} %get-tuple-element.30), calls=%async_computation.1 | async-start | bytes 65536 | tf_op jit(solution)/shard_map/all_to_all | solution.py:478
  26.4 5.3 %weigh.1 = (bf16[40,256,1024]{2,1,0:T(8,128)(2,1)}, f32[8,128]{1,0:T(8,128)S(1)}) custom-call(s32[8,128]{1,0:T(8,128)S(1)} %get-tuple-element.27.after_ref.group_ref, bf16[3072,48]{1,0:T(8,128)(2,1)S(1)} %get-tuple-element.32.left_ref, bf16[48,8192]{1,0:T(8,128)(2,1)S(1)} %get-tuple-element.33.right_ref.refs_2_), custom_call_target="tpu_custom_call" | custom-call | flops 5000000000 | tf_op jit(solution)/shard_map/weigh/pallas_call | solution.py:535
  31.7 1.9 %all-to-all-done.1 = f32[32,1,256]{2,1,0:T(1,128)S(1)} async-done(((f32[32,1,256]{2,1,0:T(1,128)}), f32[32,1,256]{2,1,0:T(1,128)S(1)}, u32[]{:S(2)}, u32[]{:S(2)}) %all-to-all-start.1) | async-done | bytes 32800 | tf_op jit(solution)/shard_map/all_to_all | solution.py:478
  33.6 4.2 %second_image.1 = (f32[2,8192]{1,0:T(2,128)S(1)}, f32[2,256]{1,0:T(2,128)S(1)}, f32[32,1,128]{2,1,0:T(1,128)}, f32[1,128]{1,0:T(1,128)S(1)}) custom-call(f32[1,8192]{1,0:T(1,128)S(1)} %bitcast.7, f32[1,8192]{1,0:T(1,128)S(1)} %bitcast.8, f32[1,256]{1,0:T(1,128)S(1)} %get-tuple-element.25.drive_own_ref, f32[1,256]{1,0:T(1,128)S(1)} %get-tuple-element.31.image_own_ref, ...), custom_call_target="tpu_custom_call" | custom-call | flops 2000000000 | tf_op jit(solution)/shard_map/second_image/pallas_call | solution.py:546
  37.8 4.0 %all-to-all-start.2 = ((f32[32,1,128]{2,1,0:T(1,128)}), f32[32,1,128]{2,1,0:T(1,128)S(1)}, u32[]{:S(2)}, u32[]{:S(2)}) async-start(f32[32,1,128]{2,1,0:T(1,128)} %get-tuple-element.37), calls=%async_computation.2 | async-start | bytes 32768 | tf_op jit(solution)/shard_map/all_to_all | solution.py:478
  41.8 10.6 %block_field.1.field_ref = f32[12,2048]{1,0:T(8,128)S(1)} custom-call(s32[8,128]{1,0:T(8,128)S(1)} %get-tuple-element.27.after_ref.group_ref, s32[8]{0:T(128)S(1)} %copy-done.7, s32[1,2048]{1,0:T(1,128)S(1)} %get-tuple-element.40.slot_ref, f32[8,8192]{1,0:T(8,128)S(1)} %get-tuple-element.41.moment_ref, f32[2,8192]{1,0:T(2,128)S(1)} %get-tuple-element.42.basis_ref, ...), custom_call_target="tpu_custom_call" | custom-call | flops 6000000000 | tf_op jit(solution)/shard_map/block_field/pallas_call | solution.py:556
  52.4 1.0 %combine.1 = (f32[1,256]{1,0:T(1,128)}, f32[3,2048]{1,0:T(4,128)}) custom-call(f32[32,1,128]{2,1,0:T(1,128)S(1)} %all-to-all-done.2.stats_ref, f32[1,128]{1,0:T(1,128)S(1)} %get-tuple-element.38.known_ref, f32[2,256]{1,0:T(2,128)S(1)} %get-tuple-element.39.basis_own_ref, f32[12,2048]{1,0:T(8,128)S(1)} %block_field.1.field_ref, f32[3,2048]{1,0:T(4,128)S(1)} %copy-done.3), custom_call_target="tpu_custom_call" | custom-call | tf_op jit(solution)/shard_map/combine/pallas_call | solution.py:567
  (11 shorter events, 0.0 us)
Async XLA Ops:
  2.1 14.7 %collective-permute-start.2 = (f32[6,2048]{1,0:T(8,128)}, f32[6,2048]{1,0:T(8,128)S(1)}, u32[]{:S(2)}, u32[]{:S(2)}) collective-permute-start(f32[6,2048]{1,0:T(8,128)} %get-tuple-element.29), channel_id=1, source_target_pairs={{0,24},{8,0},{16,8},{24,16},{1,25},{9,1},{17,9},{25,17},{2,26},{10... | collective-permute-start | bytes 147464 | tf_op jit(solution)/shard_map/ppermute | solution.py:495
  4.5 12.3 %collective-permute-start.1 = (f32[6,2048]{1,0:T(8,128)}, f32[6,2048]{1,0:T(8,128)S(1)}, u32[]{:S(2)}, u32[]{:S(2)}) collective-permute-start(f32[6,2048]{1,0:T(8,128)} %get-tuple-element.29), channel_id=1, source_target_pairs={{0,16},{8,24},{16,0},{24,8},{1,17},{9,25},{17,1},{25,9},{2,18},{10... | collective-permute-start | bytes 147464 | tf_op jit(solution)/shard_map/ppermute | solution.py:495
  5.2 11.7 %collective-permute-start = (f32[6,2048]{1,0:T(8,128)}, f32[6,2048]{1,0:T(8,128)S(1)}, u32[]{:S(2)}, u32[]{:S(2)}) collective-permute-start(f32[6,2048]{1,0:T(8,128)} %get-tuple-element.29), channel_id=1, source_target_pairs={{0,8},{8,16},{16,24},{24,0},{1,9},{9,17},{17,25},{25,1},{2,10},{10... | collective-permute-start | bytes 147464 | tf_op jit(solution)/shard_map/ppermute | solution.py:495
  5.3 13.1 %all-to-all-start = ((f32[32,1,256]{2,1,0:T(1,128)}), f32[32,1,256]{2,1,0:T(1,128)S(1)}, u32[]{:S(2)}, u32[]{:S(2)}) async-start(f32[32,1,256]{2,1,0:T(1,128)} %get-tuple-element.24), calls=%async_computation | async-start | bytes 65536 | tf_op jit(solution)/shard_map/all_to_all | solution.py:478
  11.3 0.8 %copy-start = (f32[3,2048]{1,0:T(4,128)S(1)}, f32[3,2048]{1,0:T(4,128)}, u32[]{:S(2)}) copy-start(f32[3,2048]{1,0:T(4,128)} %centers_in_ref.1) | copy-start | bytes 73732
  12.0 0.8 %copy-start.1 = (f32[3,2048]{1,0:T(4,128)S(1)}, f32[3,2048]{1,0:T(4,128)}, u32[]{:S(2)}) copy-start(f32[3,2048]{1,0:T(4,128)} %tangents_in_ref.1) | copy-start | bytes 73732
  12.8 0.8 %copy-start.2 = (f32[3,2048]{1,0:T(4,128)S(1)}, f32[3,2048]{1,0:T(4,128)}, u32[]{:S(2)}) copy-start(f32[3,2048]{1,0:T(4,128)} %points_ref.3) | copy-start | bytes 73732
  13.6 0.7 %copy-start.4 = (f32[256]{0:T(256)S(1)}, f32[256]{0:T(256)}, u32[]{:S(2)}) copy-start(f32[256]{0:T(256)} %param.7) | copy-start | bytes 3076
  14.2 0.7 %copy-start.5 = (s32[2048,1]{0,1:T(1,128)S(1)}, s32[2048,1]{0,1:T(1,128)}, u32[]{:S(2)}) copy-start(s32[2048,1]{0,1:T(1,128)} %param.12) | copy-start | bytes 24580
  14.9 0.7 %copy-start.6 = (f32[256]{0:T(256)S(1)}, f32[256]{0:T(256)}, u32[]{:S(2)}) copy-start(f32[256]{0:T(256)} %param.8) | copy-start | bytes 3076
  22.1 19.7 %copy-start.7 = (s32[8]{0:T(128)S(1)}, s32[8]{0:T(128)}, u32[]{:S(2)}) copy-start(s32[8]{0:T(128)} %length_ref.1) | copy-start | bytes 100
  22.1 11.5 %all-to-all-start.1 = ((f32[32,1,256]{2,1,0:T(1,128)}), f32[32,1,256]{2,1,0:T(1,128)S(1)}, u32[]{:S(2)}, u32[]{:S(2)}) async-start(f32[32,1,256]{2,1,0:T(1,128)} %get-tuple-element.30), calls=%async_computation.1 | async-start | bytes 65536 | tf_op jit(solution)/shard_map/all_to_all | solution.py:478
  33.6 18.8 %copy-start.3 = (f32[3,2048]{1,0:T(4,128)S(1)}, f32[3,2048]{1,0:T(4,128)}, u32[]{:S(2)}) copy-start(f32[3,2048]{1,0:T(4,128)} %points_ref.3) | copy-start | bytes 73732
  37.8 14.6 %all-to-all-start.2 = ((f32[32,1,128]{2,1,0:T(1,128)}), f32[32,1,128]{2,1,0:T(1,128)S(1)}, u32[]{:S(2)}, u32[]{:S(2)}) async-start(f32[32,1,128]{2,1,0:T(1,128)} %get-tuple-element.37), calls=%async_computation.2 | async-start | bytes 32768 | tf_op jit(solution)/shard_map/all_to_all | solution.py:478

commit v2 on v0

--- a/solution.py
+++ b/solution.py
@@ -14,6 +14,8 @@
 CHUNK = 128
 GROUP = 4
 TILE = 512
+COLUMNS = 256
+ROWS = 64
 KEEP_BYTES = 16 * 1024 * 1024
 VMEM_LIMIT = 32 * 1024 * 1024
 STREAM_LIMIT = 44 * 1024 * 1024
@@ -69,13 +71,6 @@
     return x.T.astype(jnp.bfloat16)
 
 
-def fold_lanes(x):
-    total = x[:, 0:128]
-    for piece in range(1, x.shape[1] // 128):
-        total = total + x[:, piece * 128:(piece + 1) * 128]
-    return total
-
-
 def iota(shape, axis):
     return lax.broadcasted_iota(jnp.int32, shape, axis)
 
@@ -84,48 +79,56 @@
     return pl.ds(pl.multiple_of(start, size), size)
 
 
-def piece_column(shift, n_col):
-    return lax.rem(lax.axis_index("col") + n_col - shift, n_col)
-
-
-def couple(pieces, vec_ref, acc_ref, kept=None, right_ref=None, moment_ref=None):
-    seg_dev = acc_ref.shape[0]
-    n_col = len(pieces)
+def sides_kernel(*refs, n_col):
+    pieces, (right_ref, moment_ref, left_ref, along_ref) = refs[:n_col], refs[n_col:]
     length = pieces[0].shape[1]
+    seg_dev = left_ref.shape[0]
     own = pieces[0][:, aligned(lax.axis_index("row") * seg_dev, seg_dev)]
-    lc = transposed(left_parts(left_center(own[0:3] - 0.5, EPS_SEG)))
-    lt = transposed(left_parts(rows8(own[3:6])))
-    acc_ref[...] = jnp.zeros_like(acc_ref)
-    count = length // TILE
+    left_ref[...] = transposed(left_parts(left_center(own[0:3] - 0.5, EPS_SEG)))
+    tangent = rows8(own[3:6]).T
+    for k in range(3):
+        along_ref[k] = jnp.broadcast_to(tangent[:, k:k + 1], (seg_dev, 128))
     for shift, piece in enumerate(pieces):
-        col = piece_column(shift, n_col)
+        col = lax.rem(lax.axis_index("col") + n_col - shift, n_col)
 
         def step(k, carry):
             geo = piece[:, aligned(k * TILE, TILE)]
-            vec_at = pl.ds(pl.multiple_of(col * length + k * TILE, TILE), TILE)
+            to = pl.ds(pl.multiple_of(col * length + k * TILE, TILE), TILE)
             center, tangent = geo[0:3] - 0.5, geo[3:6]
-            rc = right_parts(right_center(center))
-            rt = right_parts(rows8(tangent))
-            pair = dot(lt, rt) * lax.rsqrt(dot(lc, rc))
-            if kept is not None:
-                kept[0][shift * count + k] = pair
-                kept_copy(kept, shift * count + k, out=True).start()
-            if right_ref is not None:
-                cross = jnp.concatenate([
-                    tangent[1:2] * center[2:3] - tangent[2:3] * center[1:2],
-                    tangent[2:3] * center[0:1] - tangent[0:1] * center[2:3],
-                    tangent[0:1] * center[1:2] - tangent[1:2] * center[0:1],
-                ], axis=0)
-                both = rows8(tangent, cross)
-                for part in range(TILE // seg_dev):
-                    row = k * (TILE // seg_dev) + part
-                    block_at = aligned((row * n_col + col) * seg_dev, seg_dev)
-                    right_ref[:, block_at] = rc[:, part * seg_dev:(part + 1) * seg_dev]
-                    moment_ref[:, block_at] = both[:, part * seg_dev:(part + 1) * seg_dev]
-            acc_ref[...] += fold_lanes(pair * vec_ref[:, vec_at])
+            cross = jnp.concatenate([
+                tangent[1:2] * center[2:3] - tangent[2:3] * center[1:2],
+                tangent[2:3] * center[0:1] - tangent[0:1] * center[2:3],
+                tangent[0:1] * center[1:2] - tangent[1:2] * center[0:1],
+            ], axis=0)
+            right_ref[:, to] = right_parts(right_center(center))
+            moment_ref[:, to] = rows8(tangent, cross)
             return carry
 
-        lax.fori_loop(0, count, step, 0, unroll=4)
+        lax.fori_loop(0, length // TILE, step, 0, unroll=4)
+
+
+def couple(right_ref, moment_ref, left_ref, along_ref, vec_ref, acc_ref):
+    acc_ref[...] = jnp.zeros_like(acc_ref)
+
+    def step(k, carry):
+        at = aligned(k * TILE, TILE)
+        turned = moment_ref[0:3, at] * vec_ref[:, at]
+        right = right_ref[:, at]
+        for first in range(0, TILE, COLUMNS):
+            for row in range(0, acc_ref.shape[0], ROWS):
+                rows = slice(row, row + ROWS)
+                inverse = lax.rsqrt(dot(left_ref[rows], right[:, first:first + COLUMNS]))
+                total = acc_ref[rows]
+                for start in range(0, COLUMNS, 128):
+                    lanes = slice(first + start, first + start + 128)
+                    along = along_ref[0, rows] * turned[0:1, lanes]
+                    along = along + along_ref[1, rows] * turned[1:2, lanes]
+                    along = along + along_ref[2, rows] * turned[2:3, lanes]
+                    total = total + along * inverse[:, start:start + 128]
+                acc_ref[rows] = total
+        return carry
+
+    lax.fori_loop(0, vec_ref.shape[1] // TILE, step, 0, unroll=4)
     return jnp.sum(acc_ref[...].T, axis=0, keepdims=True)
 
 
@@ -134,23 +137,6 @@
     if out:
         return pltpu.make_async_copy(local.at[index], remote.at[index], sems.at[index])
     return pltpu.make_async_copy(remote.at[index], local.at[index], sems.at[index])
-
-
-def couple_kept(kept, vec_ref, acc_ref, n_col):
-    acc_ref[...] = jnp.zeros_like(acc_ref)
-    length = vec_ref.shape[1] // n_col
-    count = length // TILE
-    for shift in range(n_col):
-        col = piece_column(shift, n_col)
-
-        def step(k, carry):
-            kept_copy(kept, shift * count + k, out=False).wait()
-            vec_at = pl.ds(pl.multiple_of(col * length + k * TILE, TILE), TILE)
-            acc_ref[...] += fold_lanes(kept[0][shift * count + k] * vec_ref[:, vec_at])
-            return carry
-
-        lax.fori_loop(0, count, step, 0, unroll=2)
-    return jnp.sum(acc_ref[...].T, axis=0, keepdims=True)
 
 
 def spread_rows(ref, row):
@@ -170,39 +156,20 @@
     geo_ref[3:6] = tangents[...]
 
 
-def first_kernel(coupling, n_col, keep, drive_ref, drive_own_ref, resist_ref, after_ref, *refs):
-    pieces, refs = refs[:n_col], refs[n_col:]
-    image_ref, spread_ref, right_ref, moment_ref = refs[0:4]
-    kept = None
-    if keep:
-        kept_hbm = refs[4]
-        vec_ref, acc_ref, kept_ref, sems = refs[5:]
-        kept = (kept_ref, kept_hbm, sems)
-    else:
-        vec_ref, acc_ref = refs[4:]
+def first_kernel(coupling, drive_ref, drive_own_ref, resist_ref, after_ref, right_ref, moment_ref, left_ref, along_ref,
+                 image_ref, spread_ref, vec_ref, acc_ref):
     drive = drive_ref[...]
     scale = 1.0 / jnp.sqrt(jnp.sum(drive * drive, keepdims=True))
     vec_ref[...] = drive * scale
-    product = couple(pieces, vec_ref, acc_ref, kept, right_ref, moment_ref)
+    product = couple(right_ref, moment_ref, left_ref, along_ref, vec_ref, acc_ref)
     image = resist_ref[...] * (drive_own_ref[...] * scale) + coupling * product
     image_ref[...] = image
     spread_rows(spread_ref, image)
-    if keep:
-        for index in range(kept_ref.shape[0]):
-            kept_copy(kept, index, out=True).wait()
-
-
-def second_kernel(coupling, n_col, keep, drive_ref, image_ref, drive_own_ref, image_own_ref, resist_ref, after_ref, *refs):
-    if keep:
-        kept_hbm, refs = refs[0], refs[1:]
-        vec_ref, acc_ref, kept_ref, sems = refs[4:]
-        kept = (kept_ref, kept_hbm, sems)
-        for index in range(kept_ref.shape[0]):
-            kept_copy(kept, index, out=False).start()
-    else:
-        pieces, refs = refs[:n_col], refs[n_col:]
-        vec_ref, acc_ref = refs[4:]
-    basis_ref, basis_own_ref, stats_ref, known_ref = refs[0:4]
+
+
+def second_kernel(coupling, drive_ref, image_ref, drive_own_ref, image_own_ref, resist_ref, after_ref,
+                  right_ref, moment_ref, left_ref, along_ref,
+                  basis_ref, basis_own_ref, stats_ref, known_ref, vec_ref, acc_ref):
     drive = drive_ref[...]
     norm = jnp.sqrt(jnp.sum(drive * drive, keepdims=True))
     scale = 1.0 / norm
@@ -220,10 +187,7 @@
     own_b = (image_own_ref[...] - hessen_a * own_a) * inverse
     basis_own_ref[0:1, :] = own_a
     basis_own_ref[1:2, :] = own_b
-    if keep:
-        product = couple_kept(kept, vec_ref, acc_ref, n_col)
-    else:
-        product = couple(pieces, vec_ref, acc_ref)
+    product = couple(right_ref, moment_ref, left_ref, along_ref, vec_ref, acc_ref)
     second = resist_ref[...] * own_b + coupling * product
     lane = iota((1, 128), 1)
 
@@ -297,19 +261,28 @@
     return high, (cube - high.astype(jnp.float32)).astype(jnp.bfloat16)
 
 
-def weigh_kernel(group_ref, left_ref, right_ref, cubes_hbm, done_ref, cubes_ref, sems, *, n_row):
-    width = right_ref.shape[1] // n_row
+def block_part(block, col, n_row, seg_dev):
+    return aligned((col * n_row + block) * seg_dev, seg_dev)
+
+
+def chunk_steps(group_ref):
+    return (group_ref[1, 0] + GROUP - 1) // GROUP
+
+
+def weigh_kernel(group_ref, left_ref, right_ref, cubes_hbm, done_ref, cubes_ref, sems, *, n_row, n_col):
+    seg_dev = right_ref.shape[1] // (n_row * n_col)
     done_ref[...] = jnp.zeros_like(done_ref)
     kept = (cubes_ref, cubes_hbm, sems)
-    steps = (group_ref[1, 0] + GROUP - 1) // GROUP
 
     def step(k, carry):
         for part in range(GROUP):
             chunk = k * GROUP + part
-            block_at = aligned(group_ref[0, chunk] * width, width)
-            high, low = cube_halves(left_ref[aligned(chunk * CHUNK, CHUNK), :], right_ref[:, block_at])
-            cubes_ref[chunk, 0:CHUNK] = high
-            cubes_ref[chunk, CHUNK:2 * CHUNK] = low
+            left = left_ref[aligned(chunk * CHUNK, CHUNK), :]
+            for col in range(n_col):
+                to = slice(col * seg_dev, (col + 1) * seg_dev)
+                high, low = cube_halves(left, right_ref[:, block_part(group_ref[0, chunk], col, n_row, seg_dev)])
+                cubes_ref[chunk, 0:CHUNK, to] = high
+                cubes_ref[chunk, CHUNK:2 * CHUNK, to] = low
             kept_copy(kept, chunk, out=True).start()
         return carry
 
@@ -318,13 +291,11 @@
             kept_copy(kept, k * GROUP + part, out=True).wait()
         return carry
 
-    lax.fori_loop(0, steps, step, 0)
-    lax.fori_loop(0, steps, finish, 0)
+    lax.fori_loop(0, chunk_steps(group_ref), step, 0)
+    lax.fori_loop(0, chunk_steps(group_ref), finish, 0)
 
 
 def field_kernel(group_ref, length_ref, slot_ref, moment_ref, basis_ref, *refs, n_row, n_col, keep):
-    chunk_count = refs[-1].shape[0] // 16 if not keep else refs[-3].shape[0] // 16
-    steps = (group_ref[1, 0] + GROUP - 1) // GROUP
     if keep:
         cubes_hbm, out_ref, table_ref, sums_ref, cubes_ref, sems = refs
         kept = (cubes_ref, cubes_hbm, sems)
@@ -334,48 +305,55 @@
                 kept_copy(kept, k * GROUP + part, out=False).start()
             return carry
 
-        lax.fori_loop(0, steps, begin, 0)
+        lax.fori_loop(0, chunk_steps(group_ref), begin, 0)
     else:
         left_ref, right_ref, out_ref, table_ref, sums_ref = refs
-    segments = moment_ref.shape[1]
-    width = segments // n_row
-    seg_dev = width // n_col
-    scale = 1.0 / math.sqrt(width)
+    chunk_count = sums_ref.shape[0] // 16
+    seg_dev = moment_ref.shape[1] // (n_row * n_col)
+    scale = 1.0 / math.sqrt(n_col * seg_dev)
     lane = iota((1, seg_dev), 1)
     sums_ref[...] = jnp.zeros_like(sums_ref)
 
     def table_step(block, carry):
         length = length_ref[block]
         for col in range(n_col):
-            vec_at = aligned((col * n_row + block) * seg_dev, seg_dev)
-            block_at = aligned((block * n_col + col) * seg_dev, seg_dev)
-            both = moment_ref[:, block_at]
+            at = block_part(block, col, n_row, seg_dev)
+            both = moment_ref[:, at]
             active = jnp.where(lane + col * seg_dev < length, scale, 0.0)
-            first = both * (basis_ref[0:1, vec_at] * active)
-            second = both * (basis_ref[1:2, vec_at] * active)
+            first = both * (basis_ref[0:1, at] * active)
+            second = both * (basis_ref[1:2, at] * active)
             parts = jnp.concatenate([first, second], axis=0)
             high = parts.astype(jnp.bfloat16).astype(jnp.float32)
-            table_ref[:, block_at] = jnp.concatenate([high, parts - high], axis=0).astype(jnp.bfloat16)
+            table_ref[:, at] = jnp.concatenate([high, parts - high], axis=0).astype(jnp.bfloat16)
         return carry
 
-    lax.fori_loop(0, n_row, table_step, 0, unroll=2)
+    lax.fori_loop(0, n_row, table_step, 0, unroll=min(n_row, 8))
+
+    def block_row(ref, chunk):
+        block = group_ref[0, chunk]
+        return jnp.concatenate([ref[:, block_part(block, col, n_row, seg_dev)] for col in range(n_col)], axis=1)
+
+    def cubes_of(chunk):
+        return jnp.concatenate(cube_halves(left_ref[aligned(chunk * CHUNK, CHUNK), :], block_row(right_ref, chunk)), axis=0)
 
     def step(k, carry):
-        for part in range(GROUP):
+        for part in range(0, GROUP, 2):
             chunk = k * GROUP + part
-            block_at = aligned(group_ref[0, chunk] * width, width)
+            tables = jnp.concatenate([block_row(table_ref, chunk), block_row(table_ref, chunk + 1)], axis=0)
             if keep:
                 kept_copy(kept, chunk, out=False).wait()
-                cubes = cubes_ref[chunk]
+                kept_copy(kept, chunk + 1, out=False).wait()
+                cubes = cubes_ref[pl.ds(chunk, 2)].reshape(4 * CHUNK, n_col * seg_dev)
             else:
-                high, low = cube_halves(left_ref[aligned(chunk * CHUNK, CHUNK), :], right_ref[:, block_at])
-                cubes = jnp.concatenate([high, low], axis=0)
-            both = dot_nt(cubes, table_ref[:, block_at])
-            total = (both[0:CHUNK] + both[CHUNK:2 * CHUNK]).T
-            sums_ref[pl.ds(chunk, 16, stride=chunk_count), :] = total[0:16] + total[16:32]
+                cubes = jnp.concatenate([cubes_of(chunk), cubes_of(chunk + 1)], axis=0)
+            both = dot_nt(tables, cubes)
+            for half in range(2):
+                mine = both[32 * half:32 * half + 32, 2 * CHUNK * half:2 * CHUNK * (half + 1)]
+                total = mine[:, 0:CHUNK] + mine[:, CHUNK:2 * CHUNK]
+                sums_ref[pl.ds(chunk + half, 16, stride=chunk_count), :] = total[0:16] + total[16:32]
         return carry
 
-    lax.fori_loop(0, steps, step, 0)
+    lax.fori_loop(0, chunk_steps(group_ref), step, 0)
     sums = jnp.concatenate([sums_ref[0:6 * chunk_count], sums_ref[8 * chunk_count:14 * chunk_count]], axis=0)
     sums = jnp.concatenate(split3(sums), axis=1).astype(jnp.bfloat16)
     for tile in range(slot_ref.shape[1] // TILE):
@@ -424,12 +402,8 @@
     width = n_col * seg_dev
     points_count = iron_points.shape[1]
     coupling = 0.5 / math.sqrt(segments)
-    keep = seg_dev * segments * 4 <= KEEP_BYTES
-    tiles = segments // TILE
     call = functools.partial(pl.pallas_call, compiler_params=pltpu.CompilerParams(vmem_limit_bytes=VMEM_LIMIT))
     scratch = [pltpu.VMEM((1, segments), jnp.float32), pltpu.VMEM((seg_dev, 128), jnp.float32)]
-    if keep:
-        scratch += [pltpu.VMEM((tiles, seg_dev, TILE), jnp.float32), pltpu.SemaphoreType.DMA((tiles,))]
     hbm = pl.BlockSpec(memory_space=pltpu.HBM)
     smem = pl.BlockSpec(memory_space=pltpu.SMEM)
     vmem = pl.BlockSpec(memory_space=pltpu.VMEM)
@@ -479,26 +453,33 @@
     )(owner.reshape(1, points_count), iron_points, drive[None, :], resist[None, :], centers, tangents)
     pieces = [own_geometry] + pieces
 
+    cube_shape = (chunk_count, 2 * CHUNK, width)
+    keep = 2 * math.prod(cube_shape) <= KEEP_BYTES
     stream = functools.partial(
         pl.pallas_call, compiler_params=pltpu.CompilerParams(vmem_limit_bytes=STREAM_LIMIT if keep else VMEM_LIMIT)
     )
-    first = stream(
-        functools.partial(first_kernel, coupling, n_col, keep),
+    sides = call(
+        functools.partial(sides_kernel, n_col=n_col),
         out_shape=(
-            shape(1, seg_dev), shape(n_dev, 1, seg_dev), shape(48, segments, dtype=jnp.bfloat16), shape(8, segments),
-        ) + ((shape(roomy(seg_dev * TILE * 4), seg_dev, TILE),) if keep else ()),
-        out_specs=(vmem,) * 4 + ((hbm,) if keep else ()),
+            shape(48, segments, dtype=jnp.bfloat16), shape(8, segments),
+            shape(seg_dev, 48, dtype=jnp.bfloat16), shape(3, seg_dev, 128),
+        ),
+        cost_estimate=work(1),
+        name="sides",
+    )(*pieces)
+    right, moment = sides[0:2]
+    image_own, image_spread = call(
+        functools.partial(first_kernel, coupling),
+        out_shape=(shape(1, seg_dev), shape(n_dev, 1, seg_dev)),
         scratch_shapes=scratch,
-        cost_estimate=work(5),
+        cost_estimate=work(3),
         name="first_image",
-    )(drive_all, drive_own, resist_own, group_table, *pieces)
-    image_own, image_spread, right, moment = first[0:4]
+    )(drive_all, drive_own, resist_own, group_table, *sides)
     image_all = exchange(image_spread).reshape(1, segments)
-    cube_shape = (chunk_count, 2 * CHUNK, width)
     cube_scratch = [pltpu.VMEM(cube_shape, jnp.bfloat16), pltpu.SemaphoreType.DMA((chunk_count,))]
     if keep:
         cubes, after = stream(
-            functools.partial(weigh_kernel, n_row=n_row),
+            functools.partial(weigh_kernel, n_row=n_row, n_col=n_col),
             out_shape=(shape(roomy(4 * CHUNK * width), *cube_shape[1:], dtype=jnp.bfloat16), shape(8, 128)),
             in_specs=[smem, vmem, vmem],
             out_specs=(hbm, vmem),
@@ -508,14 +489,13 @@
         )(group_table, left, right)
     else:
         after = group_table
-    basis, basis_own, stats, known = stream(
-        functools.partial(second_kernel, coupling, n_col, keep),
+    basis, basis_own, stats, known = call(
+        functools.partial(second_kernel, coupling),
         out_shape=(shape(2, segments), shape(2, seg_dev), shape(n_dev, 1, 128), shape(1, 128)),
-        in_specs=[vmem] * 6 + ([hbm] if keep else [vmem] * n_col),
         scratch_shapes=scratch,
-        cost_estimate=work(2),
+        cost_estimate=work(3),
         name="second_image",
-    )(drive_all, image_all, drive_own, image_own, resist_own, after, *(first[4:5] if keep else pieces))
+    )(drive_all, image_all, drive_own, image_own, resist_own, after, *sides)
     stats_all = exchange(stats)
 
     field = stream(

time: 56.3 us -> 52.1 us (0.925)
  Pallas kernels: 29.4 us -> 25.5 us
  waiting for transfers between devices: 3.45 us -> 2.75 us
  starting transfers between devices: 17.5 us -> 18.1 us
    pallas_call x1, Pallas kernels: 11.5 us -> 7.51 us  [shards(): stream(functools.partial(field_kernel, n_row=n_row, n_col=n_col, keep=kee...]
    all_to_all x3, waiting for transfers between devices: 3.44 us -> 2.74 us  [exchange(): return lax.all_to_all(x, AXES, 0, 0, tiled=True)]
    all_to_all x3, starting transfers between devices: 14.2 us -> 14.9 us  [exchange(): return lax.all_to_all(x, AXES, 0, 0, tiled=True)]
    pallas_call x3 -> x4, Pallas kernels: 14.2 us -> 14.4 us  [the longest x1 5.36 us: shards(): stream(functools.partial(weigh_kernel, n_row=n_row, n_col=n_col), out_sha...]
  transfers between devices with their start and end apart: 6 -> 6, of which waited for: 2 -> 2; matrix products, arithmetic and copies ran while one was open for 0% -> 0% of each run, Pallas kernels for 33% -> 29%
where the time goes in v2:
time: 52.1 us; the launch traced here: 51.5 us
  Pallas kernels  25.5 us (49%)
  starting transfers between devices  18.1 us (35%)
  local copies, waits for them, and re-layouts  4.33 us (8%)
  waiting for transfers between devices  2.75 us (5%)
  between operations  0.77 us (1%)
    all_to_all x3, starting transfers between devices, exchange(): return lax.all_to_all(x, AXES, 0, 0, tiled=True)  14.9 us
    pallas_call x1, Pallas kernels, shards(): stream(functools.partial(field_kernel, n_row=n_row, n_col=n_col, keep=kee...  7.51 us
    pallas_call x1, Pallas kernels, shards(): stream(functools.partial(weigh_kernel, n_row=n_row, n_col=n_col), out_sha...  5.36 us
    pallas_call x1, Pallas kernels, shards(): call(functools.partial(second_kernel, coupling), out_shape=(shape(2, segm...  4.42 us
    unnamed x16, local copies, waits for them, and re-layouts  4.33 us
    pallas_call x1, Pallas kernels, shards(): call(functools.partial(first_kernel, coupling), out_shape=(shape(1, seg_d...  3.94 us
    ppermute x3, starting transfers between devices, shards(): lax.ppermute(geometry, 'col', [(k, (k + shift) % n_col) for k in range(n_...  3.23 us
    all_to_all x3, waiting for transfers between devices, exchange(): return lax.all_to_all(x, AXES, 0, 0, tiled=True)  2.74 us
  transfers between devices with their start and end apart: 6, of which 2 were waited for; matrix products, arithmetic and copies ran while one was open for 0% of the time, Pallas kernels for 29%

profile of v2, /device:TPU:0, one launch (start us, length us, event | category | flops | bytes accessed | tf_op | source)
XLA Modules:
  0.0 51.5 jit_solution(8562630918578399430)
XLA Ops:
  0.6 1.5 %entry.1 = (f32[32,1,256]{2,1,0:T(1,128)}, f32[6,2048]{1,0:T(8,128)}) custom-call(f32[1,256]{1,0:T(1,128)} %bitcast.9, f32[3,2048]{1,0:T(4,128)} %centers_in_ref.1, f32[3,2048]{1,0:T(4,128)} %tangents_in_ref.1), custom_call_target="tpu_custom_call" | custom-call | tf_op jit(solution)/shard_map/entry/pallas_call | solution.py:420
  2.1 2.4 %collective-permute-start.2 = (f32[6,2048]{1,0:T(8,128)}, f32[6,2048]{1,0:T(8,128)S(1)}, u32[]{:S(2)}, u32[]{:S(2)}) collective-permute-start(f32[6,2048]{1,0:T(8,128)} %get-tuple-element.29), channel_id=1, source_target_pairs={{0,24},{8,0},{16,8},{24,16},{1,25},{9,1},{17,9},{25,17},{2,26},{10... | collective-permute-start | bytes 147464 | tf_op jit(solution)/shard_map/ppermute | solution.py:435
  4.5 0.6 %collective-permute-start.1 = (f32[6,2048]{1,0:T(8,128)}, f32[6,2048]{1,0:T(8,128)S(1)}, u32[]{:S(2)}, u32[]{:S(2)}) collective-permute-start(f32[6,2048]{1,0:T(8,128)} %get-tuple-element.29), channel_id=1, source_target_pairs={{0,16},{8,24},{16,0},{24,8},{1,17},{9,25},{17,1},{25,9},{2,18},{10... | collective-permute-start | bytes 147464 | tf_op jit(solution)/shard_map/ppermute | solution.py:435
  5.2 0.2 collective-permute-start
  5.3 5.9 %all-to-all-start = ((f32[32,1,256]{2,1,0:T(1,128)}), f32[32,1,256]{2,1,0:T(1,128)S(1)}, u32[]{:S(2)}, u32[]{:S(2)}) async-start(f32[32,1,256]{2,1,0:T(1,128)} %get-tuple-element.24), calls=%async_computation | async-start | bytes 65536 | tf_op jit(solution)/shard_map/all_to_all | solution.py:418
  11.3 0.0 copy-start
  11.3 0.7 %copy-done = f32[3,2048]{1,0:T(4,128)S(1)} copy-done((f32[3,2048]{1,0:T(4,128)S(1)}, f32[3,2048]{1,0:T(4,128)}, u32[]{:S(2)}) %copy-start) | copy-done | bytes 24600
  12.0 0.8 %copy-done.1 = f32[3,2048]{1,0:T(4,128)S(1)} copy-done((f32[3,2048]{1,0:T(4,128)S(1)}, f32[3,2048]{1,0:T(4,128)}, u32[]{:S(2)}) %copy-start.1) | copy-done | bytes 24600
  12.8 0.8 %copy-done.2 = f32[3,2048]{1,0:T(4,128)S(1)} copy-done((f32[3,2048]{1,0:T(4,128)S(1)}, f32[3,2048]{1,0:T(4,128)}, u32[]{:S(2)}) %copy-start.2) | copy-done | bytes 24600
  13.6 0.7 %copy-done.4 = f32[256]{0:T(256)S(1)} copy-done((f32[256]{0:T(256)S(1)}, f32[256]{0:T(256)}, u32[]{:S(2)}) %copy-start.4) | copy-done | bytes 1048
  14.2 0.7 %copy-done.5 = s32[2048,1]{0,1:T(1,128)S(1)} copy-done((s32[2048,1]{0,1:T(1,128)S(1)}, s32[2048,1]{0,1:T(1,128)}, u32[]{:S(2)}) %copy-start.5) | copy-done | bytes 8216
  14.9 0.7 %copy-done.6 = f32[256]{0:T(256)S(1)} copy-done((f32[256]{0:T(256)S(1)}, f32[256]{0:T(256)}, u32[]{:S(2)}) %copy-start.6) | copy-done | bytes 1048
  15.6 1.2 %group_points.1 = (s32[1,2048]{1,0:T(1,128)S(1)}, s32[8,128]{1,0:T(8,128)S(1)}, bf16[3072,48]{1,0:T(8,128)(2,1)S(1)}, f32[1,256]{1,0:T(1,128)S(1)}, f32[1,256]{1,0:T(1,128)S(1)}, /*index=5*/f32[6,2048]{1,0:T(8,128)S(1)}) custom-call(s32[1,2048]{1,0:T(1,128)S(1)} %bitcast.11, f32[3,2048]{1,0:T(4,128)S(1)} %copy-done.2, f32[1,256]{1,0:T(1,128)S(1)} %bitcast.10, ...), custom_call_target="tpu_custom_call" | custom-call | flops 3000000000 | tf_op jit(solution)/shard_map/group_points/pallas_call | solution.py:440
  16.9 0.6 %sides.1 = (bf16[48,8192]{1,0:T(8,128)(2,1)S(1)}, f32[8,8192]{1,0:T(8,128)S(1)}, bf16[256,48]{1,0:T(8,128)(2,1)S(1)}, f32[3,256,128]{2,1,0:T(8,128)S(1)}) custom-call(f32[6,2048]{1,0:T(8,128)S(1)} %get-tuple-element.28.refs_0_, f32[6,2048]{1,0:T(8,128)S(1)} %collective-permute-done.refs_1_, f32[6,2048]{1,0:T(8,128)S(1)} %collective-permute-done.1.refs_2_, ...), custom_call_target="tpu_custom_call" | custom-call | flops 1000000000 | tf_op jit(solution)/shard_map/sides/pallas_call | solution.py:461
  17.5 0.0 copy-start.7
  17.5 0.9 %all-to-all-done = f32[32,1,256]{2,1,0:T(1,128)S(1)} async-done(((f32[32,1,256]{2,1,0:T(1,128)}), f32[32,1,256]{2,1,0:T(1,128)S(1)}, u32[]{:S(2)}, u32[]{:S(2)}) %all-to-all-start) | async-done | bytes 32800 | tf_op jit(solution)/shard_map/all_to_all | solution.py:418
  18.5 3.9 %first_image.1 = (f32[1,256]{1,0:T(1,128)S(1)}, f32[32,1,256]{2,1,0:T(1,128)}) custom-call(f32[1,8192]{1,0:T(1,128)S(1)} %bitcast.6, f32[1,256]{1,0:T(1,128)S(1)} %get-tuple-element.25.drive_own_ref, f32[1,256]{1,0:T(1,128)S(1)} %get-tuple-element.26.resist_ref, s32[8,128]{1,0:T(8,128)S(1)} %get-tuple-element.27.after_ref.group_ref, ...), custom_call_target="tpu_custom_call" | custom-call | flops 3000000000 | tf_op jit(solution)/shard_map/first_image/pallas_call | solution.py:471
  22.4 4.9 %all-to-all-start.1 = ((f32[32,1,256]{2,1,0:T(1,128)}), f32[32,1,256]{2,1,0:T(1,128)S(1)}, u32[]{:S(2)}, u32[]{:S(2)}) async-start(f32[32,1,256]{2,1,0:T(1,128)} %get-tuple-element.34), calls=%async_computation.1 | async-start | bytes 65536 | tf_op jit(solution)/shard_map/all_to_all | solution.py:418
  27.3 5.4 %weigh.1 = (bf16[40,256,1024]{2,1,0:T(8,128)(2,1)}, f32[8,128]{1,0:T(8,128)S(1)}) custom-call(s32[8,128]{1,0:T(8,128)S(1)} %get-tuple-element.27.after_ref.group_ref, bf16[3072,48]{1,0:T(8,128)(2,1)S(1)} %get-tuple-element.36.left_ref, bf16[48,8192]{1,0:T(8,128)(2,1)S(1)} %get-tuple-element.30.right_ref), custom_call_target="tpu_custom_call" | custom-call | flops 5000000000 | tf_op jit(solution)/shard_map/weigh/pallas_call | solution.py:481
  32.7 1.8 %all-to-all-done.1 = f32[32,1,256]{2,1,0:T(1,128)S(1)} async-done(((f32[32,1,256]{2,1,0:T(1,128)}), f32[32,1,256]{2,1,0:T(1,128)S(1)}, u32[]{:S(2)}, u32[]{:S(2)}) %all-to-all-start.1) | async-done | bytes 32800 | tf_op jit(solution)/shard_map/all_to_all | solution.py:418
  34.5 4.4 %second_image.1 = (f32[2,8192]{1,0:T(2,128)S(1)}, f32[2,256]{1,0:T(2,128)S(1)}, f32[32,1,128]{2,1,0:T(1,128)}, f32[1,128]{1,0:T(1,128)S(1)}) custom-call(f32[1,8192]{1,0:T(1,128)S(1)} %bitcast.7, f32[1,8192]{1,0:T(1,128)S(1)} %bitcast.8, f32[1,256]{1,0:T(1,128)S(1)} %get-tuple-element.25.drive_own_ref, f32[1,256]{1,0:T(1,128)S(1)} %get-tuple-element.35.image_own_ref, ...), custom_call_target="tpu_custom_call" | custom-call | flops 3000000000 | tf_op jit(solution)/shard_map/second_image/pallas_call | solution.py:492
  38.9 4.1 %all-to-all-start.2 = ((f32[32,1,128]{2,1,0:T(1,128)}), f32[32,1,128]{2,1,0:T(1,128)S(1)}, u32[]{:S(2)}, u32[]{:S(2)}) async-start(f32[32,1,128]{2,1,0:T(1,128)} %get-tuple-element.38), calls=%async_computation.2 | async-start | bytes 32768 | tf_op jit(solution)/shard_map/all_to_all | solution.py:418
  43.0 7.5 %block_field.1.field_ref = f32[12,2048]{1,0:T(8,128)S(1)} custom-call(s32[8,128]{1,0:T(8,128)S(1)} %get-tuple-element.27.after_ref.group_ref, s32[8]{0:T(128)S(1)} %copy-done.7, s32[1,2048]{1,0:T(1,128)S(1)} %get-tuple-element.41.slot_ref, f32[8,8192]{1,0:T(8,128)S(1)} %get-tuple-element.31.moment_ref, f32[2,8192]{1,0:T(2,128)S(1)} %get-tuple-element.42.basis_ref, ...), custom_call_target="tpu_custom_call" | custom-call | flops 6000000000 | tf_op jit(solution)/shard_map/block_field/pallas_call | solution.py:501
  50.5 1.0 %combine.1 = (f32[1,256]{1,0:T(1,128)}, f32[3,2048]{1,0:T(4,128)}) custom-call(f32[32,1,128]{2,1,0:T(1,128)S(1)} %all-to-all-done.2.stats_ref, f32[1,128]{1,0:T(1,128)S(1)} %get-tuple-element.39.known_ref, f32[2,256]{1,0:T(2,128)S(1)} %get-tuple-element.40.basis_own_ref, f32[12,2048]{1,0:T(8,128)S(1)} %block_field.1.field_ref, f32[3,2048]{1,0:T(4,128)S(1)} %copy-done.3), custom_call_target="tpu_custom_call" | custom-call | tf_op jit(solution)/shard_map/combine/pallas_call | solution.py:512
  (12 shorter events, 0.0 us)
Async XLA Ops:
  2.1 14.8 %collective-permute-start.2 = (f32[6,2048]{1,0:T(8,128)}, f32[6,2048]{1,0:T(8,128)S(1)}, u32[]{:S(2)}, u32[]{:S(2)}) collective-permute-start(f32[6,2048]{1,0:T(8,128)} %get-tuple-element.29), channel_id=1, source_target_pairs={{0,24},{8,0},{16,8},{24,16},{1,25},{9,1},{17,9},{25,17},{2,26},{10... | collective-permute-start | bytes 147464 | tf_op jit(solution)/shard_map/ppermute | solution.py:435
  4.5 12.3 %collective-permute-start.1 = (f32[6,2048]{1,0:T(8,128)}, f32[6,2048]{1,0:T(8,128)S(1)}, u32[]{:S(2)}, u32[]{:S(2)}) collective-permute-start(f32[6,2048]{1,0:T(8,128)} %get-tuple-element.29), channel_id=1, source_target_pairs={{0,16},{8,24},{16,0},{24,8},{1,17},{9,25},{17,1},{25,9},{2,18},{10... | collective-permute-start | bytes 147464 | tf_op jit(solution)/shard_map/ppermute | solution.py:435
  5.2 11.7 %collective-permute-start = (f32[6,2048]{1,0:T(8,128)}, f32[6,2048]{1,0:T(8,128)S(1)}, u32[]{:S(2)}, u32[]{:S(2)}) collective-permute-start(f32[6,2048]{1,0:T(8,128)} %get-tuple-element.29), channel_id=1, source_target_pairs={{0,8},{8,16},{16,24},{24,0},{1,9},{9,17},{17,25},{25,1},{2,10},{10... | collective-permute-start | bytes 147464 | tf_op jit(solution)/shard_map/ppermute | solution.py:435
  5.3 13.1 %all-to-all-start = ((f32[32,1,256]{2,1,0:T(1,128)}), f32[32,1,256]{2,1,0:T(1,128)S(1)}, u32[]{:S(2)}, u32[]{:S(2)}) async-start(f32[32,1,256]{2,1,0:T(1,128)} %get-tuple-element.24), calls=%async_computation | async-start | bytes 65536 | tf_op jit(solution)/shard_map/all_to_all | solution.py:418
  11.3 0.8 %copy-start = (f32[3,2048]{1,0:T(4,128)S(1)}, f32[3,2048]{1,0:T(4,128)}, u32[]{:S(2)}) copy-start(f32[3,2048]{1,0:T(4,128)} %centers_in_ref.1) | copy-start | bytes 73732
  12.0 0.8 %copy-start.1 = (f32[3,2048]{1,0:T(4,128)S(1)}, f32[3,2048]{1,0:T(4,128)}, u32[]{:S(2)}) copy-start(f32[3,2048]{1,0:T(4,128)} %tangents_in_ref.1) | copy-start | bytes 73732
  12.8 0.8 %copy-start.2 = (f32[3,2048]{1,0:T(4,128)S(1)}, f32[3,2048]{1,0:T(4,128)}, u32[]{:S(2)}) copy-start(f32[3,2048]{1,0:T(4,128)} %points_ref.3) | copy-start | bytes 73732
  13.6 0.7 %copy-start.4 = (f32[256]{0:T(256)S(1)}, f32[256]{0:T(256)}, u32[]{:S(2)}) copy-start(f32[256]{0:T(256)} %param.7) | copy-start | bytes 3076
  14.2 0.7 %copy-start.5 = (s32[2048,1]{0,1:T(1,128)S(1)}, s32[2048,1]{0,1:T(1,128)}, u32[]{:S(2)}) copy-start(s32[2048,1]{0,1:T(1,128)} %param.12) | copy-start | bytes 24580
  14.9 0.7 %copy-start.6 = (f32[256]{0:T(256)S(1)}, f32[256]{0:T(256)}, u32[]{:S(2)}) copy-start(f32[256]{0:T(256)} %param.8) | copy-start | bytes 3076
  17.5 25.4 %copy-start.7 = (s32[8]{0:T(128)S(1)}, s32[8]{0:T(128)}, u32[]{:S(2)}) copy-start(s32[8]{0:T(128)} %length_ref.1) | copy-start | bytes 100
  22.4 12.1 %all-to-all-start.1 = ((f32[32,1,256]{2,1,0:T(1,128)}), f32[32,1,256]{2,1,0:T(1,128)S(1)}, u32[]{:S(2)}, u32[]{:S(2)}) async-start(f32[32,1,256]{2,1,0:T(1,128)} %get-tuple-element.34), calls=%async_computation.1 | async-start | bytes 65536 | tf_op jit(solution)/shard_map/all_to_all | solution.py:418
  32.7 17.8 %copy-start.3 = (f32[3,2048]{1,0:T(4,128)S(1)}, f32[3,2048]{1,0:T(4,128)}, u32[]{:S(2)}) copy-start(f32[3,2048]{1,0:T(4,128)} %points_ref.3) | copy-start | bytes 73732
  38.9 11.6 %all-to-all-start.2 = ((f32[32,1,128]{2,1,0:T(1,128)}), f32[32,1,128]{2,1,0:T(1,128)S(1)}, u32[]{:S(2)}, u32[]{:S(2)}) async-start(f32[32,1,128]{2,1,0:T(1,128)} %get-tuple-element.38), calls=%async_computation.2 | async-start | bytes 32768 | tf_op jit(solution)/shard_map/all_to_all | solution.py:418

commit v3 on v2

--- a/solution.py
+++ b/solution.py
@@ -81,18 +81,20 @@
 
 def sides_kernel(*refs, n_col):
     pieces, (right_ref, moment_ref, left_ref, along_ref) = refs[:n_col], refs[n_col:]
-    length = pieces[0].shape[1]
-    seg_dev = left_ref.shape[0]
-    own = pieces[0][:, aligned(lax.axis_index("row") * seg_dev, seg_dev)]
-    left_ref[...] = transposed(left_parts(left_center(own[0:3] - 0.5, EPS_SEG)))
-    tangent = rows8(own[3:6]).T
+    length = right_ref.shape[1] // n_col
+    seg_dev = left_ref.shape[1]
+    own_at = aligned(lax.axis_index("row") * seg_dev, seg_dev)
+    tangent = rows8(pieces[0][3:6, own_at])
+    left_ref[0] = transposed(left_parts(left_center(pieces[0][0:3, own_at] - 0.5, EPS_SEG)))
+    left_ref[1] = transposed(left_parts(tangent))
+    tangent = tangent.T
     for k in range(3):
         along_ref[k] = jnp.broadcast_to(tangent[:, k:k + 1], (seg_dev, 128))
     for shift, piece in enumerate(pieces):
         col = lax.rem(lax.axis_index("col") + n_col - shift, n_col)
 
         def step(k, carry):
-            geo = piece[:, aligned(k * TILE, TILE)]
+            geo = piece[0:6, aligned(k * TILE, TILE)]
             to = pl.ds(pl.multiple_of(col * length + k * TILE, TILE), TILE)
             center, tangent = geo[0:3] - 0.5, geo[3:6]
             cross = jnp.concatenate([
@@ -115,16 +117,25 @@
         turned = moment_ref[0:3, at] * vec_ref[:, at]
         right = right_ref[:, at]
         for first in range(0, TILE, COLUMNS):
+            columns = slice(first, first + COLUMNS)
+            by_product = first % (2 * COLUMNS) == 0
+            if by_product:
+                turned_parts = right_parts(rows8(turned[:, columns]))
             for row in range(0, acc_ref.shape[0], ROWS):
                 rows = slice(row, row + ROWS)
-                inverse = lax.rsqrt(dot(left_ref[rows], right[:, first:first + COLUMNS]))
+                inverse = lax.rsqrt(dot(left_ref[0, rows], right[:, columns]))
                 total = acc_ref[rows]
-                for start in range(0, COLUMNS, 128):
-                    lanes = slice(first + start, first + start + 128)
-                    along = along_ref[0, rows] * turned[0:1, lanes]
-                    along = along + along_ref[1, rows] * turned[1:2, lanes]
-                    along = along + along_ref[2, rows] * turned[2:3, lanes]
-                    total = total + along * inverse[:, start:start + 128]
+                if by_product:
+                    pair = dot(left_ref[1, rows], turned_parts) * inverse
+                    for start in range(0, COLUMNS, 128):
+                        total = total + pair[:, start:start + 128]
+                else:
+                    for start in range(0, COLUMNS, 128):
+                        lanes = slice(first + start, first + start + 128)
+                        along = along_ref[0, rows] * turned[0:1, lanes]
+                        along = along + along_ref[1, rows] * turned[1:2, lanes]
+                        along = along + along_ref[2, rows] * turned[2:3, lanes]
+                        total = total + along * inverse[:, start:start + 128]
                 acc_ref[rows] = total
         return carry
 
@@ -144,30 +155,35 @@
         ref[k] = row
 
 
-def entry_kernel(drive_hbm, centers_hbm, tangents_hbm, spread_ref, geo_ref, drive_ref, centers, tangents, sems):
-    pairs = ((drive_hbm, drive_ref), (centers_hbm, centers), (tangents_hbm, tangents))
+def pack_kernel(centers_hbm, tangents_hbm, geo_ref, centers, tangents, sems):
+    pairs = ((centers_hbm, centers), (tangents_hbm, tangents))
     copies = [pltpu.make_async_copy(source, target, sems.at[k]) for k, (source, target) in enumerate(pairs)]
     for copy in copies:
         copy.start()
     for copy in copies:
         copy.wait()
-    spread_rows(spread_ref, drive_ref[...])
     geo_ref[0:3] = centers[...]
     geo_ref[3:6] = tangents[...]
 
 
-def first_kernel(coupling, drive_ref, drive_own_ref, resist_ref, after_ref, right_ref, moment_ref, left_ref, along_ref,
+def own_rows(bundle_ref, like_ref):
+    seg_dev = like_ref.shape[1]
+    return bundle_ref[10:11, 0:seg_dev], bundle_ref[10:11, seg_dev:2 * seg_dev]
+
+
+def first_kernel(coupling, drive_ref, bundle_ref, after_ref, right_ref, moment_ref, left_ref, along_ref,
                  image_ref, spread_ref, vec_ref, acc_ref):
     drive = drive_ref[...]
     scale = 1.0 / jnp.sqrt(jnp.sum(drive * drive, keepdims=True))
     vec_ref[...] = drive * scale
     product = couple(right_ref, moment_ref, left_ref, along_ref, vec_ref, acc_ref)
-    image = resist_ref[...] * (drive_own_ref[...] * scale) + coupling * product
+    drive_own, resist_own = own_rows(bundle_ref, image_ref)
+    image = resist_own * (drive_own * scale) + coupling * product
     image_ref[...] = image
     spread_rows(spread_ref, image)
 
 
-def second_kernel(coupling, drive_ref, image_ref, drive_own_ref, image_own_ref, resist_ref, after_ref,
+def second_kernel(coupling, drive_ref, image_ref, image_own_ref, bundle_ref, after_ref,
                   right_ref, moment_ref, left_ref, along_ref,
                   basis_ref, basis_own_ref, stats_ref, known_ref, vec_ref, acc_ref):
     drive = drive_ref[...]
@@ -183,12 +199,13 @@
     vec_ref[...] = basis_b
     basis_ref[0:1, :] = basis_a
     basis_ref[1:2, :] = basis_b
-    own_a = drive_own_ref[...] * scale
+    drive_own, resist_own = own_rows(bundle_ref, image_own_ref)
+    own_a = drive_own * scale
     own_b = (image_own_ref[...] - hessen_a * own_a) * inverse
     basis_own_ref[0:1, :] = own_a
     basis_own_ref[1:2, :] = own_b
     product = couple(right_ref, moment_ref, left_ref, along_ref, vec_ref, acc_ref)
-    second = resist_ref[...] * own_b + coupling * product
+    second = resist_own * own_b + coupling * product
     lane = iota((1, 128), 1)
 
     def three(a, b, c):
@@ -202,15 +219,10 @@
     known_ref[...] = three(norm, hessen_a, hessen_b)
 
 
-def group_kernel(owner_ref, points_ref, drive_in_ref, resist_in_ref, centers_in_ref, tangents_in_ref,
-                 slot_ref, table_ref, left_ref, drive_ref, resist_ref, geo_ref, planes_ref, *, n_row):
-    drive_ref[...] = drive_in_ref[...]
-    resist_ref[...] = resist_in_ref[...]
-    geo_ref[0:3] = centers_in_ref[...]
-    geo_ref[3:6] = tangents_in_ref[...]
-    points = owner_ref.shape[1]
+def group_kernel(bundle_ref, slot_ref, table_ref, left_ref, planes_ref, *, n_row):
+    points = slot_ref.shape[1]
     chunk_count = left_ref.shape[0] // CHUNK
-    owner = owner_ref[...]
+    owner = bundle_ref[9:10, 0:points].astype(jnp.int32)
     rows = max(8, n_row)
     marks = jnp.where(iota((rows, points), 0) == owner, 1.0, 0.0)
     tile = 256
@@ -238,7 +250,7 @@
     table_ref[...] = jnp.where(place == 0, block, start).astype(jnp.int32)
     high = jnp.where(iota((chunk_count, points), 0) == slot // CHUNK, 1.0, 0.0)
     low = jnp.where(iota((CHUNK, points), 0) == slot % CHUNK, 1.0, 0.0).astype(jnp.bfloat16)
-    parts = split3(points_ref[...] - 0.5)
+    parts = split3(bundle_ref[6:9, 0:points] - 0.5)
     spread = jnp.concatenate([high * part[k:k + 1] for k in range(3) for part in parts], axis=0).astype(jnp.bfloat16)
     placed = dot_nt(spread, low)
     planes = [placed[k * chunk_count:(k + 1) * chunk_count] for k in range(9)]
@@ -367,7 +379,7 @@
             out_ref[row:row + 1, at] = jnp.sum(picked, axis=0, keepdims=True)
 
 
-def final_kernel(stats_ref, known_ref, basis_own_ref, field_ref, points_ref, currents_ref, iron_ref):
+def final_kernel(stats_ref, known_ref, basis_own_ref, field_ref, bundle_ref, currents_ref, iron_ref):
     stats = jnp.sum(stats_ref[...], axis=0)
     known = known_ref[...]
     initial_norm, hessen_a, hessen_b = known[:, 0:1], known[:, 1:2], known[:, 2:3]
@@ -381,7 +393,7 @@
     weight_second = (normal_first * target_second - normal_cross * target_first) / determinant
     currents_ref[...] = weight_first * basis_own_ref[0:1, :] + weight_second * basis_own_ref[1:2, :]
     moments = weight_first * field_ref[0:6, :] + weight_second * field_ref[6:12, :]
-    points = points_ref[...] - 0.5
+    points = bundle_ref[6:9, 0:iron_ref.shape[1]] - 0.5
     px, py, pz = points[0:1], points[1:2], points[2:3]
     iron_ref[0:1, :] = pz * moments[1:2] - py * moments[2:3] - moments[3:4]
     iron_ref[1:2, :] = px * moments[2:3] - pz * moments[0:1] - moments[4:5]
@@ -417,41 +429,46 @@
     def exchange(x):
         return lax.all_to_all(x, AXES, 0, 0, tiled=True)
 
-    spread, geometry = pl.pallas_call(
-        entry_kernel,
-        out_shape=(shape(n_dev, 1, seg_dev), shape(6, col_len)),
-        in_specs=[hbm] * 3,
+    drive_all = exchange(jnp.broadcast_to(drive[None, None, :], (n_dev, 1, seg_dev))).reshape(1, segments)
+    geometry = pl.pallas_call(
+        pack_kernel,
+        out_shape=shape(6, col_len),
+        in_specs=[hbm] * 2,
         scratch_shapes=[
-            pltpu.VMEM((1, seg_dev), jnp.float32),
             pltpu.VMEM((3, col_len), jnp.float32),
             pltpu.VMEM((3, col_len), jnp.float32),
-            pltpu.SemaphoreType.DMA((3,)),
+            pltpu.SemaphoreType.DMA((2,)),
         ],
         compiler_params=pltpu.CompilerParams(vmem_limit_bytes=ENTRY_LIMIT),
-        name="entry",
-    )(drive[None, :], centers, tangents)
-    drive_all = exchange(spread).reshape(1, segments)
-    pieces = [
+        cost_estimate=work(8),
+        name="pack",
+    )(centers, tangents)
+    longest = max(col_len, points_count, 2 * seg_dev)
+
+    def wide(row):
+        return jnp.pad(row, ((0, 0), (0, longest - row.shape[1])))
+
+    bundle = jnp.concatenate([
+        wide(centers), wide(tangents), wide(iron_points), wide(owner.reshape(1, points_count).astype(jnp.float32)),
+        wide(jnp.concatenate([drive, resist])[None, :]),
+    ], axis=0)
+    pieces = [bundle] + [
         lax.ppermute(geometry, "col", [(k, (k + shift) % n_col) for k in range(n_col)]) for shift in range(1, n_col)
     ]
 
     chunk_count = points_count // CHUNK + n_row * (CHUNK - 1) // CHUNK
     chunk_count = -(-chunk_count // 8) * 8
-    slot, group_table, left, drive_own, resist_own, own_geometry = call(
+    slot, group_table, left = call(
         functools.partial(group_kernel, n_row=n_row),
         out_shape=(
             shape(1, points_count, dtype=jnp.int32),
             shape(8, 128, dtype=jnp.int32),
             shape(chunk_count * CHUNK, 48, dtype=jnp.bfloat16),
-            shape(1, seg_dev),
-            shape(1, seg_dev),
-            shape(6, col_len),
         ),
         scratch_shapes=[pltpu.VMEM((48 * chunk_count, CHUNK), jnp.float32)],
         cost_estimate=work(3),
         name="group_points",
-    )(owner.reshape(1, points_count), iron_points, drive[None, :], resist[None, :], centers, tangents)
-    pieces = [own_geometry] + pieces
+    )(bundle)
 
     cube_shape = (chunk_count, 2 * CHUNK, width)
     keep = 2 * math.prod(cube_shape) <= KEEP_BYTES
@@ -462,7 +479,7 @@
         functools.partial(sides_kernel, n_col=n_col),
         out_shape=(
             shape(48, segments, dtype=jnp.bfloat16), shape(8, segments),
-            shape(seg_dev, 48, dtype=jnp.bfloat16), shape(3, seg_dev, 128),
+            shape(2, seg_dev, 48, dtype=jnp.bfloat16), shape(3, seg_dev, 128),
         ),
         cost_estimate=work(1),
         name="sides",
@@ -474,7 +491,7 @@
         scratch_shapes=scratch,
         cost_estimate=work(3),
         name="first_image",
-    )(drive_all, drive_own, resist_own, group_table, *sides)
+    )(drive_all, bundle, group_table, *sides)
     image_all = exchange(image_spread).reshape(1, segments)
     cube_scratch = [pltpu.VMEM(cube_shape, jnp.bfloat16), pltpu.SemaphoreType.DMA((chunk_count,))]
     if keep:
@@ -495,7 +512,7 @@
         scratch_shapes=scratch,
         cost_estimate=work(3),
         name="second_image",
-    )(drive_all, image_all, drive_own, image_own, resist_own, after, *sides)
+    )(drive_all, image_all, image_own, bundle, after, *sides)
     stats_all = exchange(stats)
 
     field = stream(
@@ -513,7 +530,7 @@
         final_kernel,
         out_shape=(shape(1, seg_dev), shape(3, points_count)),
         name="combine",
-    )(stats_all, known, basis_own, field, iron_points)
+    )(stats_all, known, basis_own, field, bundle)
     return (currents[0], iron_field)
 
 

time: 52.1 us -> 48.7 us (0.935)
  waiting for transfers between devices: 2.75 us -> 6.79 us
  local copies, waits for them, and re-layouts: 4.33 us -> 0.89 us
  starting transfers between devices: 18.1 us -> 15.8 us
  Pallas kernels: 25.5 us -> 24.1 us
    unnamed x16 -> x14, local copies, waits for them, and re-layouts: 4.33 us -> 0.03 us
    all_to_all x3, waiting for transfers between devices: 2.74 us -> 6.79 us  [exchange(): return lax.all_to_all(x, AXES, 0, 0, tiled=True)]
    all_to_all x3, starting transfers between devices: 14.9 us -> 12.5 us  [exchange(): return lax.all_to_all(x, AXES, 0, 0, tiled=True)]
    pallas_call x1, Pallas kernels: 3.94 us -> 3.22 us  [shards(): call(functools.partial(first_kernel, coupling), out_shape=(shape(1, seg_d...]
    pallas_call x1, Pallas kernels: 4.42 us -> 3.72 us  [shards(): call(functools.partial(second_kernel, coupling), out_shape=(shape(2, segm...]
    broadcast_in_dim x0 -> x1, local copies, waits for them, and re-layouts: none -> 0.63 us  [shards(): jnp.broadcast_to(drive[None, None, :], (n_dev, 1, seg_dev))]
  transfers between devices with their start and end apart: 6 -> 6, of which waited for: 2 -> 2; matrix products, arithmetic and copies ran while one was open for 0% -> 2% of each run, Pallas kernels for 29% -> 30%
where the time goes in v3:
time: 48.7 us; the launch traced here: 48.5 us
  Pallas kernels  24.1 us (49%)
  starting transfers between devices  15.8 us (32%)
  waiting for transfers between devices  6.79 us (14%)
  local copies, waits for them, and re-layouts  0.89 us (2%)
  between operations  0.85 us (2%)
    all_to_all x3, starting transfers between devices, exchange(): return lax.all_to_all(x, AXES, 0, 0, tiled=True)  12.5 us
    pallas_call x1, Pallas kernels, shards(): stream(functools.partial(field_kernel, n_row=n_row, n_col=n_col, keep=kee...  7.5 us
    all_to_all x3, waiting for transfers between devices, exchange(): return lax.all_to_all(x, AXES, 0, 0, tiled=True)  6.79 us
    pallas_call x1, Pallas kernels, shards(): stream(functools.partial(weigh_kernel, n_row=n_row, n_col=n_col), out_sha...  5.36 us
    pallas_call x1, Pallas kernels, shards(): call(functools.partial(second_kernel, coupling), out_shape=(shape(2, segm...  3.72 us
    ppermute x3, starting transfers between devices, shards(): lax.ppermute(geometry, 'col', [(k, (k + shift) % n_col) for k in range(n_...  3.23 us
    pallas_call x1, Pallas kernels, shards(): call(functools.partial(first_kernel, coupling), out_shape=(shape(1, seg_d...  3.22 us
    pallas_call x1, Pallas kernels, shards(): pl.pallas_call(pack_kernel, out_shape=shape(6, col_len), in_specs=[hbm] *...  1.44 us
  transfers between devices with their start and end apart: 6, of which 2 were waited for; matrix products, arithmetic and copies ran while one was open for 2% of the time, Pallas kernels for 30%

profile of v3, /device:TPU:0, one launch (start us, length us, event | category | flops | bytes accessed | tf_op | source)
XLA Modules:
  0.0 48.5 jit_solution(2088843982732582698)
XLA Ops:
  0.6 0.0 copy-start.2
  0.7 1.4 %pack.1 = f32[6,2048]{1,0:T(8,128)} custom-call(f32[3,2048]{1,0:T(4,128)} %centers_hbm.1, f32[3,2048]{1,0:T(4,128)} %tangents_hbm.1), custom_call_target="tpu_custom_call" | custom-call | flops 8000000000 | tf_op jit(solution)/shard_map/pack/pallas_call | solution.py:433
  2.1 2.4 %collective-permute-start.2 = (f32[6,2048]{1,0:T(8,128)}, f32[6,2048]{1,0:T(8,128)S(1)}, u32[]{:S(2)}, u32[]{:S(2)}) collective-permute-start(f32[6,2048]{1,0:T(8,128)} %pack.1), channel_id=1, source_target_pairs={{0,24},{8,0},{16,8},{24,16},{1,25},{9,1},{17,9},{25,17},{2,26},{10... | collective-permute-start | bytes 147464 | tf_op jit(solution)/shard_map/ppermute | solution.py:456
  4.6 0.6 %collective-permute-start.1 = (f32[6,2048]{1,0:T(8,128)}, f32[6,2048]{1,0:T(8,128)S(1)}, u32[]{:S(2)}, u32[]{:S(2)}) collective-permute-start(f32[6,2048]{1,0:T(8,128)} %pack.1), channel_id=1, source_target_pairs={{0,16},{8,24},{16,0},{24,8},{1,17},{9,25},{17,1},{25,9},{2,18},{10... | collective-permute-start | bytes 147464 | tf_op jit(solution)/shard_map/ppermute | solution.py:456
  5.2 0.2 collective-permute-start
  5.4 0.6 %broadcast_in_dim.4 = f32[32,1,256]{2,1,0:T(1,128)} broadcast(f32[256]{0:T(256)S(1)} %copy-done.5), dimensions={2} | broadcast | bytes 33792 | tf_op jit(solution)/shard_map/broadcast_in_dim | solution.py:432
  6.0 5.9 %all-to-all-start = ((f32[32,1,256]{2,1,0:T(1,128)}), f32[32,1,256]{2,1,0:T(1,128)S(1)}, u32[]{:S(2)}, u32[]{:S(2)}) async-start(f32[32,1,256]{2,1,0:T(1,128)} %broadcast_in_dim.4), calls=%async_computation | async-start | bytes 65536 | tf_op jit(solution)/shard_map/all_to_all | solution.py:430
  12.1 0.2 concatenate.7.bundle_ref.refs_0_
  12.3 1.2 %group_points.1 = (s32[1,2048]{1,0:T(1,128)S(1)}, s32[8,128]{1,0:T(8,128)S(1)}, bf16[3072,48]{1,0:T(8,128)(2,1)S(1)}) custom-call(f32[11,2048]{1,0:T(8,128)S(1)} %concatenate.7.bundle_ref.refs_0_), custom_call_target="tpu_custom_call" | custom-call | flops 3000000000 | tf_op jit(solution)/shard_map/group_points/pallas_call | solution.py:461
  13.5 0.0 collective-permute-done.2.refs_3_
  13.5 0.0 collective-permute-done.1.refs_2_
  13.5 0.0 collective-permute-done.refs_1_
  13.5 0.6 %sides.1 = (bf16[48,8192]{1,0:T(8,128)(2,1)S(1)}, f32[8,8192]{1,0:T(8,128)S(1)}, bf16[2,256,48]{2,1,0:T(8,128)(2,1)S(1)}, f32[3,256,128]{2,1,0:T(8,128)S(1)}) custom-call(f32[11,2048]{1,0:T(8,128)S(1)} %concatenate.7.bundle_ref.refs_0_, f32[6,2048]{1,0:T(8,128)S(1)} %collective-permute-done.refs_1_, f32[6,2048]{1,0:T(8,128)S(1)} %collective-permute-done.1.refs_2_, ...), custom_call_target="tpu_custom_call" | custom-call | flops 1000000000 | tf_op jit(solution)/shard_map/sides/pallas_call | solution.py:478
  14.2 0.0 copy-start
  14.2 5.0 %all-to-all-done = f32[32,1,256]{2,1,0:T(1,128)S(1)} async-done(((f32[32,1,256]{2,1,0:T(1,128)}), f32[32,1,256]{2,1,0:T(1,128)S(1)}, u32[]{:S(2)}, u32[]{:S(2)}) %all-to-all-start) | async-done | bytes 32800 | tf_op jit(solution)/shard_map/all_to_all | solution.py:430
  19.1 3.2 %first_image.1 = (f32[1,256]{1,0:T(1,128)S(1)}, f32[32,1,256]{2,1,0:T(1,128)}) custom-call(f32[1,8192]{1,0:T(1,128)S(1)} %bitcast.6, f32[11,2048]{1,0:T(8,128)S(1)} %concatenate.7.bundle_ref.refs_0_, s32[8,128]{1,0:T(8,128)S(1)} %get-tuple-element.19.after_ref.group_ref, bf16[48,8192]{1,0:T(8,128)(2,1)S(1)} %get-tuple-element.20.right_ref, ...), custom_call_target="tpu_custom_call" | custom-call | flops 3000000000 | tf_op jit(solution)/shard_map/first_image/pallas_call | solution.py:488
  22.4 2.6 %all-to-all-start.1 = ((f32[32,1,256]{2,1,0:T(1,128)}), f32[32,1,256]{2,1,0:T(1,128)S(1)}, u32[]{:S(2)}, u32[]{:S(2)}) async-start(f32[32,1,256]{2,1,0:T(1,128)} %get-tuple-element.24), calls=%async_computation.1 | async-start | bytes 65536 | tf_op jit(solution)/shard_map/all_to_all | solution.py:430
  24.9 5.4 %weigh.1 = (bf16[40,256,1024]{2,1,0:T(8,128)(2,1)}, f32[8,128]{1,0:T(8,128)S(1)}) custom-call(s32[8,128]{1,0:T(8,128)S(1)} %get-tuple-element.19.after_ref.group_ref, bf16[3072,48]{1,0:T(8,128)(2,1)S(1)} %get-tuple-element.26.left_ref, bf16[48,8192]{1,0:T(8,128)(2,1)S(1)} %get-tuple-element.20.right_ref), custom_call_target="tpu_custom_call" | custom-call | flops 5000000000 | tf_op jit(solution)/shard_map/weigh/pallas_call | solution.py:498
  30.3 1.8 %all-to-all-done.1 = f32[32,1,256]{2,1,0:T(1,128)S(1)} async-done(((f32[32,1,256]{2,1,0:T(1,128)}), f32[32,1,256]{2,1,0:T(1,128)S(1)}, u32[]{:S(2)}, u32[]{:S(2)}) %all-to-all-start.1) | async-done | bytes 32800 | tf_op jit(solution)/shard_map/all_to_all | solution.py:430
  32.1 3.7 %second_image.1 = (f32[2,8192]{1,0:T(2,128)S(1)}, f32[2,256]{1,0:T(2,128)S(1)}, f32[32,1,128]{2,1,0:T(1,128)}, f32[1,128]{1,0:T(1,128)S(1)}) custom-call(f32[1,8192]{1,0:T(1,128)S(1)} %bitcast.7, f32[1,8192]{1,0:T(1,128)S(1)} %bitcast.8, f32[1,256]{1,0:T(1,128)S(1)} %get-tuple-element.25.image_own_ref, f32[11,2048]{1,0:T(8,128)S(1)} %concatenate.7.bundle_ref.refs_0_, ...), custom_call_target="tpu_custom_call" | custom-call | flops 3000000000 | tf_op jit(solution)/shard_map/second_image/pallas_call | solution.py:509
  35.8 4.0 %all-to-all-start.2 = ((f32[32,1,128]{2,1,0:T(1,128)}), f32[32,1,128]{2,1,0:T(1,128)S(1)}, u32[]{:S(2)}, u32[]{:S(2)}) async-start(f32[32,1,128]{2,1,0:T(1,128)} %get-tuple-element.28), calls=%async_computation.2 | async-start | bytes 32768 | tf_op jit(solution)/shard_map/all_to_all | solution.py:430
  39.9 7.5 %block_field.1.field_ref = f32[12,2048]{1,0:T(8,128)S(1)} custom-call(s32[8,128]{1,0:T(8,128)S(1)} %get-tuple-element.19.after_ref.group_ref, s32[8]{0:T(128)S(1)} %copy-done, s32[1,2048]{1,0:T(1,128)S(1)} %get-tuple-element.31.slot_ref, f32[8,8192]{1,0:T(8,128)S(1)} %get-tuple-element.21.moment_ref, f32[2,8192]{1,0:T(2,128)S(1)} %get-tuple-element.32.basis_ref, ...), custom_call_target="tpu_custom_call" | custom-call | flops 6000000000 | tf_op jit(solution)/shard_map/block_field/pallas_call | solution.py:518
  47.4 0.0 all-to-all-done.2.stats_ref
  47.4 1.0 %combine.1 = (f32[1,256]{1,0:T(1,128)}, f32[3,2048]{1,0:T(4,128)}) custom-call(f32[32,1,128]{2,1,0:T(1,128)S(1)} %all-to-all-done.2.stats_ref, f32[1,128]{1,0:T(1,128)S(1)} %get-tuple-element.29.known_ref, f32[2,256]{1,0:T(2,128)S(1)} %get-tuple-element.30.basis_own_ref, f32[12,2048]{1,0:T(8,128)S(1)} %block_field.1.field_ref, ...), custom_call_target="tpu_custom_call" | custom-call | tf_op jit(solution)/shard_map/combine/pallas_call | solution.py:529
  (15 shorter events, 0.0 us)
Async XLA Ops:
  0.6 11.4 %copy-start.2 = (f32[3,2048]{1,0:T(4,128)S(1)}, f32[3,2048]{1,0:T(4,128)}, u32[]{:S(2)}) copy-start(f32[3,2048]{1,0:T(4,128)} %tangents_hbm.1) | copy-start | bytes 73732
  0.6 11.4 %copy-start.1 = (f32[3,2048]{1,0:T(4,128)S(1)}, f32[3,2048]{1,0:T(4,128)}, u32[]{:S(2)}) copy-start(f32[3,2048]{1,0:T(4,128)} %centers_hbm.1) | copy-start | bytes 73732
  0.7 4.7 %copy-start.5 = (f32[256]{0:T(256)S(1)}, f32[256]{0:T(256)}, u32[]{:S(2)}) copy-start(f32[256]{0:T(256)} %param.7) | copy-start | bytes 3076
  0.7 11.3 %copy-start.6 = (f32[256]{0:T(256)S(1)}, f32[256]{0:T(256)}, u32[]{:S(2)}) copy-start(f32[256]{0:T(256)} %param.8) | copy-start | bytes 3076
  0.7 11.3 %copy-start.4 = (s32[2048,1]{0,1:T(1,128)S(1)}, s32[2048,1]{0,1:T(1,128)}, u32[]{:S(2)}) copy-start(s32[2048,1]{0,1:T(1,128)} %param.12) | copy-start | bytes 24580
  0.7 11.4 %copy-start.3 = (f32[3,2048]{1,0:T(4,128)S(1)}, f32[3,2048]{1,0:T(4,128)}, u32[]{:S(2)}) copy-start(f32[3,2048]{1,0:T(4,128)} %param.11) | copy-start | bytes 73732
  2.1 11.4 %collective-permute-start.2 = (f32[6,2048]{1,0:T(8,128)}, f32[6,2048]{1,0:T(8,128)S(1)}, u32[]{:S(2)}, u32[]{:S(2)}) collective-permute-start(f32[6,2048]{1,0:T(8,128)} %pack.1), channel_id=1, source_target_pairs={{0,24},{8,0},{16,8},{24,16},{1,25},{9,1},{17,9},{25,17},{2,26},{10... | collective-permute-start | bytes 147464 | tf_op jit(solution)/shard_map/ppermute | solution.py:456
  4.6 8.9 %collective-permute-start.1 = (f32[6,2048]{1,0:T(8,128)}, f32[6,2048]{1,0:T(8,128)S(1)}, u32[]{:S(2)}, u32[]{:S(2)}) collective-permute-start(f32[6,2048]{1,0:T(8,128)} %pack.1), channel_id=1, source_target_pairs={{0,16},{8,24},{16,0},{24,8},{1,17},{9,25},{17,1},{25,9},{2,18},{10... | collective-permute-start | bytes 147464 | tf_op jit(solution)/shard_map/ppermute | solution.py:456
  5.2 8.3 %collective-permute-start = (f32[6,2048]{1,0:T(8,128)}, f32[6,2048]{1,0:T(8,128)S(1)}, u32[]{:S(2)}, u32[]{:S(2)}) collective-permute-start(f32[6,2048]{1,0:T(8,128)} %pack.1), channel_id=1, source_target_pairs={{0,8},{8,16},{16,24},{24,0},{1,9},{9,17},{17,25},{25,1},{2,10},{10... | collective-permute-start | bytes 147464 | tf_op jit(solution)/shard_map/ppermute | solution.py:456
  6.0 13.1 %all-to-all-start = ((f32[32,1,256]{2,1,0:T(1,128)}), f32[32,1,256]{2,1,0:T(1,128)S(1)}, u32[]{:S(2)}, u32[]{:S(2)}) async-start(f32[32,1,256]{2,1,0:T(1,128)} %broadcast_in_dim.4), calls=%async_computation | async-start | bytes 65536 | tf_op jit(solution)/shard_map/all_to_all | solution.py:430
  14.2 25.7 %copy-start = (s32[8]{0:T(128)S(1)}, s32[8]{0:T(128)}, u32[]{:S(2)}) copy-start(s32[8]{0:T(128)} %length_ref.1) | copy-start | bytes 100
  22.4 9.8 %all-to-all-start.1 = ((f32[32,1,256]{2,1,0:T(1,128)}), f32[32,1,256]{2,1,0:T(1,128)S(1)}, u32[]{:S(2)}, u32[]{:S(2)}) async-start(f32[32,1,256]{2,1,0:T(1,128)} %get-tuple-element.24), calls=%async_computation.1 | async-start | bytes 65536 | tf_op jit(solution)/shard_map/all_to_all | solution.py:430
  35.8 11.6 %all-to-all-start.2 = ((f32[32,1,128]{2,1,0:T(1,128)}), f32[32,1,128]{2,1,0:T(1,128)S(1)}, u32[]{:S(2)}, u32[]{:S(2)}) async-start(f32[32,1,128]{2,1,0:T(1,128)} %get-tuple-element.28), calls=%async_computation.2 | async-start | bytes 32768 | tf_op jit(solution)/shard_map/all_to_all | solution.py:430

commit v4 on v3

--- a/solution.py
+++ b/solution.py
@@ -79,34 +79,32 @@
     return pl.ds(pl.multiple_of(start, size), size)
 
 
-def sides_kernel(*refs, n_col):
-    pieces, (right_ref, moment_ref, left_ref, along_ref) = refs[:n_col], refs[n_col:]
-    length = right_ref.shape[1] // n_col
+def make_sides(gathered_ref, vec_ref, right_ref, moment_ref, left_ref, along_ref):
     seg_dev = left_ref.shape[1]
-    own_at = aligned(lax.axis_index("row") * seg_dev, seg_dev)
-    tangent = rows8(pieces[0][3:6, own_at])
-    left_ref[0] = transposed(left_parts(left_center(pieces[0][0:3, own_at] - 0.5, EPS_SEG)))
+    own = gathered_ref[lax.axis_index("col") * lax.axis_size("row") + lax.axis_index("row")]
+    tangent = rows8(own[3:6])
+    left_ref[0] = transposed(left_parts(left_center(own[0:3] - 0.5, EPS_SEG)))
     left_ref[1] = transposed(left_parts(tangent))
     tangent = tangent.T
     for k in range(3):
         along_ref[k] = jnp.broadcast_to(tangent[:, k:k + 1], (seg_dev, 128))
-    for shift, piece in enumerate(pieces):
-        col = lax.rem(lax.axis_index("col") + n_col - shift, n_col)
-
-        def step(k, carry):
-            geo = piece[0:6, aligned(k * TILE, TILE)]
-            to = pl.ds(pl.multiple_of(col * length + k * TILE, TILE), TILE)
-            center, tangent = geo[0:3] - 0.5, geo[3:6]
-            cross = jnp.concatenate([
-                tangent[1:2] * center[2:3] - tangent[2:3] * center[1:2],
-                tangent[2:3] * center[0:1] - tangent[0:1] * center[2:3],
-                tangent[0:1] * center[1:2] - tangent[1:2] * center[0:1],
-            ], axis=0)
-            right_ref[:, to] = right_parts(right_center(center))
-            moment_ref[:, to] = rows8(tangent, cross)
-            return carry
-
-        lax.fori_loop(0, length // TILE, step, 0, unroll=4)
+
+    def step(k, carry):
+        to = aligned(k * seg_dev, seg_dev)
+        geo = gathered_ref[k]
+        center, tangent = geo[0:3] - 0.5, geo[3:6]
+        cross = jnp.concatenate([
+            tangent[1:2] * center[2:3] - tangent[2:3] * center[1:2],
+            tangent[2:3] * center[0:1] - tangent[0:1] * center[2:3],
+            tangent[0:1] * center[1:2] - tangent[1:2] * center[0:1],
+        ], axis=0)
+        right_ref[:, to] = right_parts(right_center(center))
+        moment_ref[:, to] = rows8(tangent, cross)
+        vec_ref[:, to] = geo[6:7]
+        return carry
+
+    lax.fori_loop(0, gathered_ref.shape[0], step, 0, unroll=8)
+    return own[6:7]
 
 
 def couple(right_ref, moment_ref, left_ref, along_ref, vec_ref, acc_ref):
@@ -155,30 +153,31 @@
         ref[k] = row
 
 
-def pack_kernel(centers_hbm, tangents_hbm, geo_ref, centers, tangents, sems):
-    pairs = ((centers_hbm, centers), (tangents_hbm, tangents))
+def pack_kernel(drive_hbm, centers_hbm, tangents_hbm, out_ref, drive, centers, tangents, sems):
+    pairs = ((drive_hbm, drive), (centers_hbm, centers), (tangents_hbm, tangents))
     copies = [pltpu.make_async_copy(source, target, sems.at[k]) for k, (source, target) in enumerate(pairs)]
     for copy in copies:
         copy.start()
     for copy in copies:
         copy.wait()
-    geo_ref[0:3] = centers[...]
-    geo_ref[3:6] = tangents[...]
+    seg_dev = drive.shape[1]
+    at = aligned(lax.axis_index("row") * seg_dev, seg_dev)
+    spread_rows(out_ref, rows8(centers[:, at], tangents[:, at], drive[...]))
 
 
 def own_rows(bundle_ref, like_ref):
     seg_dev = like_ref.shape[1]
-    return bundle_ref[10:11, 0:seg_dev], bundle_ref[10:11, seg_dev:2 * seg_dev]
-
-
-def first_kernel(coupling, drive_ref, bundle_ref, after_ref, right_ref, moment_ref, left_ref, along_ref,
-                 image_ref, spread_ref, vec_ref, acc_ref):
+    return bundle_ref[4:5, 0:seg_dev], bundle_ref[4:5, seg_dev:2 * seg_dev]
+
+
+def first_kernel(coupling, gathered_ref, bundle_ref, after_ref,
+                 image_ref, spread_ref, drive_ref, right_ref, moment_ref, left_ref, along_ref, acc_ref):
+    drive_own = make_sides(gathered_ref, drive_ref, right_ref, moment_ref, left_ref, along_ref)
     drive = drive_ref[...]
     scale = 1.0 / jnp.sqrt(jnp.sum(drive * drive, keepdims=True))
-    vec_ref[...] = drive * scale
-    product = couple(right_ref, moment_ref, left_ref, along_ref, vec_ref, acc_ref)
-    drive_own, resist_own = own_rows(bundle_ref, image_ref)
-    image = resist_own * (drive_own * scale) + coupling * product
+    product = couple(right_ref, moment_ref, left_ref, along_ref, drive_ref, acc_ref)
+    _, resist_own = own_rows(bundle_ref, image_ref)
+    image = (resist_own * drive_own + coupling * product) * scale
     image_ref[...] = image
     spread_rows(spread_ref, image)
 
@@ -222,7 +221,7 @@
 def group_kernel(bundle_ref, slot_ref, table_ref, left_ref, planes_ref, *, n_row):
     points = slot_ref.shape[1]
     chunk_count = left_ref.shape[0] // CHUNK
-    owner = bundle_ref[9:10, 0:points].astype(jnp.int32)
+    owner = bundle_ref[3:4, 0:points].astype(jnp.int32)
     rows = max(8, n_row)
     marks = jnp.where(iota((rows, points), 0) == owner, 1.0, 0.0)
     tile = 256
@@ -250,7 +249,7 @@
     table_ref[...] = jnp.where(place == 0, block, start).astype(jnp.int32)
     high = jnp.where(iota((chunk_count, points), 0) == slot // CHUNK, 1.0, 0.0)
     low = jnp.where(iota((CHUNK, points), 0) == slot % CHUNK, 1.0, 0.0).astype(jnp.bfloat16)
-    parts = split3(bundle_ref[6:9, 0:points] - 0.5)
+    parts = split3(bundle_ref[0:3, 0:points] - 0.5)
     spread = jnp.concatenate([high * part[k:k + 1] for k in range(3) for part in parts], axis=0).astype(jnp.bfloat16)
     placed = dot_nt(spread, low)
     planes = [placed[k * chunk_count:(k + 1) * chunk_count] for k in range(9)]
@@ -393,7 +392,7 @@
     weight_second = (normal_first * target_second - normal_cross * target_first) / determinant
     currents_ref[...] = weight_first * basis_own_ref[0:1, :] + weight_second * basis_own_ref[1:2, :]
     moments = weight_first * field_ref[0:6, :] + weight_second * field_ref[6:12, :]
-    points = bundle_ref[6:9, 0:iron_ref.shape[1]] - 0.5
+    points = bundle_ref[0:3, 0:iron_ref.shape[1]] - 0.5
     px, py, pz = points[0:1], points[1:2], points[2:3]
     iron_ref[0:1, :] = pz * moments[1:2] - py * moments[2:3] - moments[3:4]
     iron_ref[1:2, :] = px * moments[2:3] - pz * moments[0:1] - moments[4:5]
@@ -429,33 +428,29 @@
     def exchange(x):
         return lax.all_to_all(x, AXES, 0, 0, tiled=True)
 
-    drive_all = exchange(jnp.broadcast_to(drive[None, None, :], (n_dev, 1, seg_dev))).reshape(1, segments)
-    geometry = pl.pallas_call(
+    gathered = exchange(pl.pallas_call(
         pack_kernel,
-        out_shape=shape(6, col_len),
-        in_specs=[hbm] * 2,
+        out_shape=shape(n_dev, 8, seg_dev),
+        in_specs=[hbm] * 3,
         scratch_shapes=[
+            pltpu.VMEM((1, seg_dev), jnp.float32),
             pltpu.VMEM((3, col_len), jnp.float32),
             pltpu.VMEM((3, col_len), jnp.float32),
-            pltpu.SemaphoreType.DMA((2,)),
+            pltpu.SemaphoreType.DMA((3,)),
         ],
         compiler_params=pltpu.CompilerParams(vmem_limit_bytes=ENTRY_LIMIT),
-        cost_estimate=work(8),
+        cost_estimate=work(1),
         name="pack",
-    )(centers, tangents)
-    longest = max(col_len, points_count, 2 * seg_dev)
+    )(drive[None, :], centers, tangents))
+    longest = max(points_count, 2 * seg_dev)
 
     def wide(row):
         return jnp.pad(row, ((0, 0), (0, longest - row.shape[1])))
 
     bundle = jnp.concatenate([
-        wide(centers), wide(tangents), wide(iron_points), wide(owner.reshape(1, points_count).astype(jnp.float32)),
+        wide(iron_points), wide(owner.reshape(1, points_count).astype(jnp.float32)),
         wide(jnp.concatenate([drive, resist])[None, :]),
     ], axis=0)
-    pieces = [bundle] + [
-        lax.ppermute(geometry, "col", [(k, (k + shift) % n_col) for k in range(n_col)]) for shift in range(1, n_col)
-    ]
-
     chunk_count = points_count // CHUNK + n_row * (CHUNK - 1) // CHUNK
     chunk_count = -(-chunk_count // 8) * 8
     slot, group_table, left = call(
@@ -475,23 +470,20 @@
     stream = functools.partial(
         pl.pallas_call, compiler_params=pltpu.CompilerParams(vmem_limit_bytes=STREAM_LIMIT if keep else VMEM_LIMIT)
     )
-    sides = call(
-        functools.partial(sides_kernel, n_col=n_col),
+    first = call(
+        functools.partial(first_kernel, coupling),
         out_shape=(
+            shape(1, seg_dev), shape(n_dev, 1, seg_dev), shape(1, segments),
             shape(48, segments, dtype=jnp.bfloat16), shape(8, segments),
             shape(2, seg_dev, 48, dtype=jnp.bfloat16), shape(3, seg_dev, 128),
         ),
-        cost_estimate=work(1),
-        name="sides",
-    )(*pieces)
+        scratch_shapes=scratch[1:],
+        cost_estimate=work(4),
+        name="first_image",
+    )(gathered, bundle, group_table)
+    image_own, image_spread, drive_all = first[0:3]
+    sides = first[3:]
     right, moment = sides[0:2]
-    image_own, image_spread = call(
-        functools.partial(first_kernel, coupling),
-        out_shape=(shape(1, seg_dev), shape(n_dev, 1, seg_dev)),
-        scratch_shapes=scratch,
-        cost_estimate=work(3),
-        name="first_image",
-    )(drive_all, bundle, group_table, *sides)
     image_all = exchange(image_spread).reshape(1, segments)
     cube_scratch = [pltpu.VMEM(cube_shape, jnp.bfloat16), pltpu.SemaphoreType.DMA((chunk_count,))]
     if keep:

time: 48.7 us -> 50.9 us (1.045); the launches traced: 48.5 us -> 50.1 us
  waiting for transfers between devices: 6.79 us -> 9.08 us
  other arithmetic: 0.02 us -> 2.19 us
  starting transfers between devices: 15.8 us -> 13.9 us
  local copies, waits for them, and re-layouts: 0.89 us -> 0.01 us
    ppermute x3 -> x0, starting transfers between devices: 3.23 us -> none  [shards(): lax.ppermute(geometry, 'col', [(k, (k + shift) % n_col) for k in range(n_...]
    all_to_all x3, waiting for transfers between devices: 6.79 us -> 9.08 us  [exchange(): return lax.all_to_all(x, AXES, 0, 0, tiled=True)]
    all_to_all x3, starting transfers between devices: 12.5 us -> 13.9 us  [exchange(): return lax.all_to_all(x, AXES, 0, 0, tiled=True)]
    concatenate x0 -> x1, other arithmetic: none -> 0.78 us  [shards(): jnp.concatenate([wide(iron_points), wide(owner.reshape(1, points_count).a...]
    pallas_call x1, Pallas kernels: 3.22 us -> 3.93 us  [shards(): call(functools.partial(first_kernel, coupling), out_shape=(shape(1, seg_d...]
    convert_element_type x1, other arithmetic: 0.01 us -> 0.71 us  [shards(): owner.reshape(1, points_count).astype(jnp.float32)]
    concatenate x1, other arithmetic: 0.01 us -> 0.7 us  [shards(): jnp.concatenate([drive, resist])[None, :]]
    broadcast_in_dim x1 -> x0, local copies, waits for them, and re-layouts: 0.63 us -> none  [shards(): jnp.broadcast_to(drive[None, None, :], (n_dev, 1, seg_dev))]
  transfers between devices with their start and end apart: 6 -> 3, of which waited for: 2 -> 2; matrix products, arithmetic and copies ran while one was open for 2% -> 4% of each run, Pallas kernels for 30% -> 28%
where the time goes in v4:
time: 50.9 us; the launch traced here: 50.1 us
  Pallas kernels  24.3 us (48%)
  starting transfers between devices  13.9 us (27%)
  waiting for transfers between devices  9.08 us (18%)
  other arithmetic  2.19 us (4%)
  between operations  0.71 us (1%)
    all_to_all x3, starting transfers between devices, exchange(): return lax.all_to_all(x, AXES, 0, 0, tiled=True)  13.9 us
    all_to_all x3, waiting for transfers between devices, exchange(): return lax.all_to_all(x, AXES, 0, 0, tiled=True)  9.08 us
    pallas_call x1, Pallas kernels, shards(): stream(functools.partial(field_kernel, n_row=n_row, n_col=n_col, keep=kee...  7.5 us
    pallas_call x1, Pallas kernels, shards(): stream(functools.partial(weigh_kernel, n_row=n_row, n_col=n_col), out_sha...  5.33 us
    pallas_call x1, Pallas kernels, shards(): call(functools.partial(first_kernel, coupling), out_shape=(shape(1, seg_d...  3.93 us
    pallas_call x1, Pallas kernels, shards(): call(functools.partial(second_kernel, coupling), out_shape=(shape(2, segm...  3.72 us
    pallas_call x1, Pallas kernels, shards(): pl.pallas_call(pack_kernel, out_shape=shape(n_dev, 8, seg_dev), in_specs=...  1.54 us
    pallas_call x1, Pallas kernels, shards(): call(functools.partial(group_kernel, n_row=n_row), out_shape=(shape(1, po...  1.22 us
  transfers between devices with their start and end apart: 3, of which 2 were waited for; matrix products, arithmetic and copies ran while one was open for 4% of the time, Pallas kernels for 28%

profile of v4, /device:TPU:0, one launch (start us, length us, event | category | flops | bytes accessed | tf_op | source)
XLA Modules:
  0.0 50.1 jit_solution(18095209235487522263)
XLA Ops:
  0.6 1.5 %pack.1 = f32[32,8,256]{2,1,0:T(8,128)} custom-call(f32[1,256]{1,0:T(1,128)} %bitcast.8, f32[3,2048]{1,0:T(4,128)} %centers_hbm.1, f32[3,2048]{1,0:T(4,128)} %tangents_hbm.1), custom_call_target="tpu_custom_call" | custom-call | flops 1000000000 | tf_op jit(solution)/shard_map/pack/pallas_call | solution.py:431
  2.2 7.3 %all-to-all-start = ((f32[32,8,256]{2,1,0:T(8,128)}), f32[32,8,256]{2,1,0:T(8,128)S(1)}, u32[]{:S(2)}, u32[]{:S(2)}) async-start(f32[32,8,256]{2,1,0:T(8,128)} %pack.1), calls=%async_computation | async-start | bytes 524288 | tf_op jit(solution)/shard_map/all_to_all | solution.py:429
  9.5 0.7 %convert_bitcast_fusion = f32[1,2048]{1,0:T(1,128)S(1)} fusion(s32[2048,1]{0,1:T(1,128)} %param.12), kind=kLoop, calls=%fused_computation.2 | loop fusion | flops 2048 | bytes 16384 | tf_op jit(solution)/shard_map/convert_element_type | solution.py:451
  10.2 0.7 %pad_maximum_fusion = f32[512]{0:T(512)S(1)} fusion(f32[256]{0:T(256)} %param.8, f32[256]{0:T(256)} %param.7), kind=kLoop, calls=%fused_computation.3 | loop fusion | flops 512 | bytes 4096 | tf_op jit(solution)/shard_map/concatenate | solution.py:452
  10.9 0.8 %select_maximum_fusion.bundle_ref = f32[5,2048]{1,0:T(8,128)S(1)} fusion(f32[1,512]{1,0:T(1,128)S(1)} %bitcast.7, f32[1,2048]{1,0:T(1,128)S(1)} %convert_bitcast_fusion, f32[3,2048]{1,0:T(4,128)} %param.11), kind=kLoop, calls=%fused_computation | loop fusion | flops 40960 | bytes 75776 | tf_op jit(solution)/shard_map/concatenate | solution.py:450
  11.7 1.2 %group_points.1 = (s32[1,2048]{1,0:T(1,128)S(1)}, s32[8,128]{1,0:T(8,128)S(1)}, bf16[3072,48]{1,0:T(8,128)(2,1)S(1)}) custom-call(f32[5,2048]{1,0:T(8,128)S(1)} %select_maximum_fusion.bundle_ref), custom_call_target="tpu_custom_call" | custom-call | flops 3000000000 | tf_op jit(solution)/shard_map/group_points/pallas_call | solution.py:456
  12.9 7.2 %all-to-all-done.gathered_ref = f32[32,8,256]{2,1,0:T(8,128)S(1)} async-done(((f32[32,8,256]{2,1,0:T(8,128)}), f32[32,8,256]{2,1,0:T(8,128)S(1)}, u32[]{:S(2)}, u32[]{:S(2)}) %all-to-all-start) | async-done | bytes 262176 | tf_op jit(solution)/shard_map/all_to_all | solution.py:429
  20.1 0.0 copy-start
  20.1 3.9 %first_image.1 = (f32[1,256]{1,0:T(1,128)S(1)}, f32[32,1,256]{2,1,0:T(1,128)}, f32[1,8192]{1,0:T(1,128)S(1)}, bf16[48,8192]{1,0:T(8,128)(2,1)S(1)}, f32[8,8192]{...) custom-call(f32[32,8,256]{2,1,0:T(8,128)S(1)} %all-to-all-done.gathered_ref, ...), custom_call_target="tpu_custom_call" | custom-call | flops 4000000000 | tf_op jit(solution)/shard_map/first_image/pallas_call | solution.py:473
  24.1 2.6 %all-to-all-start.1 = ((f32[32,1,256]{2,1,0:T(1,128)}), f32[32,1,256]{2,1,0:T(1,128)S(1)}, u32[]{:S(2)}, u32[]{:S(2)}) async-start(f32[32,1,256]{2,1,0:T(1,128)} %get-tuple-element.22), calls=%async_computation.1 | async-start | bytes 65536 | tf_op jit(solution)/shard_map/all_to_all | solution.py:429
  26.7 5.3 %weigh.1 = (bf16[40,256,1024]{2,1,0:T(8,128)(2,1)}, f32[8,128]{1,0:T(8,128)S(1)}) custom-call(s32[8,128]{1,0:T(8,128)S(1)} %get-tuple-element.20.after_ref.group_ref, bf16[3072,48]{1,0:T(8,128)(2,1)S(1)} %get-tuple-element.24.left_ref, bf16[48,8192]{1,0:T(8,128)(2,1)S(1)} %get-tuple-element.25.right_ref), custom_call_target="tpu_custom_call" | custom-call | flops 5000000000 | tf_op jit(solution)/shard_map/weigh/pallas_call | solution.py:490
  32.0 1.8 %all-to-all-done.1 = f32[32,1,256]{2,1,0:T(1,128)S(1)} async-done(((f32[32,1,256]{2,1,0:T(1,128)}), f32[32,1,256]{2,1,0:T(1,128)S(1)}, u32[]{:S(2)}, u32[]{:S(2)}) %all-to-all-start.1) | async-done | bytes 32800 | tf_op jit(solution)/shard_map/all_to_all | solution.py:429
  33.8 3.7 %second_image.1 = (f32[2,8192]{1,0:T(2,128)S(1)}, f32[2,256]{1,0:T(2,128)S(1)}, f32[32,1,128]{2,1,0:T(1,128)}, f32[1,128]{1,0:T(1,128)S(1)}) custom-call(f32[1,8192]{1,0:T(1,128)S(1)} %get-tuple-element.21.drive_ref, f32[1,8192]{1,0:T(1,128)S(1)} %bitcast.6, f32[1,256]{1,0:T(1,128)S(1)} %get-tuple-element.23.image_own_ref, ...), custom_call_target="tpu_custom_call" | custom-call | flops 3000000000 | tf_op jit(solution)/shard_map/second_image/pallas_call | solution.py:501
  37.6 4.0 %all-to-all-start.2 = ((f32[32,1,128]{2,1,0:T(1,128)}), f32[32,1,128]{2,1,0:T(1,128)S(1)}, u32[]{:S(2)}, u32[]{:S(2)}) async-start(f32[32,1,128]{2,1,0:T(1,128)} %get-tuple-element.30), calls=%async_computation.2 | async-start | bytes 32768 | tf_op jit(solution)/shard_map/all_to_all | solution.py:429
  41.6 0.0 copy-done
  41.6 7.5 %block_field.1.field_ref = f32[12,2048]{1,0:T(8,128)S(1)} custom-call(s32[8,128]{1,0:T(8,128)S(1)} %get-tuple-element.20.after_ref.group_ref, s32[8]{0:T(128)S(1)} %copy-done, s32[1,2048]{1,0:T(1,128)S(1)} %get-tuple-element.33.slot_ref, f32[8,8192]{1,0:T(8,128)S(1)} %get-tuple-element.27.moment_ref, f32[2,8192]{1,0:T(2,128)S(1)} %get-tuple-element.34.basis_ref, ...), custom_call_target="tpu_custom_call" | custom-call | flops 6000000000 | tf_op jit(solution)/shard_map/block_field/pallas_call | solution.py:510
  49.1 0.0 all-to-all-done.2.stats_ref
  49.1 1.0 %combine.1 = (f32[1,256]{1,0:T(1,128)}, f32[3,2048]{1,0:T(4,128)}) custom-call(f32[32,1,128]{2,1,0:T(1,128)S(1)} %all-to-all-done.2.stats_ref, f32[1,128]{1,0:T(1,128)S(1)} %get-tuple-element.31.known_ref, f32[2,256]{1,0:T(2,128)S(1)} %get-tuple-element.32.basis_own_ref, f32[12,2048]{1,0:T(8,128)S(1)} %block_field.1.field_ref, ...), custom_call_target="tpu_custom_call" | custom-call | tf_op jit(solution)/shard_map/combine/pallas_call | solution.py:521
Async XLA Ops:
  2.2 18.0 %all-to-all-start = ((f32[32,8,256]{2,1,0:T(8,128)}), f32[32,8,256]{2,1,0:T(8,128)S(1)}, u32[]{:S(2)}, u32[]{:S(2)}) async-start(f32[32,8,256]{2,1,0:T(8,128)} %pack.1), calls=%async_computation | async-start | bytes 524288 | tf_op jit(solution)/shard_map/all_to_all | solution.py:429
  20.1 21.4 %copy-start = (s32[8]{0:T(128)S(1)}, s32[8]{0:T(128)}, u32[]{:S(2)}) copy-start(s32[8]{0:T(128)} %length_ref.1) | copy-start | bytes 100
  24.1 9.8 %all-to-all-start.1 = ((f32[32,1,256]{2,1,0:T(1,128)}), f32[32,1,256]{2,1,0:T(1,128)S(1)}, u32[]{:S(2)}, u32[]{:S(2)}) async-start(f32[32,1,256]{2,1,0:T(1,128)} %get-tuple-element.22), calls=%async_computation.1 | async-start | bytes 65536 | tf_op jit(solution)/shard_map/all_to_all | solution.py:429
  37.6 11.5 %all-to-all-start.2 = ((f32[32,1,128]{2,1,0:T(1,128)}), f32[32,1,128]{2,1,0:T(1,128)S(1)}, u32[]{:S(2)}, u32[]{:S(2)}) async-start(f32[32,1,128]{2,1,0:T(1,128)} %get-tuple-element.30), calls=%async_computation.2 | async-start | bytes 32768 | tf_op jit(solution)/shard_map/all_to_all | solution.py:429

commit v5 on v3

--- a/solution.py
+++ b/solution.py
@@ -20,7 +20,6 @@
 VMEM_LIMIT = 32 * 1024 * 1024
 STREAM_LIMIT = 44 * 1024 * 1024
 STREAM_BYTES = 20 * 1024 * 1024
-ENTRY_LIMIT = 60 * 1024 * 1024
 
 
 def split3(x):
@@ -79,22 +78,24 @@
     return pl.ds(pl.multiple_of(start, size), size)
 
 
-def sides_kernel(*refs, n_col):
-    pieces, (right_ref, moment_ref, left_ref, along_ref) = refs[:n_col], refs[n_col:]
+def sides_kernel(joined_ref, other_ref, right_ref, moment_ref, left_ref, along_ref, *, offsets):
+    n_col = len(offsets)
+    half = n_col // 2
     length = right_ref.shape[1] // n_col
     seg_dev = left_ref.shape[1]
     own_at = aligned(lax.axis_index("row") * seg_dev, seg_dev)
-    tangent = rows8(pieces[0][3:6, own_at])
-    left_ref[0] = transposed(left_parts(left_center(pieces[0][0:3, own_at] - 0.5, EPS_SEG)))
+    tangent = rows8(joined_ref[0, 3:6, own_at])
+    left_ref[0] = transposed(left_parts(left_center(joined_ref[0, 0:3, own_at] - 0.5, EPS_SEG)))
     left_ref[1] = transposed(left_parts(tangent))
     tangent = tangent.T
     for k in range(3):
         along_ref[k] = jnp.broadcast_to(tangent[:, k:k + 1], (seg_dev, 128))
-    for shift, piece in enumerate(pieces):
-        col = lax.rem(lax.axis_index("col") + n_col - shift, n_col)
+    for index, offset in enumerate(offsets):
+        piece = joined_ref.at[index] if index < half else other_ref.at[index - half]
+        col = jnp.bitwise_xor(lax.axis_index("col"), offset)
 
         def step(k, carry):
-            geo = piece[0:6, aligned(k * TILE, TILE)]
+            geo = piece[:, aligned(k * TILE, TILE)]
             to = pl.ds(pl.multiple_of(col * length + k * TILE, TILE), TILE)
             center, tangent = geo[0:3] - 0.5, geo[3:6]
             cross = jnp.concatenate([
@@ -155,15 +156,17 @@
         ref[k] = row
 
 
-def pack_kernel(centers_hbm, tangents_hbm, geo_ref, centers, tangents, sems):
-    pairs = ((centers_hbm, centers), (tangents_hbm, tangents))
-    copies = [pltpu.make_async_copy(source, target, sems.at[k]) for k, (source, target) in enumerate(pairs)]
-    for copy in copies:
-        copy.start()
-    for copy in copies:
-        copy.wait()
-    geo_ref[0:3] = centers[...]
-    geo_ref[3:6] = tangents[...]
+def join_kernel(*refs):
+    out_ref = refs[-1]
+    if len(refs) == 4:
+        bundle_ref, centers_ref, tangents_ref = refs[0:3]
+        out_ref[0] = bundle_ref[0:6, 0:out_ref.shape[2]]
+        out_ref[1, 0:3] = centers_ref[...]
+        out_ref[1, 3:6] = tangents_ref[...]
+    else:
+        held = refs[0].shape[0]
+        out_ref[0:held] = refs[0][...]
+        out_ref[held:2 * held] = refs[1][...]
 
 
 def own_rows(bundle_ref, like_ref):
@@ -430,19 +433,6 @@
         return lax.all_to_all(x, AXES, 0, 0, tiled=True)
 
     drive_all = exchange(jnp.broadcast_to(drive[None, None, :], (n_dev, 1, seg_dev))).reshape(1, segments)
-    geometry = pl.pallas_call(
-        pack_kernel,
-        out_shape=shape(6, col_len),
-        in_specs=[hbm] * 2,
-        scratch_shapes=[
-            pltpu.VMEM((3, col_len), jnp.float32),
-            pltpu.VMEM((3, col_len), jnp.float32),
-            pltpu.SemaphoreType.DMA((2,)),
-        ],
-        compiler_params=pltpu.CompilerParams(vmem_limit_bytes=ENTRY_LIMIT),
-        cost_estimate=work(8),
-        name="pack",
-    )(centers, tangents)
     longest = max(col_len, points_count, 2 * seg_dev)
 
     def wide(row):
@@ -452,9 +442,21 @@
         wide(centers), wide(tangents), wide(iron_points), wide(owner.reshape(1, points_count).astype(jnp.float32)),
         wide(jnp.concatenate([drive, resist])[None, :]),
     ], axis=0)
-    pieces = [bundle] + [
-        lax.ppermute(geometry, "col", [(k, (k + shift) % n_col) for k in range(n_col)]) for shift in range(1, n_col)
-    ]
+
+    def swap(x, bit):
+        return lax.ppermute(x, "col", [(k, k ^ bit) for k in range(n_col)])
+
+    bit = n_col // 2
+    offsets = [0, bit]
+    joined = call(
+        join_kernel, out_shape=shape(2, 6, col_len), cost_estimate=work(1), name="join"
+    )(bundle, swap(centers, bit), swap(tangents, bit))
+    while bit > 1:
+        bit //= 2
+        other = swap(joined, bit)
+        offsets = offsets + [offset ^ bit for offset in offsets]
+        if bit > 1:
+            joined = call(join_kernel, out_shape=shape(len(offsets), 6, col_len), name="join")(joined, other)
 
     chunk_count = points_count // CHUNK + n_row * (CHUNK - 1) // CHUNK
     chunk_count = -(-chunk_count // 8) * 8
@@ -476,14 +478,14 @@
         pl.pallas_call, compiler_params=pltpu.CompilerParams(vmem_limit_bytes=STREAM_LIMIT if keep else VMEM_LIMIT)
     )
     sides = call(
-        functools.partial(sides_kernel, n_col=n_col),
+        functools.partial(sides_kernel, offsets=offsets),
         out_shape=(
             shape(48, segments, dtype=jnp.bfloat16), shape(8, segments),
             shape(2, seg_dev, 48, dtype=jnp.bfloat16), shape(3, seg_dev, 128),
         ),
         cost_estimate=work(1),
         name="sides",
-    )(*pieces)
+    )(joined, other)
     right, moment = sides[0:2]
     image_own, image_spread = call(
         functools.partial(first_kernel, coupling),

time: 48.7 us -> 49.9 us (1.025)
  waiting for transfers between devices: 6.79 us -> 2.7 us
  starting transfers between devices: 15.8 us -> 18.6 us
  local copies, waits for them, and re-layouts: 0.89 us -> 3.07 us
  other arithmetic: 0.02 us -> 1.4 us
  Pallas kernels: 24.1 us -> 22.9 us
    all_to_all x3, waiting for transfers between devices: 6.79 us -> 1.84 us  [exchange(): return lax.all_to_all(x, AXES, 0, 0, tiled=True)]
    all_to_all x3, starting transfers between devices: 12.5 us -> 16.5 us  [exchange(): return lax.all_to_all(x, AXES, 0, 0, tiled=True)]
    concatenate x1, local copies, waits for them, and re-layouts: 0.22 us -> 1.74 us  [shards(): jnp.concatenate([wide(centers), wide(tangents), wide(iron_points), wide(o...]
    pallas_call x2, Pallas kernels: 2.07 us -> 0.65 us  [the longest x1 0.63 us: shards(): call(functools.partial(sides_kernel, offsets=offsets), out_shape=(shape(4...]
    ppermute x3, starting transfers between devices: 3.23 us -> 2.16 us  [swap(): return lax.ppermute(x, 'col', [(k, k ^ bit) for k in range(n_col)])]
    ppermute x3, waiting for transfers between devices: 0.01 us -> 0.85 us  [swap(): return lax.ppermute(x, 'col', [(k, k ^ bit) for k in range(n_col)])]
    convert_element_type x1, other arithmetic: 0.01 us -> 0.7 us  [shards(): owner.reshape(1, points_count).astype(jnp.float32)]
    concatenate x1, other arithmetic: 0.01 us -> 0.7 us  [shards(): jnp.concatenate([drive, resist])[None, :]]
  transfers between devices with their start and end apart: 6 -> 6, of which waited for: 2 -> 3; matrix products, arithmetic and copies ran while one was open for 2% -> 6% of each run, Pallas kernels for 30% -> 30%
where the time goes in v5:
time: 49.9 us; the launch traced here: 49.4 us
  Pallas kernels  22.9 us (46%)
  starting transfers between devices  18.6 us (37%)
  local copies, waits for them, and re-layouts  3.07 us (6%)
  waiting for transfers between devices  2.7 us (5%)
  other arithmetic  1.4 us (3%)
  between operations  0.74 us (1%)
    all_to_all x3, starting transfers between devices, exchange(): return lax.all_to_all(x, AXES, 0, 0, tiled=True)  16.5 us
    pallas_call x1, Pallas kernels, shards(): stream(functools.partial(field_kernel, n_row=n_row, n_col=n_col, keep=kee...  7.5 us
    pallas_call x1, Pallas kernels, shards(): stream(functools.partial(weigh_kernel, n_row=n_row, n_col=n_col), out_sha...  5.34 us
    pallas_call x1, Pallas kernels, shards(): call(functools.partial(second_kernel, coupling), out_shape=(shape(2, segm...  3.84 us
    pallas_call x1, Pallas kernels, shards(): call(functools.partial(first_kernel, coupling), out_shape=(shape(1, seg_d...  3.33 us
    ppermute x3, starting transfers between devices, swap(): return lax.ppermute(x, 'col', [(k, k ^ bit) for k in range(n_col)])  2.16 us
    all_to_all x3, waiting for transfers between devices, exchange(): return lax.all_to_all(x, AXES, 0, 0, tiled=True)  1.84 us
    concatenate x1, local copies, waits for them, and re-layouts, shards(): jnp.concatenate([wide(centers), wide(tangents), wide(iron_points), wide(o...  1.74 us
  transfers between devices with their start and end apart: 6, of which 3 were waited for; matrix products, arithmetic and copies ran while one was open for 6% of the time, Pallas kernels for 30%

profile of v5, /device:TPU:0, one launch (start us, length us, event | category | flops | bytes accessed | tf_op | source)
XLA Modules:
  0.0 49.4 jit_solution(5853892033351854889)
XLA Ops:
  0.6 1.3 %broadcast_in_dim.4 = f32[32,1,256]{2,1,0:T(1,128)} broadcast(f32[256]{0:T(256)} %param.7), dimensions={2} | broadcast | bytes 33792 | tf_op jit(solution)/shard_map/broadcast_in_dim | solution.py:435
  1.9 7.3 %all-to-all-start = ((f32[32,1,256]{2,1,0:T(1,128)}), f32[32,1,256]{2,1,0:T(1,128)S(1)}, u32[]{:S(2)}, u32[]{:S(2)}) async-start(f32[32,1,256]{2,1,0:T(1,128)} %broadcast_in_dim.4), calls=%async_computation | async-start | bytes 65536 | tf_op jit(solution)/shard_map/all_to_all | solution.py:433
  9.2 1.8 %collective-permute-start = (f32[3,2048]{1,0:T(4,128)}, f32[3,2048]{1,0:T(4,128)S(1)}, u32[]{:S(2)}, u32[]{:S(2)}) collective-permute-start(f32[3,2048]{1,0:T(4,128)} %param.9), channel_id=1, source_target_pairs={{0,16},{8,24},{16,0},{24,8},{1,17},{9,25},{17,1},{25,9},{2,18},{10... | collective-permute-start | bytes 73736 | tf_op jit(solution)/shard_map/ppermute | solution.py:447
  11.1 0.3 collective-permute-start.1
  11.3 0.7 %convert_bitcast_fusion = f32[1,2048]{1,0:T(1,128)S(1)} fusion(s32[2048,1]{0,1:T(1,128)} %param.12), kind=kLoop, calls=%fused_computation | loop fusion | flops 2048 | bytes 16384 | tf_op jit(solution)/shard_map/convert_element_type | solution.py:442
  12.0 0.7 %pad_maximum_fusion = f32[512]{0:T(512)S(1)} fusion(f32[256]{0:T(256)} %param.8, f32[256]{0:T(256)} %param.7), kind=kLoop, calls=%fused_computation.1 | loop fusion | flops 512 | bytes 4096 | tf_op jit(solution)/shard_map/concatenate | solution.py:443
  12.8 1.7 %concatenate.7.bundle_ref.refs_0_ = f32[11,2048]{1,0:T(8,128)S(1)} concatenate(f32[3,2048]{1,0:T(4,128)} %param.9, f32[3,2048]{1,0:T(4,128)} %param.10, f32[3,2048]{1,0:T(4,128)} %param.11, f32[1,2048]{1,0:T(1,128)S(1)} %convert_bitcast_fusion, f32[1,2048]{1,0:T(1,128)S(1)} %pad.4), dimensions={0} | concatenate | bytes 180224 | tf_op jit(solution)/shard_map/concatenate | solution.py:441
  14.5 0.0 collective-permute-done.refs_1_
  14.5 0.7 %collective-permute-done.1.refs_2_ = f32[3,2048]{1,0:T(4,128)S(1)} collective-permute-done((f32[3,2048]{1,0:T(4,128)}, f32[3,2048]{1,0:T(4,128)S(1)}, u32[]{:S(2)}, u32[]{:S(2)}) %collective-permute-start.1) | collective-permute-done | bytes 24608 | tf_op jit(solution)/shard_map/ppermute | solution.py:447
  15.3 0.1 collective-permute-start.2
  15.3 1.2 %group_points.1 = (s32[1,2048]{1,0:T(1,128)S(1)}, s32[8,128]{1,0:T(8,128)S(1)}, bf16[3072,48]{1,0:T(8,128)(2,1)S(1)}) custom-call(f32[11,2048]{1,0:T(8,128)S(1)} %concatenate.7.bundle_ref.refs_0_), custom_call_target="tpu_custom_call" | custom-call | flops 3000000000 | tf_op jit(solution)/shard_map/group_points/pallas_call | solution.py:463
  16.6 0.1 collective-permute-done.2.other_ref
  16.7 0.6 %sides.1 = (bf16[48,8192]{1,0:T(8,128)(2,1)S(1)}, f32[8,8192]{1,0:T(8,128)S(1)}, bf16[2,256,48]{2,1,0:T(8,128)(2,1)S(1)}, f32[3,256,128]{2,1,0:T(8,128)S(1)}) custom-call(f32[2,6,2048]{2,1,0:T(8,128)S(1)} %join.1.joined_ref, f32[2,6,2048]{2,1,0:T(8,128)S(1)} %collective-permute-done.2.other_ref), custom_call_target="tpu_custom_call" | custom-call | flops 1000000000 | tf_op jit(solution)/shard_map/sides/pallas_call | solution.py:480
  17.3 0.0 copy-start
  17.3 0.0 all-to-all-done
  17.3 3.3 %first_image.1 = (f32[1,256]{1,0:T(1,128)S(1)}, f32[32,1,256]{2,1,0:T(1,128)}) custom-call(f32[1,8192]{1,0:T(1,128)S(1)} %bitcast.6, f32[11,2048]{1,0:T(8,128)S(1)} %concatenate.7.bundle_ref.refs_0_, s32[8,128]{1,0:T(8,128)S(1)} %get-tuple-element.19.after_ref.group_ref, bf16[48,8192]{1,0:T(8,128)(2,1)S(1)} %get-tuple-element.20.right_ref, ...), custom_call_target="tpu_custom_call" | custom-call | flops 3000000000 | tf_op jit(solution)/shard_map/first_image/pallas_call | solution.py:490
  20.7 5.1 %all-to-all-start.1 = ((f32[32,1,256]{2,1,0:T(1,128)}), f32[32,1,256]{2,1,0:T(1,128)S(1)}, u32[]{:S(2)}, u32[]{:S(2)}) async-start(f32[32,1,256]{2,1,0:T(1,128)} %get-tuple-element.24), calls=%async_computation.1 | async-start | bytes 65536 | tf_op jit(solution)/shard_map/all_to_all | solution.py:433
  25.8 5.3 %weigh.1 = (bf16[40,256,1024]{2,1,0:T(8,128)(2,1)}, f32[8,128]{1,0:T(8,128)S(1)}) custom-call(s32[8,128]{1,0:T(8,128)S(1)} %get-tuple-element.19.after_ref.group_ref, bf16[3072,48]{1,0:T(8,128)(2,1)S(1)} %get-tuple-element.26.left_ref, bf16[48,8192]{1,0:T(8,128)(2,1)S(1)} %get-tuple-element.20.right_ref), custom_call_target="tpu_custom_call" | custom-call | flops 5000000000 | tf_op jit(solution)/shard_map/weigh/pallas_call | solution.py:500
  31.2 1.8 %all-to-all-done.1 = f32[32,1,256]{2,1,0:T(1,128)S(1)} async-done(((f32[32,1,256]{2,1,0:T(1,128)}), f32[32,1,256]{2,1,0:T(1,128)S(1)}, u32[]{:S(2)}, u32[]{:S(2)}) %all-to-all-start.1) | async-done | bytes 32800 | tf_op jit(solution)/shard_map/all_to_all | solution.py:433
  33.0 3.8 %second_image.1 = (f32[2,8192]{1,0:T(2,128)S(1)}, f32[2,256]{1,0:T(2,128)S(1)}, f32[32,1,128]{2,1,0:T(1,128)}, f32[1,128]{1,0:T(1,128)S(1)}) custom-call(f32[1,8192]{1,0:T(1,128)S(1)} %bitcast.7, f32[1,8192]{1,0:T(1,128)S(1)} %bitcast.8, f32[1,256]{1,0:T(1,128)S(1)} %get-tuple-element.25.image_own_ref, f32[11,2048]{1,0:T(8,128)S(1)} %concatenate.7.bundle_ref.refs_0_, ...), custom_call_target="tpu_custom_call" | custom-call | flops 3000000000 | tf_op jit(solution)/shard_map/second_image/pallas_call | solution.py:511
  36.8 4.0 %all-to-all-start.2 = ((f32[32,1,128]{2,1,0:T(1,128)}), f32[32,1,128]{2,1,0:T(1,128)S(1)}, u32[]{:S(2)}, u32[]{:S(2)}) async-start(f32[32,1,128]{2,1,0:T(1,128)} %get-tuple-element.28), calls=%async_computation.2 | async-start | bytes 32768 | tf_op jit(solution)/shard_map/all_to_all | solution.py:433
  40.9 7.5 %block_field.1.field_ref = f32[12,2048]{1,0:T(8,128)S(1)} custom-call(s32[8,128]{1,0:T(8,128)S(1)} %get-tuple-element.19.after_ref.group_ref, s32[8]{0:T(128)S(1)} %copy-done, s32[1,2048]{1,0:T(1,128)S(1)} %get-tuple-element.31.slot_ref, f32[8,8192]{1,0:T(8,128)S(1)} %get-tuple-element.21.moment_ref, f32[2,8192]{1,0:T(2,128)S(1)} %get-tuple-element.32.basis_ref, ...), custom_call_target="tpu_custom_call" | custom-call | flops 6000000000 | tf_op jit(solution)/shard_map/block_field/pallas_call | solution.py:520
  48.4 0.0 all-to-all-done.2.stats_ref
  48.4 1.0 %combine.1 = (f32[1,256]{1,0:T(1,128)}, f32[3,2048]{1,0:T(4,128)}) custom-call(f32[32,1,128]{2,1,0:T(1,128)S(1)} %all-to-all-done.2.stats_ref, f32[1,128]{1,0:T(1,128)S(1)} %get-tuple-element.29.known_ref, f32[2,256]{1,0:T(2,128)S(1)} %get-tuple-element.30.basis_own_ref, f32[12,2048]{1,0:T(8,128)S(1)} %block_field.1.field_ref, ...), custom_call_target="tpu_custom_call" | custom-call | tf_op jit(solution)/shard_map/combine/pallas_call | solution.py:531
  (3 shorter events, 0.0 us)
Async XLA Ops:
  1.9 15.4 %all-to-all-start = ((f32[32,1,256]{2,1,0:T(1,128)}), f32[32,1,256]{2,1,0:T(1,128)S(1)}, u32[]{:S(2)}, u32[]{:S(2)}) async-start(f32[32,1,256]{2,1,0:T(1,128)} %broadcast_in_dim.4), calls=%async_computation | async-start | bytes 65536 | tf_op jit(solution)/shard_map/all_to_all | solution.py:433
  9.2 5.2 %collective-permute-start = (f32[3,2048]{1,0:T(4,128)}, f32[3,2048]{1,0:T(4,128)S(1)}, u32[]{:S(2)}, u32[]{:S(2)}) collective-permute-start(f32[3,2048]{1,0:T(4,128)} %param.9), channel_id=1, source_target_pairs={{0,16},{8,24},{16,0},{24,8},{1,17},{9,25},{17,1},{25,9},{2,18},{10... | collective-permute-start | bytes 73736 | tf_op jit(solution)/shard_map/ppermute | solution.py:447
  11.1 4.2 %collective-permute-start.1 = (f32[3,2048]{1,0:T(4,128)}, f32[3,2048]{1,0:T(4,128)S(1)}, u32[]{:S(2)}, u32[]{:S(2)}) collective-permute-start(f32[3,2048]{1,0:T(4,128)} %param.10), channel_id=1, source_target_pairs={{0,16},{8,24},{16,0},{24,8},{1,17},{9,25},{17,1},{25,9},{2,18},{10... | collective-permute-start | bytes 73736 | tf_op jit(solution)/shard_map/ppermute | solution.py:447
  15.3 1.4 %collective-permute-start.2 = (f32[2,6,2048]{2,1,0:T(8,128)S(1)}, f32[2,6,2048]{2,1,0:T(8,128)S(1)}, u32[]{:S(2)}, u32[]{:S(2)}) collective-permute-start(f32[2,6,2048]{2,1,0:T(8,128)S(1)} %join.1.joined_ref), channel_id=1, source_target_pairs={{0,8},{8,0},{16,24},{24,16},{1,9},{9,1},{17,25},{25,17},{2,10},{10... | collective-permute-start | bytes 294920 | tf_op jit(solution)/shard_map/ppermute | solution.py:447
  17.3 23.6 %copy-start = (s32[8]{0:T(128)S(1)}, s32[8]{0:T(128)}, u32[]{:S(2)}) copy-start(s32[8]{0:T(128)} %length_ref.1) | copy-start | bytes 100
  20.7 12.3 %all-to-all-start.1 = ((f32[32,1,256]{2,1,0:T(1,128)}), f32[32,1,256]{2,1,0:T(1,128)S(1)}, u32[]{:S(2)}, u32[]{:S(2)}) async-start(f32[32,1,256]{2,1,0:T(1,128)} %get-tuple-element.24), calls=%async_computation.1 | async-start | bytes 65536 | tf_op jit(solution)/shard_map/all_to_all | solution.py:433
  36.8 11.5 %all-to-all-start.2 = ((f32[32,1,128]{2,1,0:T(1,128)}), f32[32,1,128]{2,1,0:T(1,128)S(1)}, u32[]{:S(2)}, u32[]{:S(2)}) async-start(f32[32,1,128]{2,1,0:T(1,128)} %get-tuple-element.28), calls=%async_computation.2 | async-start | bytes 32768 | tf_op jit(solution)/shard_map/all_to_all | solution.py:433

commit v6 on v5

--- a/solution.py
+++ b/solution.py
@@ -19,6 +19,7 @@
 KEEP_BYTES = 16 * 1024 * 1024
 VMEM_LIMIT = 32 * 1024 * 1024
 STREAM_LIMIT = 44 * 1024 * 1024
+ENTRY_LIMIT = 60 * 1024 * 1024
 STREAM_BYTES = 20 * 1024 * 1024
 
 
@@ -154,6 +155,13 @@
 def spread_rows(ref, row):
     for k in range(ref.shape[0]):
         ref[k] = row
+
+
+def spread_kernel(drive_hbm, out_ref, drive, sem):
+    copy = pltpu.make_async_copy(drive_hbm, drive, sem)
+    copy.start()
+    copy.wait()
+    spread_rows(out_ref, drive[...])
 
 
 def join_kernel(*refs):
@@ -432,7 +440,15 @@
     def exchange(x):
         return lax.all_to_all(x, AXES, 0, 0, tiled=True)
 
-    drive_all = exchange(jnp.broadcast_to(drive[None, None, :], (n_dev, 1, seg_dev))).reshape(1, segments)
+    drive_all = exchange(pl.pallas_call(
+        spread_kernel,
+        out_shape=shape(n_dev, 1, seg_dev),
+        in_specs=[hbm],
+        scratch_shapes=[pltpu.VMEM((1, seg_dev), jnp.float32), pltpu.SemaphoreType.DMA],
+        compiler_params=pltpu.CompilerParams(vmem_limit_bytes=ENTRY_LIMIT),
+        cost_estimate=work(8),
+        name="spread",
+    )(drive[None, :])).reshape(1, segments)
     longest = max(col_len, points_count, 2 * seg_dev)
 
     def wide(row):

time: 49.9 us -> 49.3 us (0.988)
  local copies, waits for them, and re-layouts: 3.07 us -> 0.26 us
  waiting for transfers between devices: 2.7 us -> 5.31 us
  other arithmetic: 1.4 us -> 0.01 us
  Pallas kernels: 22.9 us -> 24 us
  starting transfers between devices: 18.6 us -> 18.1 us
    ppermute x3, waiting for transfers between devices: 0.85 us -> 3.49 us  [swap(): return lax.ppermute(x, 'col', [(k, k ^ bit) for k in range(n_col)])]
    concatenate x1, local copies, waits for them, and re-layouts: 1.74 us -> 0.22 us  [shards(): jnp.concatenate([wide(centers), wide(tangents), wide(iron_points), wide(o...]
    pallas_call x0 -> x1, Pallas kernels: none -> 1.32 us  [shards(): pl.pallas_call(spread_kernel, out_shape=shape(n_dev, 1, seg_dev), in_spec...]
    broadcast_in_dim x1 -> x0, local copies, waits for them, and re-layouts: 1.31 us -> none  [shards(): jnp.broadcast_to(drive[None, None, :], (n_dev, 1, seg_dev))]
    convert_element_type x1, other arithmetic: 0.7 us -> 0.01 us  [shards(): owner.reshape(1, points_count).astype(jnp.float32)]
    concatenate x1, other arithmetic: 0.7 us -> 0.01 us  [shards(): jnp.concatenate([drive, resist])[None, :]]
  transfers between devices with their start and end apart: 6 -> 6, of which waited for: 3 -> 4; matrix products, arithmetic and copies ran while one was open for 6% -> 0% of each run, Pallas kernels for 30% -> 30%
where the time goes in v6:
time: 49.3 us; the launch traced here: 48.6 us
  Pallas kernels  24 us (49%)
  starting transfers between devices  18.1 us (37%)
  waiting for transfers between devices  5.31 us (11%)
  between operations  0.83 us (2%)
    all_to_all x3, starting transfers between devices, exchange(): return lax.all_to_all(x, AXES, 0, 0, tiled=True)  16 us
    pallas_call x1, Pallas kernels, shards(): stream(functools.partial(field_kernel, n_row=n_row, n_col=n_col, keep=kee...  7.5 us
    pallas_call x1, Pallas kernels, shards(): stream(functools.partial(weigh_kernel, n_row=n_row, n_col=n_col), out_sha...  5.36 us
    pallas_call x1, Pallas kernels, shards(): call(functools.partial(second_kernel, coupling), out_shape=(shape(2, segm...  3.72 us
    ppermute x3, waiting for transfers between devices, swap(): return lax.ppermute(x, 'col', [(k, k ^ bit) for k in range(n_col)])  3.49 us
    pallas_call x1, Pallas kernels, shards(): call(functools.partial(first_kernel, coupling), out_shape=(shape(1, seg_d...  3.22 us
    ppermute x3, starting transfers between devices, swap(): return lax.ppermute(x, 'col', [(k, k ^ bit) for k in range(n_col)])  2.16 us
    all_to_all x3, waiting for transfers between devices, exchange(): return lax.all_to_all(x, AXES, 0, 0, tiled=True)  1.82 us
  transfers between devices with their start and end apart: 6, of which 4 were waited for; matrix products, arithmetic and copies ran while one was open for 0% of the time, Pallas kernels for 30%

profile of v6, /device:TPU:0, one launch (start us, length us, event | category | flops | bytes accessed | tf_op | source)
XLA Modules:
  0.0 48.6 jit_solution(1035185756661445816)
XLA Ops:
  0.7 1.3 %spread.1 = f32[32,1,256]{2,1,0:T(1,128)} custom-call(f32[1,256]{1,0:T(1,128)} %bitcast.11), custom_call_target="tpu_custom_call" | custom-call | flops 8000000000 | tf_op jit(solution)/shard_map/spread/pallas_call | solution.py:443
  2.0 7.3 %all-to-all-start = ((f32[32,1,256]{2,1,0:T(1,128)}), f32[32,1,256]{2,1,0:T(1,128)S(1)}, u32[]{:S(2)}, u32[]{:S(2)}) async-start(f32[32,1,256]{2,1,0:T(1,128)} %spread.1), calls=%async_computation | async-start | bytes 65536 | tf_op jit(solution)/shard_map/all_to_all | solution.py:441
  9.3 0.0 copy-done.2
  9.3 1.8 %collective-permute-start = (f32[3,2048]{1,0:T(4,128)S(1)}, f32[3,2048]{1,0:T(4,128)S(1)}, u32[]{:S(2)}, u32[]{:S(2)}) collective-permute-start(f32[3,2048]{1,0:T(4,128)S(1)} %copy-done.2), channel_id=1, source_target_pairs={{0,16},{8,24},{16,0},{24,8},{1,17},{9,25},{17,1},{25,9},{2,18},{10... | collective-permute-start | bytes 73736 | tf_op jit(solution)/shard_map/ppermute | solution.py:463
  11.2 0.0 copy-done.3
  11.2 0.3 collective-permute-start.1
  11.5 0.2 concatenate.7.bundle_ref.refs_0_
  11.7 1.6 %collective-permute-done.refs_1_ = f32[3,2048]{1,0:T(4,128)S(1)} collective-permute-done((f32[3,2048]{1,0:T(4,128)S(1)}, f32[3,2048]{1,0:T(4,128)S(1)}, u32[]{:S(2)}, u32[]{:S(2)}) %collective-permute-start) | collective-permute-done | bytes 24608 | tf_op jit(solution)/shard_map/ppermute | solution.py:463
  13.4 1.7 %collective-permute-done.1.refs_2_ = f32[3,2048]{1,0:T(4,128)S(1)} collective-permute-done((f32[3,2048]{1,0:T(4,128)S(1)}, f32[3,2048]{1,0:T(4,128)S(1)}, u32[]{:S(2)}, u32[]{:S(2)}) %collective-permute-start.1) | collective-permute-done | bytes 24608 | tf_op jit(solution)/shard_map/ppermute | solution.py:463
  15.1 0.1 collective-permute-start.2
  15.2 1.2 %group_points.1 = (s32[1,2048]{1,0:T(1,128)S(1)}, s32[8,128]{1,0:T(8,128)S(1)}, bf16[3072,48]{1,0:T(8,128)(2,1)S(1)}) custom-call(f32[11,2048]{1,0:T(8,128)S(1)} %concatenate.7.bundle_ref.refs_0_), custom_call_target="tpu_custom_call" | custom-call | flops 3000000000 | tf_op jit(solution)/shard_map/group_points/pallas_call | solution.py:479
  16.4 0.1 collective-permute-done.2.other_ref
  16.6 0.6 %sides.1 = (bf16[48,8192]{1,0:T(8,128)(2,1)S(1)}, f32[8,8192]{1,0:T(8,128)S(1)}, bf16[2,256,48]{2,1,0:T(8,128)(2,1)S(1)}, f32[3,256,128]{2,1,0:T(8,128)S(1)}) custom-call(f32[2,6,2048]{2,1,0:T(8,128)S(1)} %join.1.joined_ref, f32[2,6,2048]{2,1,0:T(8,128)S(1)} %collective-permute-done.2.other_ref), custom_call_target="tpu_custom_call" | custom-call | flops 1000000000 | tf_op jit(solution)/shard_map/sides/pallas_call | solution.py:496
  17.2 0.0 copy-start
  17.2 0.0 all-to-all-done
  17.2 3.2 %first_image.1 = (f32[1,256]{1,0:T(1,128)S(1)}, f32[32,1,256]{2,1,0:T(1,128)}) custom-call(f32[1,8192]{1,0:T(1,128)S(1)} %bitcast.7, f32[11,2048]{1,0:T(8,128)S(1)} %concatenate.7.bundle_ref.refs_0_, s32[8,128]{1,0:T(8,128)S(1)} %get-tuple-element.19.after_ref.group_ref, bf16[48,8192]{1,0:T(8,128)(2,1)S(1)} %get-tuple-element.20.right_ref, ...), custom_call_target="tpu_custom_call" | custom-call | flops 3000000000 | tf_op jit(solution)/shard_map/first_image/pallas_call | solution.py:506
  20.4 4.6 %all-to-all-start.1 = ((f32[32,1,256]{2,1,0:T(1,128)}), f32[32,1,256]{2,1,0:T(1,128)S(1)}, u32[]{:S(2)}, u32[]{:S(2)}) async-start(f32[32,1,256]{2,1,0:T(1,128)} %get-tuple-element.24), calls=%async_computation.1 | async-start | bytes 65536 | tf_op jit(solution)/shard_map/all_to_all | solution.py:441
  25.1 5.4 %weigh.1 = (bf16[40,256,1024]{2,1,0:T(8,128)(2,1)}, f32[8,128]{1,0:T(8,128)S(1)}) custom-call(s32[8,128]{1,0:T(8,128)S(1)} %get-tuple-element.19.after_ref.group_ref, bf16[3072,48]{1,0:T(8,128)(2,1)S(1)} %get-tuple-element.26.left_ref, bf16[48,8192]{1,0:T(8,128)(2,1)S(1)} %get-tuple-element.20.right_ref), custom_call_target="tpu_custom_call" | custom-call | flops 5000000000 | tf_op jit(solution)/shard_map/weigh/pallas_call | solution.py:516
  30.5 1.8 %all-to-all-done.1 = f32[32,1,256]{2,1,0:T(1,128)S(1)} async-done(((f32[32,1,256]{2,1,0:T(1,128)}), f32[32,1,256]{2,1,0:T(1,128)S(1)}, u32[]{:S(2)}, u32[]{:S(2)}) %all-to-all-start.1) | async-done | bytes 32800 | tf_op jit(solution)/shard_map/all_to_all | solution.py:441
  32.3 3.7 %second_image.1 = (f32[2,8192]{1,0:T(2,128)S(1)}, f32[2,256]{1,0:T(2,128)S(1)}, f32[32,1,128]{2,1,0:T(1,128)}, f32[1,128]{1,0:T(1,128)S(1)}) custom-call(f32[1,8192]{1,0:T(1,128)S(1)} %bitcast.8, f32[1,8192]{1,0:T(1,128)S(1)} %bitcast.9, f32[1,256]{1,0:T(1,128)S(1)} %get-tuple-element.25.image_own_ref, f32[11,2048]{1,0:T(8,128)S(1)} %concatenate.7.bundle_ref.refs_0_, ...), custom_call_target="tpu_custom_call" | custom-call | flops 3000000000 | tf_op jit(solution)/shard_map/second_image/pallas_call | solution.py:527
  36.0 4.0 %all-to-all-start.2 = ((f32[32,1,128]{2,1,0:T(1,128)}), f32[32,1,128]{2,1,0:T(1,128)S(1)}, u32[]{:S(2)}, u32[]{:S(2)}) async-start(f32[32,1,128]{2,1,0:T(1,128)} %get-tuple-element.28), calls=%async_computation.2 | async-start | bytes 32768 | tf_op jit(solution)/shard_map/all_to_all | solution.py:441
  40.0 7.5 %block_field.1.field_ref = f32[12,2048]{1,0:T(8,128)S(1)} custom-call(s32[8,128]{1,0:T(8,128)S(1)} %get-tuple-element.19.after_ref.group_ref, s32[8]{0:T(128)S(1)} %copy-done, s32[1,2048]{1,0:T(1,128)S(1)} %get-tuple-element.31.slot_ref, f32[8,8192]{1,0:T(8,128)S(1)} %get-tuple-element.21.moment_ref, f32[2,8192]{1,0:T(2,128)S(1)} %get-tuple-element.32.basis_ref, ...), custom_call_target="tpu_custom_call" | custom-call | flops 6000000000 | tf_op jit(solution)/shard_map/block_field/pallas_call | solution.py:536
  47.5 0.0 all-to-all-done.2.stats_ref
  47.6 1.0 %combine.1 = (f32[1,256]{1,0:T(1,128)}, f32[3,2048]{1,0:T(4,128)}) custom-call(f32[32,1,128]{2,1,0:T(1,128)S(1)} %all-to-all-done.2.stats_ref, f32[1,128]{1,0:T(1,128)S(1)} %get-tuple-element.29.known_ref, f32[2,256]{1,0:T(2,128)S(1)} %get-tuple-element.30.basis_own_ref, f32[12,2048]{1,0:T(8,128)S(1)} %block_field.1.field_ref, ...), custom_call_target="tpu_custom_call" | custom-call | tf_op jit(solution)/shard_map/combine/pallas_call | solution.py:547
  (15 shorter events, 0.1 us)
Async XLA Ops:
  0.6 10.8 %copy-start.5 = (f32[256]{0:T(256)S(1)}, f32[256]{0:T(256)}, u32[]{:S(2)}) copy-start(f32[256]{0:T(256)} %param.7) | copy-start | bytes 3076
  0.6 8.7 %copy-start.2 = (f32[3,2048]{1,0:T(4,128)S(1)}, f32[3,2048]{1,0:T(4,128)}, u32[]{:S(2)}) copy-start(f32[3,2048]{1,0:T(4,128)} %param.9) | copy-start | bytes 73732
  0.7 10.5 %copy-start.3 = (f32[3,2048]{1,0:T(4,128)S(1)}, f32[3,2048]{1,0:T(4,128)}, u32[]{:S(2)}) copy-start(f32[3,2048]{1,0:T(4,128)} %param.10) | copy-start | bytes 73732
  0.7 10.8 %copy-start.4 = (s32[2048,1]{0,1:T(1,128)S(1)}, s32[2048,1]{0,1:T(1,128)}, u32[]{:S(2)}) copy-start(s32[2048,1]{0,1:T(1,128)} %param.12) | copy-start | bytes 24580
  0.7 10.8 %copy-start.6 = (f32[256]{0:T(256)S(1)}, f32[256]{0:T(256)}, u32[]{:S(2)}) copy-start(f32[256]{0:T(256)} %param.8) | copy-start | bytes 3076
  0.7 10.8 %copy-start.1 = (f32[3,2048]{1,0:T(4,128)S(1)}, f32[3,2048]{1,0:T(4,128)}, u32[]{:S(2)}) copy-start(f32[3,2048]{1,0:T(4,128)} %param.11) | copy-start | bytes 73732
  2.0 15.2 %all-to-all-start = ((f32[32,1,256]{2,1,0:T(1,128)}), f32[32,1,256]{2,1,0:T(1,128)S(1)}, u32[]{:S(2)}, u32[]{:S(2)}) async-start(f32[32,1,256]{2,1,0:T(1,128)} %spread.1), calls=%async_computation | async-start | bytes 65536 | tf_op jit(solution)/shard_map/all_to_all | solution.py:441
  9.3 4.0 %collective-permute-start = (f32[3,2048]{1,0:T(4,128)S(1)}, f32[3,2048]{1,0:T(4,128)S(1)}, u32[]{:S(2)}, u32[]{:S(2)}) collective-permute-start(f32[3,2048]{1,0:T(4,128)S(1)} %copy-done.2), channel_id=1, source_target_pairs={{0,16},{8,24},{16,0},{24,8},{1,17},{9,25},{17,1},{25,9},{2,18},{10... | collective-permute-start | bytes 73736 | tf_op jit(solution)/shard_map/ppermute | solution.py:463
  11.2 3.9 %collective-permute-start.1 = (f32[3,2048]{1,0:T(4,128)S(1)}, f32[3,2048]{1,0:T(4,128)S(1)}, u32[]{:S(2)}, u32[]{:S(2)}) collective-permute-start(f32[3,2048]{1,0:T(4,128)S(1)} %copy-done.3), channel_id=1, source_target_pairs={{0,16},{8,24},{16,0},{24,8},{1,17},{9,25},{17,1},{25,9},{2,18},{10... | collective-permute-start | bytes 73736 | tf_op jit(solution)/shard_map/ppermute | solution.py:463
  15.1 1.4 %collective-permute-start.2 = (f32[2,6,2048]{2,1,0:T(8,128)S(1)}, f32[2,6,2048]{2,1,0:T(8,128)S(1)}, u32[]{:S(2)}, u32[]{:S(2)}) collective-permute-start(f32[2,6,2048]{2,1,0:T(8,128)S(1)} %join.1.joined_ref), channel_id=1, source_target_pairs={{0,8},{8,0},{16,24},{24,16},{1,9},{9,1},{17,25},{25,17},{2,10},{10... | collective-permute-start | bytes 294920 | tf_op jit(solution)/shard_map/ppermute | solution.py:463
  17.2 22.8 %copy-start = (s32[8]{0:T(128)S(1)}, s32[8]{0:T(128)}, u32[]{:S(2)}) copy-start(s32[8]{0:T(128)} %length_ref.1) | copy-start | bytes 100
  20.4 11.8 %all-to-all-start.1 = ((f32[32,1,256]{2,1,0:T(1,128)}), f32[32,1,256]{2,1,0:T(1,128)S(1)}, u32[]{:S(2)}, u32[]{:S(2)}) async-start(f32[32,1,256]{2,1,0:T(1,128)} %get-tuple-element.24), calls=%async_computation.1 | async-start | bytes 65536 | tf_op jit(solution)/shard_map/all_to_all | solution.py:441
  36.0 11.6 %all-to-all-start.2 = ((f32[32,1,128]{2,1,0:T(1,128)}), f32[32,1,128]{2,1,0:T(1,128)S(1)}, u32[]{:S(2)}, u32[]{:S(2)}) async-start(f32[32,1,128]{2,1,0:T(1,128)} %get-tuple-element.28), calls=%async_computation.2 | async-start | bytes 32768 | tf_op jit(solution)/shard_map/all_to_all | solution.py:441

commit v7 on v6

--- a/solution.py
+++ b/solution.py
@@ -79,20 +79,18 @@
     return pl.ds(pl.multiple_of(start, size), size)
 
 
-def sides_kernel(joined_ref, other_ref, right_ref, moment_ref, left_ref, along_ref, *, offsets):
-    n_col = len(offsets)
-    half = n_col // 2
+def sides_kernel(*refs, n_col):
+    pieces, (right_ref, moment_ref, left_ref, along_ref) = refs[:n_col], refs[n_col:]
     length = right_ref.shape[1] // n_col
     seg_dev = left_ref.shape[1]
     own_at = aligned(lax.axis_index("row") * seg_dev, seg_dev)
-    tangent = rows8(joined_ref[0, 3:6, own_at])
-    left_ref[0] = transposed(left_parts(left_center(joined_ref[0, 0:3, own_at] - 0.5, EPS_SEG)))
+    tangent = rows8(pieces[0][3:6, own_at])
+    left_ref[0] = transposed(left_parts(left_center(pieces[0][0:3, own_at] - 0.5, EPS_SEG)))
     left_ref[1] = transposed(left_parts(tangent))
     tangent = tangent.T
     for k in range(3):
         along_ref[k] = jnp.broadcast_to(tangent[:, k:k + 1], (seg_dev, 128))
-    for index, offset in enumerate(offsets):
-        piece = joined_ref.at[index] if index < half else other_ref.at[index - half]
+    for offset, piece in enumerate(pieces):
         col = jnp.bitwise_xor(lax.axis_index("col"), offset)
 
         def step(k, carry):
@@ -164,17 +162,8 @@
     spread_rows(out_ref, drive[...])
 
 
-def join_kernel(*refs):
-    out_ref = refs[-1]
-    if len(refs) == 4:
-        bundle_ref, centers_ref, tangents_ref = refs[0:3]
-        out_ref[0] = bundle_ref[0:6, 0:out_ref.shape[2]]
-        out_ref[1, 0:3] = centers_ref[...]
-        out_ref[1, 3:6] = tangents_ref[...]
-    else:
-        held = refs[0].shape[0]
-        out_ref[0:held] = refs[0][...]
-        out_ref[held:2 * held] = refs[1][...]
+def take_kernel(bundle_ref, out_ref):
+    out_ref[...] = bundle_ref[0:6, 0:out_ref.shape[1]]
 
 
 def own_rows(bundle_ref, like_ref):
@@ -459,20 +448,10 @@
         wide(jnp.concatenate([drive, resist])[None, :]),
     ], axis=0)
 
-    def swap(x, bit):
-        return lax.ppermute(x, "col", [(k, k ^ bit) for k in range(n_col)])
-
-    bit = n_col // 2
-    offsets = [0, bit]
-    joined = call(
-        join_kernel, out_shape=shape(2, 6, col_len), cost_estimate=work(1), name="join"
-    )(bundle, swap(centers, bit), swap(tangents, bit))
-    while bit > 1:
-        bit //= 2
-        other = swap(joined, bit)
-        offsets = offsets + [offset ^ bit for offset in offsets]
-        if bit > 1:
-            joined = call(join_kernel, out_shape=shape(len(offsets), 6, col_len), name="join")(joined, other)
+    own_geometry = call(take_kernel, out_shape=shape(6, col_len), cost_estimate=work(1), name="take")(bundle)
+    pieces = [own_geometry] + [
+        lax.ppermute(own_geometry, "col", [(k, k ^ offset) for k in range(n_col)]) for offset in range(1, n_col)
+    ]
 
     chunk_count = points_count // CHUNK + n_row * (CHUNK - 1) // CHUNK
     chunk_count = -(-chunk_count // 8) * 8
@@ -484,7 +463,7 @@
             shape(chunk_count * CHUNK, 48, dtype=jnp.bfloat16),
         ),
         scratch_shapes=[pltpu.VMEM((48 * chunk_count, CHUNK), jnp.float32)],
-        cost_estimate=work(3),
+        cost_estimate=work(30),
         name="group_points",
     )(bundle)
 
@@ -494,14 +473,14 @@
         pl.pallas_call, compiler_params=pltpu.CompilerParams(vmem_limit_bytes=STREAM_LIMIT if keep else VMEM_LIMIT)
     )
     sides = call(
-        functools.partial(sides_kernel, offsets=offsets),
+        functools.partial(sides_kernel, n_col=n_col),
         out_shape=(
             shape(48, segments, dtype=jnp.bfloat16), shape(8, segments),
             shape(2, seg_dev, 48, dtype=jnp.bfloat16), shape(3, seg_dev, 128),
         ),
         cost_estimate=work(1),
         name="sides",
-    )(joined, other)
+    )(*pieces)
     right, moment = sides[0:2]
     image_own, image_spread = call(
         functools.partial(first_kernel, coupling),

time: 49.3 us -> 51.3 us (1.041)
  starting transfers between devices: 18.1 us -> 15.8 us
  waiting for transfers between devices: 5.31 us -> 7.13 us
  local copies, waits for them, and re-layouts: 0.26 us -> 1.75 us
  other arithmetic: 0.01 us -> 1.41 us
    all_to_all x3, waiting for transfers between devices: 1.82 us -> 7.12 us  [exchange(): return lax.all_to_all(x, AXES, 0, 0, tiled=True)]
    ppermute x3, waiting for transfers between devices: 3.49 us -> 0.01 us  [shards(): lax.ppermute(own_geometry, 'col', [(k, k ^ offset) for k in range(n_col)])]
    all_to_all x3, starting transfers between devices: 16 us -> 12.7 us  [exchange(): return lax.all_to_all(x, AXES, 0, 0, tiled=True)]
    concatenate x1, local copies, waits for them, and re-layouts: 0.22 us -> 1.74 us  [shards(): jnp.concatenate([wide(centers), wide(tangents), wide(iron_points), wide(o...]
    ppermute x3, starting transfers between devices: 2.16 us -> 3.12 us  [shards(): lax.ppermute(own_geometry, 'col', [(k, k ^ offset) for k in range(n_col)])]
    convert_element_type x1, other arithmetic: 0.01 us -> 0.7 us  [shards(): owner.reshape(1, points_count).astype(jnp.float32)]
    concatenate x1, other arithmetic: 0.01 us -> 0.7 us  [shards(): jnp.concatenate([drive, resist])[None, :]]
  transfers between devices with their start and end apart: 6 -> 6, of which waited for: 4 -> 2; matrix products, arithmetic and copies ran while one was open for 0% -> 0% of each run, Pallas kernels for 30% -> 32%
where the time goes in v7:
time: 51.3 us; the launch traced here: 50.8 us
  Pallas kernels  24 us (47%)
  starting transfers between devices  15.8 us (31%)
  waiting for transfers between devices  7.13 us (14%)
  local copies, waits for them, and re-layouts  1.75 us (3%)
  other arithmetic  1.41 us (3%)
  between operations  0.75 us (1%)
    all_to_all x3, starting transfers between devices, exchange(): return lax.all_to_all(x, AXES, 0, 0, tiled=True)  12.7 us
    pallas_call x1, Pallas kernels, shards(): stream(functools.partial(field_kernel, n_row=n_row, n_col=n_col, keep=kee...  7.5 us
    all_to_all x3, waiting for transfers between devices, exchange(): return lax.all_to_all(x, AXES, 0, 0, tiled=True)  7.12 us
    pallas_call x1, Pallas kernels, shards(): stream(functools.partial(weigh_kernel, n_row=n_row, n_col=n_col), out_sha...  5.34 us
    pallas_call x1, Pallas kernels, shards(): call(functools.partial(second_kernel, coupling), out_shape=(shape(2, segm...  3.72 us
    pallas_call x1, Pallas kernels, shards(): call(functools.partial(first_kernel, coupling), out_shape=(shape(1, seg_d...  3.22 us
    ppermute x3, starting transfers between devices, shards(): lax.ppermute(own_geometry, 'col', [(k, k ^ offset) for k in range(n_col)])  3.12 us
    concatenate x1, local copies, waits for them, and re-layouts, shards(): jnp.concatenate([wide(centers), wide(tangents), wide(iron_points), wide(o...  1.74 us
  transfers between devices with their start and end apart: 6, of which 2 were waited for; matrix products, arithmetic and copies ran while one was open for 0% of the time, Pallas kernels for 32%

profile of v7, /device:TPU:0, one launch (start us, length us, event | category | flops | bytes accessed | tf_op | source)
XLA Modules:
  0.0 50.8 jit_solution(7077115714116738185)
XLA Ops:
  0.6 0.7 %convert_bitcast_fusion = f32[1,2048]{1,0:T(1,128)S(1)} fusion(s32[2048,1]{0,1:T(1,128)} %param.12), kind=kLoop, calls=%fused_computation | loop fusion | flops 2048 | bytes 16384 | tf_op jit(solution)/shard_map/convert_element_type | solution.py:447
  1.3 0.7 %pad_maximum_fusion = f32[512]{0:T(512)S(1)} fusion(f32[256]{0:T(256)} %param.8, f32[256]{0:T(256)} %param.7), kind=kLoop, calls=%fused_computation.1 | loop fusion | flops 512 | bytes 4096 | tf_op jit(solution)/shard_map/concatenate | solution.py:448
  2.0 1.7 %concatenate.7.bundle_ref = f32[11,2048]{1,0:T(8,128)S(1)} concatenate(f32[3,2048]{1,0:T(4,128)} %param.9, f32[3,2048]{1,0:T(4,128)} %param.10, f32[3,2048]{1,0:T(4,128)} %param.11, f32[1,2048]{1,0:T(1,128)S(1)} %convert_bitcast_fusion, f32[1,2048]{1,0:T(1,128)S(1)} %pad.4), dimensions={0} | concatenate | bytes 180224 | tf_op jit(solution)/shard_map/concatenate | solution.py:446
  3.8 2.4 %collective-permute-start.2 = (f32[6,2048]{1,0:T(8,128)S(1)}, f32[6,2048]{1,0:T(8,128)S(1)}, u32[]{:S(2)}, u32[]{:S(2)}) collective-permute-start(f32[6,2048]{1,0:T(8,128)S(1)} %take.1.refs_0_), channel_id=1, source_target_pairs={{0,24},{8,16},{16,8},{24,0},{1,25},{9,17},{17,9},{25,1},{2,26},{10... | collective-permute-start | bytes 147464 | tf_op jit(solution)/shard_map/ppermute | solution.py:453
  6.2 0.6 %collective-permute-start.1 = (f32[6,2048]{1,0:T(8,128)S(1)}, f32[6,2048]{1,0:T(8,128)S(1)}, u32[]{:S(2)}, u32[]{:S(2)}) collective-permute-start(f32[6,2048]{1,0:T(8,128)S(1)} %take.1.refs_0_), channel_id=1, source_target_pairs={{0,16},{8,24},{16,0},{24,8},{1,17},{9,25},{17,1},{25,9},{2,18},{10... | collective-permute-start | bytes 147464 | tf_op jit(solution)/shard_map/ppermute | solution.py:453
  6.9 0.0 collective-permute-start
  6.9 1.3 %spread.1 = f32[32,1,256]{2,1,0:T(1,128)} custom-call(f32[1,256]{1,0:T(1,128)} %bitcast.11), custom_call_target="tpu_custom_call" | custom-call | flops 8000000000 | tf_op jit(solution)/shard_map/spread/pallas_call | solution.py:432
  8.2 6.1 %all-to-all-start = ((f32[32,1,256]{2,1,0:T(1,128)}), f32[32,1,256]{2,1,0:T(1,128)S(1)}, u32[]{:S(2)}, u32[]{:S(2)}) async-start(f32[32,1,256]{2,1,0:T(1,128)} %spread.1), calls=%async_computation | async-start | bytes 65536 | tf_op jit(solution)/shard_map/all_to_all | solution.py:430
  14.4 1.2 %group_points.1 = (s32[1,2048]{1,0:T(1,128)S(1)}, s32[8,128]{1,0:T(8,128)S(1)}, bf16[3072,48]{1,0:T(8,128)(2,1)S(1)}) custom-call(f32[11,2048]{1,0:T(8,128)S(1)} %concatenate.7.bundle_ref), custom_call_target="tpu_custom_call" | custom-call | flops 30000001024 | tf_op jit(solution)/shard_map/group_points/pallas_call | solution.py:458
  15.6 0.0 collective-permute-done.2.refs_3_
  15.6 0.0 collective-permute-done.1.refs_2_
  15.6 0.0 collective-permute-done.refs_1_
  15.6 0.6 %sides.1 = (bf16[48,8192]{1,0:T(8,128)(2,1)S(1)}, f32[8,8192]{1,0:T(8,128)S(1)}, bf16[2,256,48]{2,1,0:T(8,128)(2,1)S(1)}, f32[3,256,128]{2,1,0:T(8,128)S(1)}) custom-call(f32[6,2048]{1,0:T(8,128)S(1)} %take.1.refs_0_, f32[6,2048]{1,0:T(8,128)S(1)} %collective-permute-done.refs_1_, f32[6,2048]{1,0:T(8,128)S(1)} %collective-permute-done.1.refs_2_, ...), custom_call_target="tpu_custom_call" | custom-call | flops 1000000000 | tf_op jit(solution)/shard_map/sides/pallas_call | solution.py:475
  16.3 0.0 copy-start
  16.3 5.3 %all-to-all-done = f32[32,1,256]{2,1,0:T(1,128)S(1)} async-done(((f32[32,1,256]{2,1,0:T(1,128)}), f32[32,1,256]{2,1,0:T(1,128)S(1)}, u32[]{:S(2)}, u32[]{:S(2)}) %all-to-all-start) | async-done | bytes 32800 | tf_op jit(solution)/shard_map/all_to_all | solution.py:430
  21.5 3.2 %first_image.1 = (f32[1,256]{1,0:T(1,128)S(1)}, f32[32,1,256]{2,1,0:T(1,128)}) custom-call(f32[1,8192]{1,0:T(1,128)S(1)} %bitcast.7, f32[11,2048]{1,0:T(8,128)S(1)} %concatenate.7.bundle_ref, s32[8,128]{1,0:T(8,128)S(1)} %get-tuple-element.19.after_ref.group_ref, bf16[48,8192]{1,0:T(8,128)(2,1)S(1)} %get-tuple-element.20.right_ref, ...), custom_call_target="tpu_custom_call" | custom-call | flops 3000000000 | tf_op jit(solution)/shard_map/first_image/pallas_call | solution.py:485
  24.8 2.6 %all-to-all-start.1 = ((f32[32,1,256]{2,1,0:T(1,128)}), f32[32,1,256]{2,1,0:T(1,128)S(1)}, u32[]{:S(2)}, u32[]{:S(2)}) async-start(f32[32,1,256]{2,1,0:T(1,128)} %get-tuple-element.24), calls=%async_computation.1 | async-start | bytes 65536 | tf_op jit(solution)/shard_map/all_to_all | solution.py:430
  27.3 5.3 %weigh.1 = (bf16[40,256,1024]{2,1,0:T(8,128)(2,1)}, f32[8,128]{1,0:T(8,128)S(1)}) custom-call(s32[8,128]{1,0:T(8,128)S(1)} %get-tuple-element.19.after_ref.group_ref, bf16[3072,48]{1,0:T(8,128)(2,1)S(1)} %get-tuple-element.26.left_ref, bf16[48,8192]{1,0:T(8,128)(2,1)S(1)} %get-tuple-element.20.right_ref), custom_call_target="tpu_custom_call" | custom-call | flops 5000000000 | tf_op jit(solution)/shard_map/weigh/pallas_call | solution.py:495
  32.7 1.8 %all-to-all-done.1 = f32[32,1,256]{2,1,0:T(1,128)S(1)} async-done(((f32[32,1,256]{2,1,0:T(1,128)}), f32[32,1,256]{2,1,0:T(1,128)S(1)}, u32[]{:S(2)}, u32[]{:S(2)}) %all-to-all-start.1) | async-done | bytes 32800 | tf_op jit(solution)/shard_map/all_to_all | solution.py:430
  34.5 3.7 %second_image.1 = (f32[2,8192]{1,0:T(2,128)S(1)}, f32[2,256]{1,0:T(2,128)S(1)}, f32[32,1,128]{2,1,0:T(1,128)}, f32[1,128]{1,0:T(1,128)S(1)}) custom-call(f32[1,8192]{1,0:T(1,128)S(1)} %bitcast.8, f32[1,8192]{1,0:T(1,128)S(1)} %bitcast.9, f32[1,256]{1,0:T(1,128)S(1)} %get-tuple-element.25.image_own_ref, f32[11,2048]{1,0:T(8,128)S(1)} %concatenate.7.bundle_ref, ...), custom_call_target="tpu_custom_call" | custom-call | flops 3000000000 | tf_op jit(solution)/shard_map/second_image/pallas_call | solution.py:506
  38.2 4.0 %all-to-all-start.2 = ((f32[32,1,128]{2,1,0:T(1,128)}), f32[32,1,128]{2,1,0:T(1,128)S(1)}, u32[]{:S(2)}, u32[]{:S(2)}) async-start(f32[32,1,128]{2,1,0:T(1,128)} %get-tuple-element.28), calls=%async_computation.2 | async-start | bytes 32768 | tf_op jit(solution)/shard_map/all_to_all | solution.py:430
  42.3 7.5 %block_field.1.field_ref = f32[12,2048]{1,0:T(8,128)S(1)} custom-call(s32[8,128]{1,0:T(8,128)S(1)} %get-tuple-element.19.after_ref.group_ref, s32[8]{0:T(128)S(1)} %copy-done, s32[1,2048]{1,0:T(1,128)S(1)} %get-tuple-element.31.slot_ref, f32[8,8192]{1,0:T(8,128)S(1)} %get-tuple-element.21.moment_ref, f32[2,8192]{1,0:T(2,128)S(1)} %get-tuple-element.32.basis_ref, ...), custom_call_target="tpu_custom_call" | custom-call | flops 6000000000 | tf_op jit(solution)/shard_map/block_field/pallas_call | solution.py:515
  49.8 0.0 all-to-all-done.2.stats_ref
  49.8 1.0 %combine.1 = (f32[1,256]{1,0:T(1,128)}, f32[3,2048]{1,0:T(4,128)}) custom-call(f32[32,1,128]{2,1,0:T(1,128)S(1)} %all-to-all-done.2.stats_ref, f32[1,128]{1,0:T(1,128)S(1)} %get-tuple-element.29.known_ref, f32[2,256]{1,0:T(2,128)S(1)} %get-tuple-element.30.basis_own_ref, f32[12,2048]{1,0:T(8,128)S(1)} %block_field.1.field_ref, ...), custom_call_target="tpu_custom_call" | custom-call | tf_op jit(solution)/shard_map/combine/pallas_call | solution.py:526
  (3 shorter events, 0.0 us)
Async XLA Ops:
  3.8 11.8 %collective-permute-start.2 = (f32[6,2048]{1,0:T(8,128)S(1)}, f32[6,2048]{1,0:T(8,128)S(1)}, u32[]{:S(2)}, u32[]{:S(2)}) collective-permute-start(f32[6,2048]{1,0:T(8,128)S(1)} %take.1.refs_0_), channel_id=1, source_target_pairs={{0,24},{8,16},{16,8},{24,0},{1,25},{9,17},{17,9},{25,1},{2,26},{10... | collective-permute-start | bytes 147464 | tf_op jit(solution)/shard_map/ppermute | solution.py:453
  6.2 9.4 %collective-permute-start.1 = (f32[6,2048]{1,0:T(8,128)S(1)}, f32[6,2048]{1,0:T(8,128)S(1)}, u32[]{:S(2)}, u32[]{:S(2)}) collective-permute-start(f32[6,2048]{1,0:T(8,128)S(1)} %take.1.refs_0_), channel_id=1, source_target_pairs={{0,16},{8,24},{16,0},{24,8},{1,17},{9,25},{17,1},{25,9},{2,18},{10... | collective-permute-start | bytes 147464 | tf_op jit(solution)/shard_map/ppermute | solution.py:453
  6.9 8.7 %collective-permute-start = (f32[6,2048]{1,0:T(8,128)S(1)}, f32[6,2048]{1,0:T(8,128)S(1)}, u32[]{:S(2)}, u32[]{:S(2)}) collective-permute-start(f32[6,2048]{1,0:T(8,128)S(1)} %take.1.refs_0_), channel_id=1, source_target_pairs={{0,8},{8,0},{16,24},{24,16},{1,9},{9,1},{17,25},{25,17},{2,10},{10... | collective-permute-start | bytes 147464 | tf_op jit(solution)/shard_map/ppermute | solution.py:453
  8.2 13.3 %all-to-all-start = ((f32[32,1,256]{2,1,0:T(1,128)}), f32[32,1,256]{2,1,0:T(1,128)S(1)}, u32[]{:S(2)}, u32[]{:S(2)}) async-start(f32[32,1,256]{2,1,0:T(1,128)} %spread.1), calls=%async_computation | async-start | bytes 65536 | tf_op jit(solution)/shard_map/all_to_all | solution.py:430
  16.3 26.0 %copy-start = (s32[8]{0:T(128)S(1)}, s32[8]{0:T(128)}, u32[]{:S(2)}) copy-start(s32[8]{0:T(128)} %length_ref.1) | copy-start | bytes 100
  24.8 9.8 %all-to-all-start.1 = ((f32[32,1,256]{2,1,0:T(1,128)}), f32[32,1,256]{2,1,0:T(1,128)S(1)}, u32[]{:S(2)}, u32[]{:S(2)}) async-start(f32[32,1,256]{2,1,0:T(1,128)} %get-tuple-element.24), calls=%async_computation.1 | async-start | bytes 65536 | tf_op jit(solution)/shard_map/all_to_all | solution.py:430
  38.2 11.5 %all-to-all-start.2 = ((f32[32,1,128]{2,1,0:T(1,128)}), f32[32,1,128]{2,1,0:T(1,128)S(1)}, u32[]{:S(2)}, u32[]{:S(2)}) async-start(f32[32,1,128]{2,1,0:T(1,128)} %get-tuple-element.28), calls=%async_computation.2 | async-start | bytes 32768 | tf_op jit(solution)/shard_map/all_to_all | solution.py:430

commit v8 on v6

--- a/solution.py
+++ b/solution.py
@@ -462,16 +462,16 @@
     def swap(x, bit):
         return lax.ppermute(x, "col", [(k, k ^ bit) for k in range(n_col)])
 
-    bit = n_col // 2
+    bit = 1
     offsets = [0, bit]
     joined = call(
         join_kernel, out_shape=shape(2, 6, col_len), cost_estimate=work(1), name="join"
     )(bundle, swap(centers, bit), swap(tangents, bit))
-    while bit > 1:
-        bit //= 2
+    while 2 * bit < n_col:
+        bit *= 2
         other = swap(joined, bit)
         offsets = offsets + [offset ^ bit for offset in offsets]
-        if bit > 1:
+        if 2 * bit < n_col:
             joined = call(join_kernel, out_shape=shape(len(offsets), 6, col_len), name="join")(joined, other)
 
     chunk_count = points_count // CHUNK + n_row * (CHUNK - 1) // CHUNK

time: 49.3 us -> 50.1 us (1.016)
  starting transfers between devices: 18.1 us -> 19.3 us
    all_to_all x3, starting transfers between devices: 16 us -> 17 us  [exchange(): return lax.all_to_all(x, AXES, 0, 0, tiled=True)]
where the time goes in v8:
time: 50.1 us; the launch traced here: 49.9 us
  Pallas kernels  24 us (48%)
  starting transfers between devices  19.3 us (39%)
  waiting for transfers between devices  5.44 us (11%)
  between operations  0.83 us (2%)
    all_to_all x3, starting transfers between devices, exchange(): return lax.all_to_all(x, AXES, 0, 0, tiled=True)  17 us
    pallas_call x1, Pallas kernels, shards(): stream(functools.partial(field_kernel, n_row=n_row, n_col=n_col, keep=kee...  7.51 us
    pallas_call x1, Pallas kernels, shards(): stream(functools.partial(weigh_kernel, n_row=n_row, n_col=n_col), out_sha...  5.36 us
    pallas_call x1, Pallas kernels, shards(): call(functools.partial(second_kernel, coupling), out_shape=(shape(2, segm...  3.72 us
    ppermute x3, waiting for transfers between devices, swap(): return lax.ppermute(x, 'col', [(k, k ^ bit) for k in range(n_col)])  3.62 us
    pallas_call x1, Pallas kernels, shards(): call(functools.partial(first_kernel, coupling), out_shape=(shape(1, seg_d...  3.23 us
    ppermute x3, starting transfers between devices, swap(): return lax.ppermute(x, 'col', [(k, k ^ bit) for k in range(n_col)])  2.32 us
    all_to_all x3, waiting for transfers between devices, exchange(): return lax.all_to_all(x, AXES, 0, 0, tiled=True)  1.82 us
  transfers between devices with their start and end apart: 6, of which 4 were waited for; matrix products, arithmetic and copies ran while one was open for 0% of the time, Pallas kernels for 30%

profile of v8, /device:TPU:0, one launch (start us, length us, event | category | flops | bytes accessed | tf_op | source)
XLA Modules:
  0.0 49.9 jit_solution(13755948392719593291)
XLA Ops:
  0.7 1.3 %spread.1 = f32[32,1,256]{2,1,0:T(1,128)} custom-call(f32[1,256]{1,0:T(1,128)} %bitcast.11), custom_call_target="tpu_custom_call" | custom-call | flops 8000000000 | tf_op jit(solution)/shard_map/spread/pallas_call | solution.py:443
  2.0 7.3 %all-to-all-start = ((f32[32,1,256]{2,1,0:T(1,128)}), f32[32,1,256]{2,1,0:T(1,128)S(1)}, u32[]{:S(2)}, u32[]{:S(2)}) async-start(f32[32,1,256]{2,1,0:T(1,128)} %spread.1), calls=%async_computation | async-start | bytes 65536 | tf_op jit(solution)/shard_map/all_to_all | solution.py:441
  9.3 0.3 collective-permute-start
  9.7 0.0 copy-done.3
  9.7 0.3 collective-permute-start.1
  10.0 0.2 concatenate.7.bundle_ref.refs_0_
  10.2 0.4 collective-permute-done.refs_1_
  10.6 0.3 collective-permute-done.1.refs_2_
  10.9 1.7 %collective-permute-start.2 = (f32[2,6,2048]{2,1,0:T(8,128)S(1)}, f32[2,6,2048]{2,1,0:T(8,128)S(1)}, u32[]{:S(2)}, u32[]{:S(2)}) collective-permute-start(f32[2,6,2048]{2,1,0:T(8,128)S(1)} %join.1.joined_ref), channel_id=1, source_target_pairs={{0,16},{8,24},{16,0},{24,8},{1,17},{9,25},{17,1},{25,9},{2,18},{10... | collective-permute-start | bytes 294920 | tf_op jit(solution)/shard_map/ppermute | solution.py:463
  12.6 1.2 %group_points.1 = (s32[1,2048]{1,0:T(1,128)S(1)}, s32[8,128]{1,0:T(8,128)S(1)}, bf16[3072,48]{1,0:T(8,128)(2,1)S(1)}) custom-call(f32[11,2048]{1,0:T(8,128)S(1)} %concatenate.7.bundle_ref.refs_0_), custom_call_target="tpu_custom_call" | custom-call | flops 3000000000 | tf_op jit(solution)/shard_map/group_points/pallas_call | solution.py:479
  13.9 3.0 %collective-permute-done.2.other_ref = f32[2,6,2048]{2,1,0:T(8,128)S(1)} collective-permute-done((f32[2,6,2048]{2,1,0:T(8,128)S(1)}, f32[2,6,2048]{2,1,0:T(8,128)S(1)}, u32[]{:S(2)}, u32[]{:S(2)}) %collective-permute-start.2) | collective-permute-done | bytes 98336 | tf_op jit(solution)/shard_map/ppermute | solution.py:463
  16.8 0.6 %sides.1 = (bf16[48,8192]{1,0:T(8,128)(2,1)S(1)}, f32[8,8192]{1,0:T(8,128)S(1)}, bf16[2,256,48]{2,1,0:T(8,128)(2,1)S(1)}, f32[3,256,128]{2,1,0:T(8,128)S(1)}) custom-call(f32[2,6,2048]{2,1,0:T(8,128)S(1)} %join.1.joined_ref, f32[2,6,2048]{2,1,0:T(8,128)S(1)} %collective-permute-done.2.other_ref), custom_call_target="tpu_custom_call" | custom-call | flops 1000000000 | tf_op jit(solution)/shard_map/sides/pallas_call | solution.py:496
  17.5 0.0 copy-start
  17.5 0.0 all-to-all-done
  17.5 3.2 %first_image.1 = (f32[1,256]{1,0:T(1,128)S(1)}, f32[32,1,256]{2,1,0:T(1,128)}) custom-call(f32[1,8192]{1,0:T(1,128)S(1)} %bitcast.7, f32[11,2048]{1,0:T(8,128)S(1)} %concatenate.7.bundle_ref.refs_0_, s32[8,128]{1,0:T(8,128)S(1)} %get-tuple-element.19.after_ref.group_ref, bf16[48,8192]{1,0:T(8,128)(2,1)S(1)} %get-tuple-element.20.right_ref, ...), custom_call_target="tpu_custom_call" | custom-call | flops 3000000000 | tf_op jit(solution)/shard_map/first_image/pallas_call | solution.py:506
  20.7 5.6 %all-to-all-start.1 = ((f32[32,1,256]{2,1,0:T(1,128)}), f32[32,1,256]{2,1,0:T(1,128)S(1)}, u32[]{:S(2)}, u32[]{:S(2)}) async-start(f32[32,1,256]{2,1,0:T(1,128)} %get-tuple-element.24), calls=%async_computation.1 | async-start | bytes 65536 | tf_op jit(solution)/shard_map/all_to_all | solution.py:441
  26.3 5.4 %weigh.1 = (bf16[40,256,1024]{2,1,0:T(8,128)(2,1)}, f32[8,128]{1,0:T(8,128)S(1)}) custom-call(s32[8,128]{1,0:T(8,128)S(1)} %get-tuple-element.19.after_ref.group_ref, bf16[3072,48]{1,0:T(8,128)(2,1)S(1)} %get-tuple-element.26.left_ref, bf16[48,8192]{1,0:T(8,128)(2,1)S(1)} %get-tuple-element.20.right_ref), custom_call_target="tpu_custom_call" | custom-call | flops 5000000000 | tf_op jit(solution)/shard_map/weigh/pallas_call | solution.py:516
  31.7 1.8 %all-to-all-done.1 = f32[32,1,256]{2,1,0:T(1,128)S(1)} async-done(((f32[32,1,256]{2,1,0:T(1,128)}), f32[32,1,256]{2,1,0:T(1,128)S(1)}, u32[]{:S(2)}, u32[]{:S(2)}) %all-to-all-start.1) | async-done | bytes 32800 | tf_op jit(solution)/shard_map/all_to_all | solution.py:441
  33.5 3.7 %second_image.1 = (f32[2,8192]{1,0:T(2,128)S(1)}, f32[2,256]{1,0:T(2,128)S(1)}, f32[32,1,128]{2,1,0:T(1,128)}, f32[1,128]{1,0:T(1,128)S(1)}) custom-call(f32[1,8192]{1,0:T(1,128)S(1)} %bitcast.8, f32[1,8192]{1,0:T(1,128)S(1)} %bitcast.9, f32[1,256]{1,0:T(1,128)S(1)} %get-tuple-element.25.image_own_ref, f32[11,2048]{1,0:T(8,128)S(1)} %concatenate.7.bundle_ref.refs_0_, ...), custom_call_target="tpu_custom_call" | custom-call | flops 3000000000 | tf_op jit(solution)/shard_map/second_image/pallas_call | solution.py:527
  37.2 4.0 %all-to-all-start.2 = ((f32[32,1,128]{2,1,0:T(1,128)}), f32[32,1,128]{2,1,0:T(1,128)S(1)}, u32[]{:S(2)}, u32[]{:S(2)}) async-start(f32[32,1,128]{2,1,0:T(1,128)} %get-tuple-element.28), calls=%async_computation.2 | async-start | bytes 32768 | tf_op jit(solution)/shard_map/all_to_all | solution.py:441
  41.3 0.0 copy-done
  41.3 7.5 %block_field.1.field_ref = f32[12,2048]{1,0:T(8,128)S(1)} custom-call(s32[8,128]{1,0:T(8,128)S(1)} %get-tuple-element.19.after_ref.group_ref, s32[8]{0:T(128)S(1)} %copy-done, s32[1,2048]{1,0:T(1,128)S(1)} %get-tuple-element.31.slot_ref, f32[8,8192]{1,0:T(8,128)S(1)} %get-tuple-element.21.moment_ref, f32[2,8192]{1,0:T(2,128)S(1)} %get-tuple-element.32.basis_ref, ...), custom_call_target="tpu_custom_call" | custom-call | flops 6000000000 | tf_op jit(solution)/shard_map/block_field/pallas_call | solution.py:536
  48.8 0.0 all-to-all-done.2.stats_ref
  48.8 1.0 %combine.1 = (f32[1,256]{1,0:T(1,128)}, f32[3,2048]{1,0:T(4,128)}) custom-call(f32[32,1,128]{2,1,0:T(1,128)S(1)} %all-to-all-done.2.stats_ref, f32[1,128]{1,0:T(1,128)S(1)} %get-tuple-element.29.known_ref, f32[2,256]{1,0:T(2,128)S(1)} %get-tuple-element.30.basis_own_ref, f32[12,2048]{1,0:T(8,128)S(1)} %block_field.1.field_ref, ...), custom_call_target="tpu_custom_call" | custom-call | tf_op jit(solution)/shard_map/combine/pallas_call | solution.py:547
  (15 shorter events, 0.1 us)
Async XLA Ops:
  0.6 9.3 %copy-start.5 = (f32[256]{0:T(256)S(1)}, f32[256]{0:T(256)}, u32[]{:S(2)}) copy-start(f32[256]{0:T(256)} %param.7) | copy-start | bytes 3076
  0.6 8.7 %copy-start.2 = (f32[3,2048]{1,0:T(4,128)S(1)}, f32[3,2048]{1,0:T(4,128)}, u32[]{:S(2)}) copy-start(f32[3,2048]{1,0:T(4,128)} %param.9) | copy-start | bytes 73732
  0.7 9.0 %copy-start.3 = (f32[3,2048]{1,0:T(4,128)S(1)}, f32[3,2048]{1,0:T(4,128)}, u32[]{:S(2)}) copy-start(f32[3,2048]{1,0:T(4,128)} %param.10) | copy-start | bytes 73732
  0.7 9.3 %copy-start.4 = (s32[2048,1]{0,1:T(1,128)S(1)}, s32[2048,1]{0,1:T(1,128)}, u32[]{:S(2)}) copy-start(s32[2048,1]{0,1:T(1,128)} %param.12) | copy-start | bytes 24580
  0.7 9.3 %copy-start.6 = (f32[256]{0:T(256)S(1)}, f32[256]{0:T(256)}, u32[]{:S(2)}) copy-start(f32[256]{0:T(256)} %param.8) | copy-start | bytes 3076
  0.7 9.3 %copy-start.1 = (f32[3,2048]{1,0:T(4,128)S(1)}, f32[3,2048]{1,0:T(4,128)}, u32[]{:S(2)}) copy-start(f32[3,2048]{1,0:T(4,128)} %param.11) | copy-start | bytes 73732
  2.0 15.4 %all-to-all-start = ((f32[32,1,256]{2,1,0:T(1,128)}), f32[32,1,256]{2,1,0:T(1,128)S(1)}, u32[]{:S(2)}, u32[]{:S(2)}) async-start(f32[32,1,256]{2,1,0:T(1,128)} %spread.1), calls=%async_computation | async-start | bytes 65536 | tf_op jit(solution)/shard_map/all_to_all | solution.py:441
  9.3 1.3 %collective-permute-start = (f32[3,2048]{1,0:T(4,128)S(1)}, f32[3,2048]{1,0:T(4,128)S(1)}, u32[]{:S(2)}, u32[]{:S(2)}) collective-permute-start(f32[3,2048]{1,0:T(4,128)S(1)} %copy-done.2), channel_id=1, source_target_pairs={{0,8},{8,0},{16,24},{24,16},{1,9},{9,1},{17,25},{25,17},{2,10},{10... | collective-permute-start | bytes 73736 | tf_op jit(solution)/shard_map/ppermute | solution.py:463
  9.7 1.2 %collective-permute-start.1 = (f32[3,2048]{1,0:T(4,128)S(1)}, f32[3,2048]{1,0:T(4,128)S(1)}, u32[]{:S(2)}, u32[]{:S(2)}) collective-permute-start(f32[3,2048]{1,0:T(4,128)S(1)} %copy-done.3), channel_id=1, source_target_pairs={{0,8},{8,0},{16,24},{24,16},{1,9},{9,1},{17,25},{25,17},{2,10},{10... | collective-permute-start | bytes 73736 | tf_op jit(solution)/shard_map/ppermute | solution.py:463
  10.9 5.9 %collective-permute-start.2 = (f32[2,6,2048]{2,1,0:T(8,128)S(1)}, f32[2,6,2048]{2,1,0:T(8,128)S(1)}, u32[]{:S(2)}, u32[]{:S(2)}) collective-permute-start(f32[2,6,2048]{2,1,0:T(8,128)S(1)} %join.1.joined_ref), channel_id=1, source_target_pairs={{0,16},{8,24},{16,0},{24,8},{1,17},{9,25},{17,1},{25,9},{2,18},{10... | collective-permute-start | bytes 294920 | tf_op jit(solution)/shard_map/ppermute | solution.py:463
  17.5 23.8 %copy-start = (s32[8]{0:T(128)S(1)}, s32[8]{0:T(128)}, u32[]{:S(2)}) copy-start(s32[8]{0:T(128)} %length_ref.1) | copy-start | bytes 100
  20.7 12.8 %all-to-all-start.1 = ((f32[32,1,256]{2,1,0:T(1,128)}), f32[32,1,256]{2,1,0:T(1,128)S(1)}, u32[]{:S(2)}, u32[]{:S(2)}) async-start(f32[32,1,256]{2,1,0:T(1,128)} %get-tuple-element.24), calls=%async_computation.1 | async-start | bytes 65536 | tf_op jit(solution)/shard_map/all_to_all | solution.py:441
  37.2 11.6 %all-to-all-start.2 = ((f32[32,1,128]{2,1,0:T(1,128)}), f32[32,1,128]{2,1,0:T(1,128)S(1)}, u32[]{:S(2)}, u32[]{:S(2)}) async-start(f32[32,1,128]{2,1,0:T(1,128)} %get-tuple-element.28), calls=%async_computation.2 | async-start | bytes 32768 | tf_op jit(solution)/shard_map/all_to_all | solution.py:441

commit v9 on v3

--- a/solution.py
+++ b/solution.py
@@ -143,11 +143,28 @@
     return jnp.sum(acc_ref[...].T, axis=0, keepdims=True)
 
 
-def kept_copy(kept, index, out):
+def part_bounds(n_col, seg_dev):
+    width = n_col * seg_dev
+    return ((0, width // 2), (width // 2, 3 * width // 4), (3 * width // 4, width))
+
+
+def part_copy(kept, chunk, part, bounds, out):
     local, remote, sems = kept
-    if out:
-        return pltpu.make_async_copy(local.at[index], remote.at[index], sems.at[index])
-    return pltpu.make_async_copy(remote.at[index], local.at[index], sems.at[index])
+    start, stop = bounds[part]
+    here = local.at[chunk, :, start:stop]
+    there = remote.at[chunk, :, start:stop]
+    sem = sems.at[chunk * len(bounds) + part]
+    return pltpu.make_async_copy(here, there, sem) if out else pltpu.make_async_copy(there, here, sem)
+
+
+def for_parts(group_ref, length_ref, chunk, bounds, action, otherwise=None):
+    used = chunk < group_ref[1, 0]
+    length = length_ref[group_ref[0, chunk]]
+    for part, (start, _) in enumerate(bounds):
+        active = jnp.logical_and(used, start < length)
+        pl.when(active)(functools.partial(action, part))
+        if otherwise is not None:
+            pl.when(jnp.logical_not(active))(functools.partial(otherwise, part))
 
 
 def spread_rows(ref, row):
@@ -155,13 +172,14 @@
         ref[k] = row
 
 
-def pack_kernel(centers_hbm, tangents_hbm, geo_ref, centers, tangents, sems):
-    pairs = ((centers_hbm, centers), (tangents_hbm, tangents))
+def entry_kernel(drive_hbm, centers_hbm, tangents_hbm, spread_ref, geo_ref, drive, centers, tangents, sems):
+    pairs = ((drive_hbm, drive), (centers_hbm, centers), (tangents_hbm, tangents))
     copies = [pltpu.make_async_copy(source, target, sems.at[k]) for k, (source, target) in enumerate(pairs)]
     for copy in copies:
         copy.start()
     for copy in copies:
         copy.wait()
+    spread_rows(spread_ref, drive[...])
     geo_ref[0:3] = centers[...]
     geo_ref[3:6] = tangents[...]
 
@@ -281,10 +299,11 @@
     return (group_ref[1, 0] + GROUP - 1) // GROUP
 
 
-def weigh_kernel(group_ref, left_ref, right_ref, cubes_hbm, done_ref, cubes_ref, sems, *, n_row, n_col):
+def weigh_kernel(group_ref, length_ref, left_ref, right_ref, cubes_hbm, done_ref, cubes_ref, sems, *, n_row, n_col):
     seg_dev = right_ref.shape[1] // (n_row * n_col)
     done_ref[...] = jnp.zeros_like(done_ref)
     kept = (cubes_ref, cubes_hbm, sems)
+    bounds = part_bounds(n_col, seg_dev)
 
     def step(k, carry):
         for part in range(GROUP):
@@ -295,16 +314,19 @@
                 high, low = cube_halves(left, right_ref[:, block_part(group_ref[0, chunk], col, n_row, seg_dev)])
                 cubes_ref[chunk, 0:CHUNK, to] = high
                 cubes_ref[chunk, CHUNK:2 * CHUNK, to] = low
-            kept_copy(kept, chunk, out=True).start()
+        for part in range(GROUP):
+            chunk = k * GROUP + part
+            for_parts(group_ref, length_ref, chunk, bounds,
+                      lambda piece, chunk=chunk: part_copy(kept, chunk, piece, bounds, out=True).start())
         return carry
 
-    def finish(k, carry):
-        for part in range(GROUP):
-            kept_copy(kept, k * GROUP + part, out=True).wait()
+    def finish(chunk, carry):
+        for_parts(group_ref, length_ref, chunk, bounds,
+                  lambda piece: part_copy(kept, chunk, piece, bounds, out=True).wait())
         return carry
 
     lax.fori_loop(0, chunk_steps(group_ref), step, 0)
-    lax.fori_loop(0, chunk_steps(group_ref), finish, 0)
+    lax.fori_loop(0, group_ref[1, 0], finish, 0)
 
 
 def field_kernel(group_ref, length_ref, slot_ref, moment_ref, basis_ref, *refs, n_row, n_col, keep):
@@ -312,12 +334,23 @@
         cubes_hbm, out_ref, table_ref, sums_ref, cubes_ref, sems = refs
         kept = (cubes_ref, cubes_hbm, sems)
 
-        def begin(k, carry):
-            for part in range(GROUP):
-                kept_copy(kept, k * GROUP + part, out=False).start()
+        bounds = part_bounds(n_col, moment_ref.shape[1] // (n_row * n_col))
+
+        def clear(chunk, piece):
+            start, stop = bounds[piece]
+            cubes_ref[chunk, :, start:stop] = jnp.zeros((2 * CHUNK, stop - start), jnp.bfloat16)
+
+        def begin(chunk, carry):
+            for_parts(group_ref, length_ref, chunk, bounds,
+                      lambda piece: part_copy(kept, chunk, piece, bounds, out=False).start(),
+                      lambda piece: clear(chunk, piece))
             return carry
 
-        lax.fori_loop(0, chunk_steps(group_ref), begin, 0)
+        def arrive(chunk):
+            for_parts(group_ref, length_ref, chunk, bounds,
+                      lambda piece: part_copy(kept, chunk, piece, bounds, out=False).wait())
+
+        lax.fori_loop(0, chunk_steps(group_ref) * GROUP, begin, 0)
     else:
         left_ref, right_ref, out_ref, table_ref, sums_ref = refs
     chunk_count = sums_ref.shape[0] // 16
@@ -349,12 +382,13 @@
         return jnp.concatenate(cube_halves(left_ref[aligned(chunk * CHUNK, CHUNK), :], block_row(right_ref, chunk)), axis=0)
 
     def step(k, carry):
+        if keep:
+            for part in range(GROUP):
+                arrive(k * GROUP + part)
         for part in range(0, GROUP, 2):
             chunk = k * GROUP + part
             tables = jnp.concatenate([block_row(table_ref, chunk), block_row(table_ref, chunk + 1)], axis=0)
             if keep:
-                kept_copy(kept, chunk, out=False).wait()
-                kept_copy(kept, chunk + 1, out=False).wait()
                 cubes = cubes_ref[pl.ds(chunk, 2)].reshape(4 * CHUNK, n_col * seg_dev)
             else:
                 cubes = jnp.concatenate([cubes_of(chunk), cubes_of(chunk + 1)], axis=0)
@@ -429,20 +463,21 @@
     def exchange(x):
         return lax.all_to_all(x, AXES, 0, 0, tiled=True)
 
-    drive_all = exchange(jnp.broadcast_to(drive[None, None, :], (n_dev, 1, seg_dev))).reshape(1, segments)
-    geometry = pl.pallas_call(
-        pack_kernel,
-        out_shape=shape(6, col_len),
-        in_specs=[hbm] * 2,
+    spread, geometry = pl.pallas_call(
+        entry_kernel,
+        out_shape=(shape(n_dev, 1, seg_dev), shape(6, col_len)),
+        in_specs=[hbm] * 3,
         scratch_shapes=[
+            pltpu.VMEM((1, seg_dev), jnp.float32),
             pltpu.VMEM((3, col_len), jnp.float32),
             pltpu.VMEM((3, col_len), jnp.float32),
-            pltpu.SemaphoreType.DMA((2,)),
+            pltpu.SemaphoreType.DMA((3,)),
         ],
         compiler_params=pltpu.CompilerParams(vmem_limit_bytes=ENTRY_LIMIT),
         cost_estimate=work(8),
-        name="pack",
-    )(centers, tangents)
+        name="entry",
+    )(drive[None, :], centers, tangents)
+    drive_all = exchange(spread).reshape(1, segments)
     longest = max(col_len, points_count, 2 * seg_dev)
 
     def wide(row):
@@ -493,17 +528,17 @@
         name="first_image",
     )(drive_all, bundle, group_table, *sides)
     image_all = exchange(image_spread).reshape(1, segments)
-    cube_scratch = [pltpu.VMEM(cube_shape, jnp.bfloat16), pltpu.SemaphoreType.DMA((chunk_count,))]
+    cube_scratch = [pltpu.VMEM(cube_shape, jnp.bfloat16), pltpu.SemaphoreType.DMA((3 * chunk_count,))]
     if keep:
         cubes, after = stream(
             functools.partial(weigh_kernel, n_row=n_row, n_col=n_col),
             out_shape=(shape(roomy(4 * CHUNK * width), *cube_shape[1:], dtype=jnp.bfloat16), shape(8, 128)),
-            in_specs=[smem, vmem, vmem],
+            in_specs=[smem, smem, vmem, vmem],
             out_specs=(hbm, vmem),
             scratch_shapes=cube_scratch,
             cost_estimate=work(5),
             name="weigh",
-        )(group_table, left, right)
+        )(group_table, range_len, left, right)
     else:
         after = group_table
     basis, basis_own, stats, known = call(

time: 48.7 us -> 49 us (level)
  waiting for transfers between devices: 6.79 us -> 6.08 us
  Pallas kernels: 24.1 us -> 24.8 us
  local copies, waits for them, and re-layouts: 0.89 us -> 0.25 us
  starting transfers between devices: 15.8 us -> 16.4 us
    all_to_all x3, waiting for transfers between devices: 6.79 us -> 6.07 us  [exchange(): return lax.all_to_all(x, AXES, 0, 0, tiled=True)]
    pallas_call x1, Pallas kernels: 5.36 us -> 6.06 us  [shards(): stream(functools.partial(weigh_kernel, n_row=n_row, n_col=n_col), out_sha...]
    all_to_all x3, starting transfers between devices: 12.5 us -> 13.2 us  [exchange(): return lax.all_to_all(x, AXES, 0, 0, tiled=True)]
    broadcast_in_dim x1 -> x0, local copies, waits for them, and re-layouts: 0.63 us -> none  [shards(): jnp.broadcast_to(drive[None, None, :], (n_dev, 1, seg_dev))]
  transfers between devices with their start and end apart: 6 -> 6, of which waited for: 2 -> 2; matrix products, arithmetic and copies ran while one was open for 2% -> 0% of each run, Pallas kernels for 30% -> 32%
where the time goes in v9:
time: 49 us; the launch traced here: 48.4 us
  Pallas kernels  24.8 us (51%)
  starting transfers between devices  16.4 us (33%)
  waiting for transfers between devices  6.08 us (12%)
  between operations  0.86 us (2%)
    all_to_all x3, starting transfers between devices, exchange(): return lax.all_to_all(x, AXES, 0, 0, tiled=True)  13.2 us
    pallas_call x1, Pallas kernels, shards(): stream(functools.partial(field_kernel, n_row=n_row, n_col=n_col, keep=kee...  7.45 us
    all_to_all x3, waiting for transfers between devices, exchange(): return lax.all_to_all(x, AXES, 0, 0, tiled=True)  6.07 us
    pallas_call x1, Pallas kernels, shards(): stream(functools.partial(weigh_kernel, n_row=n_row, n_col=n_col), out_sha...  6.06 us
    pallas_call x1, Pallas kernels, shards(): call(functools.partial(second_kernel, coupling), out_shape=(shape(2, segm...  3.71 us
    ppermute x3, starting transfers between devices, shards(): lax.ppermute(geometry, 'col', [(k, (k + shift) % n_col) for k in range(n_...  3.23 us
    pallas_call x1, Pallas kernels, shards(): call(functools.partial(first_kernel, coupling), out_shape=(shape(1, seg_d...  3.21 us
    pallas_call x1, Pallas kernels, shards(): pl.pallas_call(entry_kernel, out_shape=(shape(n_dev, 1, seg_dev), shape(6...  1.48 us
  transfers between devices with their start and end apart: 6, of which 2 were waited for; matrix products, arithmetic and copies ran while one was open for 0% of the time, Pallas kernels for 32%

profile of v9, /device:TPU:0, one launch (start us, length us, event | category | flops | bytes accessed | tf_op | source)
XLA Modules:
  0.0 48.4 jit_solution(3524843121404036518)
XLA Ops:
  0.7 1.5 %entry.1 = (f32[32,1,256]{2,1,0:T(1,128)}, f32[6,2048]{1,0:T(8,128)}) custom-call(f32[1,256]{1,0:T(1,128)} %bitcast.11, f32[3,2048]{1,0:T(4,128)} %centers_hbm.1, f32[3,2048]{1,0:T(4,128)} %tangents_hbm.1), custom_call_target="tpu_custom_call" | custom-call | flops 8000000000 | tf_op jit(solution)/shard_map/entry/pallas_call | solution.py:466
  2.2 2.4 %collective-permute-start.2 = (f32[6,2048]{1,0:T(8,128)}, f32[6,2048]{1,0:T(8,128)S(1)}, u32[]{:S(2)}, u32[]{:S(2)}) collective-permute-start(f32[6,2048]{1,0:T(8,128)} %get-tuple-element.23), channel_id=1, source_target_pairs={{0,24},{8,0},{16,8},{24,16},{1,25},{9,1},{17,9},{25,17},{2,26},{10... | collective-permute-start | bytes 147464 | tf_op jit(solution)/shard_map/ppermute | solution.py:491
  4.6 0.6 %collective-permute-start.1 = (f32[6,2048]{1,0:T(8,128)}, f32[6,2048]{1,0:T(8,128)S(1)}, u32[]{:S(2)}, u32[]{:S(2)}) collective-permute-start(f32[6,2048]{1,0:T(8,128)} %get-tuple-element.23), channel_id=1, source_target_pairs={{0,16},{8,24},{16,0},{24,8},{1,17},{9,25},{17,1},{25,9},{2,18},{10... | collective-permute-start | bytes 147464 | tf_op jit(solution)/shard_map/ppermute | solution.py:491
  5.3 0.2 collective-permute-start
  5.4 5.9 %all-to-all-start = ((f32[32,1,256]{2,1,0:T(1,128)}), f32[32,1,256]{2,1,0:T(1,128)S(1)}, u32[]{:S(2)}, u32[]{:S(2)}) async-start(f32[32,1,256]{2,1,0:T(1,128)} %get-tuple-element.21), calls=%async_computation | async-start | bytes 65536 | tf_op jit(solution)/shard_map/all_to_all | solution.py:464
  11.5 0.0 copy-done.2
  11.5 0.0 copy-done.1
  11.5 0.0 copy-done.3
  11.5 0.2 concatenate.7.bundle_ref.refs_0_
  11.7 1.2 %group_points.1 = (s32[1,2048]{1,0:T(1,128)S(1)}, s32[8,128]{1,0:T(8,128)S(1)}, bf16[3072,48]{1,0:T(8,128)(2,1)S(1)}) custom-call(f32[11,2048]{1,0:T(8,128)S(1)} %concatenate.7.bundle_ref.refs_0_), custom_call_target="tpu_custom_call" | custom-call | flops 3000000000 | tf_op jit(solution)/shard_map/group_points/pallas_call | solution.py:496
  12.9 0.0 collective-permute-done.2.refs_3_
  12.9 0.0 collective-permute-done.1.refs_2_
  13.0 0.0 collective-permute-done.refs_1_
  13.0 0.6 %sides.1 = (bf16[48,8192]{1,0:T(8,128)(2,1)S(1)}, f32[8,8192]{1,0:T(8,128)S(1)}, bf16[2,256,48]{2,1,0:T(8,128)(2,1)S(1)}, f32[3,256,128]{2,1,0:T(8,128)S(1)}) custom-call(f32[11,2048]{1,0:T(8,128)S(1)} %concatenate.7.bundle_ref.refs_0_, f32[6,2048]{1,0:T(8,128)S(1)} %collective-permute-done.refs_1_, f32[6,2048]{1,0:T(8,128)S(1)} %collective-permute-done.1.refs_2_, ...), custom_call_target="tpu_custom_call" | custom-call | flops 1000000000 | tf_op jit(solution)/shard_map/sides/pallas_call | solution.py:513
  13.6 5.0 %all-to-all-done = f32[32,1,256]{2,1,0:T(1,128)S(1)} async-done(((f32[32,1,256]{2,1,0:T(1,128)}), f32[32,1,256]{2,1,0:T(1,128)S(1)}, u32[]{:S(2)}, u32[]{:S(2)}) %all-to-all-start) | async-done | bytes 32800 | tf_op jit(solution)/shard_map/all_to_all | solution.py:464
  18.6 3.2 %first_image.1 = (f32[1,256]{1,0:T(1,128)S(1)}, f32[32,1,256]{2,1,0:T(1,128)}) custom-call(f32[1,8192]{1,0:T(1,128)S(1)} %bitcast.7, f32[11,2048]{1,0:T(8,128)S(1)} %concatenate.7.bundle_ref.refs_0_, s32[8,128]{1,0:T(8,128)S(1)} %get-tuple-element.22.after_ref.group_ref, bf16[48,8192]{1,0:T(8,128)(2,1)S(1)} %get-tuple-element.24.right_ref, ...), custom_call_target="tpu_custom_call" | custom-call | flops 3000000000 | tf_op jit(solution)/shard_map/first_image/pallas_call | solution.py:523
  21.8 2.6 %all-to-all-start.1 = ((f32[32,1,256]{2,1,0:T(1,128)}), f32[32,1,256]{2,1,0:T(1,128)S(1)}, u32[]{:S(2)}, u32[]{:S(2)}) async-start(f32[32,1,256]{2,1,0:T(1,128)} %get-tuple-element.28), calls=%async_computation.1 | async-start | bytes 65536 | tf_op jit(solution)/shard_map/all_to_all | solution.py:464
  24.4 6.1 %weigh.1 = (bf16[40,256,1024]{2,1,0:T(8,128)(2,1)}, f32[8,128]{1,0:T(8,128)S(1)}) custom-call(s32[8,128]{1,0:T(8,128)S(1)} %get-tuple-element.22.after_ref.group_ref, s32[8]{0:T(128)S(1)} %copy-done, bf16[3072,48]{1,0:T(8,128)(2,1)S(1)} %get-tuple-element.30.left_ref, bf16[48,8192]{1,0:T(8,128)(2,1)S(1)} %get-tuple-element.24.right_ref), custom_call_target="tpu_custom_call" | custom-call | flops 5000000000 | tf_op jit(solution)/shard_map/weigh/pallas_call | solution.py:533
  30.4 1.1 %all-to-all-done.1 = f32[32,1,256]{2,1,0:T(1,128)S(1)} async-done(((f32[32,1,256]{2,1,0:T(1,128)}), f32[32,1,256]{2,1,0:T(1,128)S(1)}, u32[]{:S(2)}, u32[]{:S(2)}) %all-to-all-start.1) | async-done | bytes 32800 | tf_op jit(solution)/shard_map/all_to_all | solution.py:464
  31.5 3.7 %second_image.1 = (f32[2,8192]{1,0:T(2,128)S(1)}, f32[2,256]{1,0:T(2,128)S(1)}, f32[32,1,128]{2,1,0:T(1,128)}, f32[1,128]{1,0:T(1,128)S(1)}) custom-call(f32[1,8192]{1,0:T(1,128)S(1)} %bitcast.8, f32[1,8192]{1,0:T(1,128)S(1)} %bitcast.9, f32[1,256]{1,0:T(1,128)S(1)} %get-tuple-element.29.image_own_ref, f32[11,2048]{1,0:T(8,128)S(1)} %concatenate.7.bundle_ref.refs_0_, ...), custom_call_target="tpu_custom_call" | custom-call | flops 3000000000 | tf_op jit(solution)/shard_map/second_image/pallas_call | solution.py:544
  35.2 4.7 %all-to-all-start.2 = ((f32[32,1,128]{2,1,0:T(1,128)}), f32[32,1,128]{2,1,0:T(1,128)S(1)}, u32[]{:S(2)}, u32[]{:S(2)}) async-start(f32[32,1,128]{2,1,0:T(1,128)} %get-tuple-element.32), calls=%async_computation.2 | async-start | bytes 32768 | tf_op jit(solution)/shard_map/all_to_all | solution.py:464
  39.9 7.4 %block_field.1.field_ref = f32[12,2048]{1,0:T(8,128)S(1)} custom-call(s32[8,128]{1,0:T(8,128)S(1)} %get-tuple-element.22.after_ref.group_ref, s32[8]{0:T(128)S(1)} %copy-done, s32[1,2048]{1,0:T(1,128)S(1)} %get-tuple-element.35.slot_ref, f32[8,8192]{1,0:T(8,128)S(1)} %get-tuple-element.25.moment_ref, f32[2,8192]{1,0:T(2,128)S(1)} %get-tuple-element.36.basis_ref, ...), custom_call_target="tpu_custom_call" | custom-call | flops 6000000000 | tf_op jit(solution)/shard_map/block_field/pallas_call | solution.py:553
  47.4 0.0 all-to-all-done.2.stats_ref
  47.4 1.0 %combine.1 = (f32[1,256]{1,0:T(1,128)}, f32[3,2048]{1,0:T(4,128)}) custom-call(f32[32,1,128]{2,1,0:T(1,128)S(1)} %all-to-all-done.2.stats_ref, f32[1,128]{1,0:T(1,128)S(1)} %get-tuple-element.33.known_ref, f32[2,256]{1,0:T(2,128)S(1)} %get-tuple-element.34.basis_own_ref, f32[12,2048]{1,0:T(8,128)S(1)} %block_field.1.field_ref, ...), custom_call_target="tpu_custom_call" | custom-call | tf_op jit(solution)/shard_map/combine/pallas_call | solution.py:564
  (14 shorter events, 0.0 us)
Async XLA Ops:
  0.6 10.8 %copy-start.2 = (f32[3,2048]{1,0:T(4,128)S(1)}, f32[3,2048]{1,0:T(4,128)}, u32[]{:S(2)}) copy-start(f32[3,2048]{1,0:T(4,128)} %tangents_hbm.1) | copy-start | bytes 73732
  0.6 10.8 %copy-start.1 = (f32[3,2048]{1,0:T(4,128)S(1)}, f32[3,2048]{1,0:T(4,128)}, u32[]{:S(2)}) copy-start(f32[3,2048]{1,0:T(4,128)} %centers_hbm.1) | copy-start | bytes 73732
  0.7 10.7 %copy-start.5 = (f32[256]{0:T(256)S(1)}, f32[256]{0:T(256)}, u32[]{:S(2)}) copy-start(f32[256]{0:T(256)} %param.7) | copy-start | bytes 3076
  0.7 10.7 %copy-start.6 = (f32[256]{0:T(256)S(1)}, f32[256]{0:T(256)}, u32[]{:S(2)}) copy-start(f32[256]{0:T(256)} %param.8) | copy-start | bytes 3076
  0.7 10.7 %copy-start.4 = (s32[2048,1]{0,1:T(1,128)S(1)}, s32[2048,1]{0,1:T(1,128)}, u32[]{:S(2)}) copy-start(s32[2048,1]{0,1:T(1,128)} %param.12) | copy-start | bytes 24580
  0.7 10.8 %copy-start.3 = (f32[3,2048]{1,0:T(4,128)S(1)}, f32[3,2048]{1,0:T(4,128)}, u32[]{:S(2)}) copy-start(f32[3,2048]{1,0:T(4,128)} %param.11) | copy-start | bytes 73732
  0.7 23.7 %copy-start = (s32[8]{0:T(128)S(1)}, s32[8]{0:T(128)}, u32[]{:S(2)}) copy-start(s32[8]{0:T(128)} %length_ref.3) | copy-start | bytes 100
  2.2 10.7 %collective-permute-start.2 = (f32[6,2048]{1,0:T(8,128)}, f32[6,2048]{1,0:T(8,128)S(1)}, u32[]{:S(2)}, u32[]{:S(2)}) collective-permute-start(f32[6,2048]{1,0:T(8,128)} %get-tuple-element.23), channel_id=1, source_target_pairs={{0,24},{8,0},{16,8},{24,16},{1,25},{9,1},{17,9},{25,17},{2,26},{10... | collective-permute-start | bytes 147464 | tf_op jit(solution)/shard_map/ppermute | solution.py:491
  4.6 8.3 %collective-permute-start.1 = (f32[6,2048]{1,0:T(8,128)}, f32[6,2048]{1,0:T(8,128)S(1)}, u32[]{:S(2)}, u32[]{:S(2)}) collective-permute-start(f32[6,2048]{1,0:T(8,128)} %get-tuple-element.23), channel_id=1, source_target_pairs={{0,16},{8,24},{16,0},{24,8},{1,17},{9,25},{17,1},{25,9},{2,18},{10... | collective-permute-start | bytes 147464 | tf_op jit(solution)/shard_map/ppermute | solution.py:491
  5.3 7.7 %collective-permute-start = (f32[6,2048]{1,0:T(8,128)}, f32[6,2048]{1,0:T(8,128)S(1)}, u32[]{:S(2)}, u32[]{:S(2)}) collective-permute-start(f32[6,2048]{1,0:T(8,128)} %get-tuple-element.23), channel_id=1, source_target_pairs={{0,8},{8,16},{16,24},{24,0},{1,9},{9,17},{17,25},{25,1},{2,10},{10... | collective-permute-start | bytes 147464 | tf_op jit(solution)/shard_map/ppermute | solution.py:491
  5.4 13.1 %all-to-all-start = ((f32[32,1,256]{2,1,0:T(1,128)}), f32[32,1,256]{2,1,0:T(1,128)S(1)}, u32[]{:S(2)}, u32[]{:S(2)}) async-start(f32[32,1,256]{2,1,0:T(1,128)} %get-tuple-element.21), calls=%async_computation | async-start | bytes 65536 | tf_op jit(solution)/shard_map/all_to_all | solution.py:464
  21.8 9.8 %all-to-all-start.1 = ((f32[32,1,256]{2,1,0:T(1,128)}), f32[32,1,256]{2,1,0:T(1,128)S(1)}, u32[]{:S(2)}, u32[]{:S(2)}) async-start(f32[32,1,256]{2,1,0:T(1,128)} %get-tuple-element.28), calls=%async_computation.1 | async-start | bytes 65536 | tf_op jit(solution)/shard_map/all_to_all | solution.py:464
  35.2 12.1 %all-to-all-start.2 = ((f32[32,1,128]{2,1,0:T(1,128)}), f32[32,1,128]{2,1,0:T(1,128)S(1)}, u32[]{:S(2)}, u32[]{:S(2)}) async-start(f32[32,1,128]{2,1,0:T(1,128)} %get-tuple-element.32), calls=%async_computation.2 | async-start | bytes 32768 | tf_op jit(solution)/shard_map/all_to_all | solution.py:464

commit v10 on v9

--- a/solution.py
+++ b/solution.py
@@ -148,13 +148,12 @@
     return ((0, width // 2), (width // 2, 3 * width // 4), (3 * width // 4, width))
 
 
-def part_copy(kept, chunk, part, bounds, out):
+def part_copy(kept, chunk, part, bounds):
     local, remote, sems = kept
     start, stop = bounds[part]
-    here = local.at[chunk, :, start:stop]
-    there = remote.at[chunk, :, start:stop]
-    sem = sems.at[chunk * len(bounds) + part]
-    return pltpu.make_async_copy(here, there, sem) if out else pltpu.make_async_copy(there, here, sem)
+    return pltpu.make_async_copy(
+        remote.at[chunk, :, start:stop], local.at[chunk, :, start:stop], sems.at[chunk * len(bounds) + part]
+    )
 
 
 def for_parts(group_ref, length_ref, chunk, bounds, action, otherwise=None):
@@ -299,11 +298,12 @@
     return (group_ref[1, 0] + GROUP - 1) // GROUP
 
 
-def weigh_kernel(group_ref, length_ref, left_ref, right_ref, cubes_hbm, done_ref, cubes_ref, sems, *, n_row, n_col):
+def weigh_kernel(group_ref, left_ref, right_ref, cubes_hbm, done_ref, cubes_ref, sems, *, n_row, n_col):
     seg_dev = right_ref.shape[1] // (n_row * n_col)
     done_ref[...] = jnp.zeros_like(done_ref)
-    kept = (cubes_ref, cubes_hbm, sems)
-    bounds = part_bounds(n_col, seg_dev)
+
+    def chunk_copy(chunk):
+        return pltpu.make_async_copy(cubes_ref.at[chunk], cubes_hbm.at[chunk], sems.at[chunk])
 
     def step(k, carry):
         for part in range(GROUP):
@@ -314,19 +314,16 @@
                 high, low = cube_halves(left, right_ref[:, block_part(group_ref[0, chunk], col, n_row, seg_dev)])
                 cubes_ref[chunk, 0:CHUNK, to] = high
                 cubes_ref[chunk, CHUNK:2 * CHUNK, to] = low
+            chunk_copy(chunk).start()
+        return carry
+
+    def finish(k, carry):
         for part in range(GROUP):
-            chunk = k * GROUP + part
-            for_parts(group_ref, length_ref, chunk, bounds,
-                      lambda piece, chunk=chunk: part_copy(kept, chunk, piece, bounds, out=True).start())
+            chunk_copy(k * GROUP + part).wait()
         return carry
 
-    def finish(chunk, carry):
-        for_parts(group_ref, length_ref, chunk, bounds,
-                  lambda piece: part_copy(kept, chunk, piece, bounds, out=True).wait())
-        return carry
-
     lax.fori_loop(0, chunk_steps(group_ref), step, 0)
-    lax.fori_loop(0, group_ref[1, 0], finish, 0)
+    lax.fori_loop(0, chunk_steps(group_ref), finish, 0)
 
 
 def field_kernel(group_ref, length_ref, slot_ref, moment_ref, basis_ref, *refs, n_row, n_col, keep):
@@ -342,13 +339,13 @@
 
         def begin(chunk, carry):
             for_parts(group_ref, length_ref, chunk, bounds,
-                      lambda piece: part_copy(kept, chunk, piece, bounds, out=False).start(),
+                      lambda piece: part_copy(kept, chunk, piece, bounds).start(),
                       lambda piece: clear(chunk, piece))
             return carry
 
         def arrive(chunk):
             for_parts(group_ref, length_ref, chunk, bounds,
-                      lambda piece: part_copy(kept, chunk, piece, bounds, out=False).wait())
+                      lambda piece: part_copy(kept, chunk, piece, bounds).wait())
 
         lax.fori_loop(0, chunk_steps(group_ref) * GROUP, begin, 0)
     else:
@@ -533,12 +530,12 @@
         cubes, after = stream(
             functools.partial(weigh_kernel, n_row=n_row, n_col=n_col),
             out_shape=(shape(roomy(4 * CHUNK * width), *cube_shape[1:], dtype=jnp.bfloat16), shape(8, 128)),
-            in_specs=[smem, smem, vmem, vmem],
+            in_specs=[smem, vmem, vmem],
             out_specs=(hbm, vmem),
             scratch_shapes=cube_scratch,
             cost_estimate=work(5),
             name="weigh",
-        )(group_table, range_len, left, right)
+        )(group_table, left, right)
     else:
         after = group_table
     basis, basis_own, stats, known = call(

time: 49 us -> 48.6 us (level)
  transfers between devices with their start and end apart: 6 -> 6, of which waited for: 2 -> 2; matrix products, arithmetic and copies ran while one was open for 0% -> 0% of each run, Pallas kernels for 32% -> 31%
where the time goes in v10:
time: 48.6 us; the launch traced here: 48.2 us
  Pallas kernels  24.5 us (50%)
  starting transfers between devices  16.2 us (33%)
  waiting for transfers between devices  6.35 us (13%)
  between operations  0.86 us (2%)
    all_to_all x3, starting transfers between devices, exchange(): return lax.all_to_all(x, AXES, 0, 0, tiled=True)  13 us
    pallas_call x1, Pallas kernels, shards(): stream(functools.partial(field_kernel, n_row=n_row, n_col=n_col, keep=kee...  7.43 us
    all_to_all x3, waiting for transfers between devices, exchange(): return lax.all_to_all(x, AXES, 0, 0, tiled=True)  6.34 us
    pallas_call x1, Pallas kernels, shards(): stream(functools.partial(weigh_kernel, n_row=n_row, n_col=n_col), out_sha...  5.79 us
    pallas_call x1, Pallas kernels, shards(): call(functools.partial(second_kernel, coupling), out_shape=(shape(2, segm...  3.72 us
    ppermute x3, starting transfers between devices, shards(): lax.ppermute(geometry, 'col', [(k, (k + shift) % n_col) for k in range(n_...  3.23 us
    pallas_call x1, Pallas kernels, shards(): call(functools.partial(first_kernel, coupling), out_shape=(shape(1, seg_d...  3.22 us
    pallas_call x1, Pallas kernels, shards(): pl.pallas_call(entry_kernel, out_shape=(shape(n_dev, 1, seg_dev), shape(6...  1.48 us
  transfers between devices with their start and end apart: 6, of which 2 were waited for; matrix products, arithmetic and copies ran while one was open for 0% of the time, Pallas kernels for 31%

profile of v10, /device:TPU:0, one launch (start us, length us, event | category | flops | bytes accessed | tf_op | source)
XLA Modules:
  0.0 48.2 jit_solution(2936116619067996583)
XLA Ops:
  0.6 0.0 copy-start.2
  0.6 0.0 copy-start.1
  0.7 1.5 %entry.1 = (f32[32,1,256]{2,1,0:T(1,128)}, f32[6,2048]{1,0:T(8,128)}) custom-call(f32[1,256]{1,0:T(1,128)} %bitcast.11, f32[3,2048]{1,0:T(4,128)} %centers_hbm.1, f32[3,2048]{1,0:T(4,128)} %tangents_hbm.1), custom_call_target="tpu_custom_call" | custom-call | flops 8000000000 | tf_op jit(solution)/shard_map/entry/pallas_call | solution.py:463
  2.2 2.4 %collective-permute-start.2 = (f32[6,2048]{1,0:T(8,128)}, f32[6,2048]{1,0:T(8,128)S(1)}, u32[]{:S(2)}, u32[]{:S(2)}) collective-permute-start(f32[6,2048]{1,0:T(8,128)} %get-tuple-element.23), channel_id=1, source_target_pairs={{0,24},{8,0},{16,8},{24,16},{1,25},{9,1},{17,9},{25,17},{2,26},{10... | collective-permute-start | bytes 147464 | tf_op jit(solution)/shard_map/ppermute | solution.py:488
  4.6 0.6 %collective-permute-start.1 = (f32[6,2048]{1,0:T(8,128)}, f32[6,2048]{1,0:T(8,128)S(1)}, u32[]{:S(2)}, u32[]{:S(2)}) collective-permute-start(f32[6,2048]{1,0:T(8,128)} %get-tuple-element.23), channel_id=1, source_target_pairs={{0,16},{8,24},{16,0},{24,8},{1,17},{9,25},{17,1},{25,9},{2,18},{10... | collective-permute-start | bytes 147464 | tf_op jit(solution)/shard_map/ppermute | solution.py:488
  5.2 0.2 collective-permute-start
  5.4 5.9 %all-to-all-start = ((f32[32,1,256]{2,1,0:T(1,128)}), f32[32,1,256]{2,1,0:T(1,128)S(1)}, u32[]{:S(2)}, u32[]{:S(2)}) async-start(f32[32,1,256]{2,1,0:T(1,128)} %get-tuple-element.21), calls=%async_computation | async-start | bytes 65536 | tf_op jit(solution)/shard_map/all_to_all | solution.py:461
  11.5 0.2 concatenate.7.bundle_ref.refs_0_
  11.7 1.2 %group_points.1 = (s32[1,2048]{1,0:T(1,128)S(1)}, s32[8,128]{1,0:T(8,128)S(1)}, bf16[3072,48]{1,0:T(8,128)(2,1)S(1)}) custom-call(f32[11,2048]{1,0:T(8,128)S(1)} %concatenate.7.bundle_ref.refs_0_), custom_call_target="tpu_custom_call" | custom-call | flops 3000000000 | tf_op jit(solution)/shard_map/group_points/pallas_call | solution.py:493
  12.9 0.0 collective-permute-done.2.refs_3_
  12.9 0.0 collective-permute-done.1.refs_2_
  12.9 0.0 collective-permute-done.refs_1_
  12.9 0.6 %sides.1 = (bf16[48,8192]{1,0:T(8,128)(2,1)S(1)}, f32[8,8192]{1,0:T(8,128)S(1)}, bf16[2,256,48]{2,1,0:T(8,128)(2,1)S(1)}, f32[3,256,128]{2,1,0:T(8,128)S(1)}) custom-call(f32[11,2048]{1,0:T(8,128)S(1)} %concatenate.7.bundle_ref.refs_0_, f32[6,2048]{1,0:T(8,128)S(1)} %collective-permute-done.refs_1_, f32[6,2048]{1,0:T(8,128)S(1)} %collective-permute-done.1.refs_2_, ...), custom_call_target="tpu_custom_call" | custom-call | flops 1000000000 | tf_op jit(solution)/shard_map/sides/pallas_call | solution.py:510
  13.6 0.0 copy-start
  13.6 5.0 %all-to-all-done = f32[32,1,256]{2,1,0:T(1,128)S(1)} async-done(((f32[32,1,256]{2,1,0:T(1,128)}), f32[32,1,256]{2,1,0:T(1,128)S(1)}, u32[]{:S(2)}, u32[]{:S(2)}) %all-to-all-start) | async-done | bytes 32800 | tf_op jit(solution)/shard_map/all_to_all | solution.py:461
  18.5 3.2 %first_image.1 = (f32[1,256]{1,0:T(1,128)S(1)}, f32[32,1,256]{2,1,0:T(1,128)}) custom-call(f32[1,8192]{1,0:T(1,128)S(1)} %bitcast.7, f32[11,2048]{1,0:T(8,128)S(1)} %concatenate.7.bundle_ref.refs_0_, s32[8,128]{1,0:T(8,128)S(1)} %get-tuple-element.22.after_ref.group_ref, bf16[48,8192]{1,0:T(8,128)(2,1)S(1)} %get-tuple-element.24.right_ref, ...), custom_call_target="tpu_custom_call" | custom-call | flops 3000000000 | tf_op jit(solution)/shard_map/first_image/pallas_call | solution.py:520
  21.8 2.6 %all-to-all-start.1 = ((f32[32,1,256]{2,1,0:T(1,128)}), f32[32,1,256]{2,1,0:T(1,128)S(1)}, u32[]{:S(2)}, u32[]{:S(2)}) async-start(f32[32,1,256]{2,1,0:T(1,128)} %get-tuple-element.28), calls=%async_computation.1 | async-start | bytes 65536 | tf_op jit(solution)/shard_map/all_to_all | solution.py:461
  24.3 5.8 %weigh.1 = (bf16[40,256,1024]{2,1,0:T(8,128)(2,1)}, f32[8,128]{1,0:T(8,128)S(1)}) custom-call(s32[8,128]{1,0:T(8,128)S(1)} %get-tuple-element.22.after_ref.group_ref, bf16[3072,48]{1,0:T(8,128)(2,1)S(1)} %get-tuple-element.30.left_ref, bf16[48,8192]{1,0:T(8,128)(2,1)S(1)} %get-tuple-element.24.right_ref), custom_call_target="tpu_custom_call" | custom-call | flops 5000000000 | tf_op jit(solution)/shard_map/weigh/pallas_call | solution.py:530
  30.1 1.4 %all-to-all-done.1 = f32[32,1,256]{2,1,0:T(1,128)S(1)} async-done(((f32[32,1,256]{2,1,0:T(1,128)}), f32[32,1,256]{2,1,0:T(1,128)S(1)}, u32[]{:S(2)}, u32[]{:S(2)}) %all-to-all-start.1) | async-done | bytes 32800 | tf_op jit(solution)/shard_map/all_to_all | solution.py:461
  31.5 3.7 %second_image.1 = (f32[2,8192]{1,0:T(2,128)S(1)}, f32[2,256]{1,0:T(2,128)S(1)}, f32[32,1,128]{2,1,0:T(1,128)}, f32[1,128]{1,0:T(1,128)S(1)}) custom-call(f32[1,8192]{1,0:T(1,128)S(1)} %bitcast.8, f32[1,8192]{1,0:T(1,128)S(1)} %bitcast.9, f32[1,256]{1,0:T(1,128)S(1)} %get-tuple-element.29.image_own_ref, f32[11,2048]{1,0:T(8,128)S(1)} %concatenate.7.bundle_ref.refs_0_, ...), custom_call_target="tpu_custom_call" | custom-call | flops 3000000000 | tf_op jit(solution)/shard_map/second_image/pallas_call | solution.py:541
  35.3 4.5 %all-to-all-start.2 = ((f32[32,1,128]{2,1,0:T(1,128)}), f32[32,1,128]{2,1,0:T(1,128)S(1)}, u32[]{:S(2)}, u32[]{:S(2)}) async-start(f32[32,1,128]{2,1,0:T(1,128)} %get-tuple-element.32), calls=%async_computation.2 | async-start | bytes 32768 | tf_op jit(solution)/shard_map/all_to_all | solution.py:461
  39.7 7.4 %block_field.1.field_ref = f32[12,2048]{1,0:T(8,128)S(1)} custom-call(s32[8,128]{1,0:T(8,128)S(1)} %get-tuple-element.22.after_ref.group_ref, s32[8]{0:T(128)S(1)} %copy-done, s32[1,2048]{1,0:T(1,128)S(1)} %get-tuple-element.35.slot_ref, f32[8,8192]{1,0:T(8,128)S(1)} %get-tuple-element.25.moment_ref, f32[2,8192]{1,0:T(2,128)S(1)} %get-tuple-element.36.basis_ref, ...), custom_call_target="tpu_custom_call" | custom-call | flops 6000000000 | tf_op jit(solution)/shard_map/block_field/pallas_call | solution.py:550
  47.2 0.0 all-to-all-done.2.stats_ref
  47.2 1.0 %combine.1 = (f32[1,256]{1,0:T(1,128)}, f32[3,2048]{1,0:T(4,128)}) custom-call(f32[32,1,128]{2,1,0:T(1,128)S(1)} %all-to-all-done.2.stats_ref, f32[1,128]{1,0:T(1,128)S(1)} %get-tuple-element.33.known_ref, f32[2,256]{1,0:T(2,128)S(1)} %get-tuple-element.34.basis_own_ref, f32[12,2048]{1,0:T(8,128)S(1)} %block_field.1.field_ref, ...), custom_call_target="tpu_custom_call" | custom-call | tf_op jit(solution)/shard_map/combine/pallas_call | solution.py:561
  (14 shorter events, 0.0 us)
Async XLA Ops:
  0.6 10.8 %copy-start.2 = (f32[3,2048]{1,0:T(4,128)S(1)}, f32[3,2048]{1,0:T(4,128)}, u32[]{:S(2)}) copy-start(f32[3,2048]{1,0:T(4,128)} %tangents_hbm.1) | copy-start | bytes 73732
  0.6 10.8 %copy-start.1 = (f32[3,2048]{1,0:T(4,128)S(1)}, f32[3,2048]{1,0:T(4,128)}, u32[]{:S(2)}) copy-start(f32[3,2048]{1,0:T(4,128)} %centers_hbm.1) | copy-start | bytes 73732
  0.7 10.7 %copy-start.5 = (f32[256]{0:T(256)S(1)}, f32[256]{0:T(256)}, u32[]{:S(2)}) copy-start(f32[256]{0:T(256)} %param.7) | copy-start | bytes 3076
  0.7 10.7 %copy-start.6 = (f32[256]{0:T(256)S(1)}, f32[256]{0:T(256)}, u32[]{:S(2)}) copy-start(f32[256]{0:T(256)} %param.8) | copy-start | bytes 3076
  0.7 10.7 %copy-start.4 = (s32[2048,1]{0,1:T(1,128)S(1)}, s32[2048,1]{0,1:T(1,128)}, u32[]{:S(2)}) copy-start(s32[2048,1]{0,1:T(1,128)} %param.12) | copy-start | bytes 24580
  0.7 10.8 %copy-start.3 = (f32[3,2048]{1,0:T(4,128)S(1)}, f32[3,2048]{1,0:T(4,128)}, u32[]{:S(2)}) copy-start(f32[3,2048]{1,0:T(4,128)} %param.11) | copy-start | bytes 73732
  2.2 10.7 %collective-permute-start.2 = (f32[6,2048]{1,0:T(8,128)}, f32[6,2048]{1,0:T(8,128)S(1)}, u32[]{:S(2)}, u32[]{:S(2)}) collective-permute-start(f32[6,2048]{1,0:T(8,128)} %get-tuple-element.23), channel_id=1, source_target_pairs={{0,24},{8,0},{16,8},{24,16},{1,25},{9,1},{17,9},{25,17},{2,26},{10... | collective-permute-start | bytes 147464 | tf_op jit(solution)/shard_map/ppermute | solution.py:488
  4.6 8.3 %collective-permute-start.1 = (f32[6,2048]{1,0:T(8,128)}, f32[6,2048]{1,0:T(8,128)S(1)}, u32[]{:S(2)}, u32[]{:S(2)}) collective-permute-start(f32[6,2048]{1,0:T(8,128)} %get-tuple-element.23), channel_id=1, source_target_pairs={{0,16},{8,24},{16,0},{24,8},{1,17},{9,25},{17,1},{25,9},{2,18},{10... | collective-permute-start | bytes 147464 | tf_op jit(solution)/shard_map/ppermute | solution.py:488
  5.2 7.7 %collective-permute-start = (f32[6,2048]{1,0:T(8,128)}, f32[6,2048]{1,0:T(8,128)S(1)}, u32[]{:S(2)}, u32[]{:S(2)}) collective-permute-start(f32[6,2048]{1,0:T(8,128)} %get-tuple-element.23), channel_id=1, source_target_pairs={{0,8},{8,16},{16,24},{24,0},{1,9},{9,17},{17,25},{25,1},{2,10},{10... | collective-permute-start | bytes 147464 | tf_op jit(solution)/shard_map/ppermute | solution.py:488
  5.4 13.1 %all-to-all-start = ((f32[32,1,256]{2,1,0:T(1,128)}), f32[32,1,256]{2,1,0:T(1,128)S(1)}, u32[]{:S(2)}, u32[]{:S(2)}) async-start(f32[32,1,256]{2,1,0:T(1,128)} %get-tuple-element.21), calls=%async_computation | async-start | bytes 65536 | tf_op jit(solution)/shard_map/all_to_all | solution.py:461
  13.6 26.1 %copy-start = (s32[8]{0:T(128)S(1)}, s32[8]{0:T(128)}, u32[]{:S(2)}) copy-start(s32[8]{0:T(128)} %length_ref.1) | copy-start | bytes 100
  21.8 9.8 %all-to-all-start.1 = ((f32[32,1,256]{2,1,0:T(1,128)}), f32[32,1,256]{2,1,0:T(1,128)S(1)}, u32[]{:S(2)}, u32[]{:S(2)}) async-start(f32[32,1,256]{2,1,0:T(1,128)} %get-tuple-element.28), calls=%async_computation.1 | async-start | bytes 65536 | tf_op jit(solution)/shard_map/all_to_all | solution.py:461
  35.3 11.9 %all-to-all-start.2 = ((f32[32,1,128]{2,1,0:T(1,128)}), f32[32,1,128]{2,1,0:T(1,128)S(1)}, u32[]{:S(2)}, u32[]{:S(2)}) async-start(f32[32,1,128]{2,1,0:T(1,128)} %get-tuple-element.32), calls=%async_computation.2 | async-start | bytes 32768 | tf_op jit(solution)/shard_map/all_to_all | solution.py:461

commit v11 on v10

--- a/solution.py
+++ b/solution.py
@@ -13,6 +13,7 @@
 AXES = ("col", "row")
 CHUNK = 128
 GROUP = 4
+EARLY = 8
 TILE = 512
 COLUMNS = 256
 ROWS = 64
@@ -148,11 +149,11 @@
     return ((0, width // 2), (width // 2, 3 * width // 4), (3 * width // 4, width))
 
 
-def part_copy(kept, chunk, part, bounds):
-    local, remote, sems = kept
+def part_copy(kept, chunk, part, bounds, remote, first):
+    local, sems = kept
     start, stop = bounds[part]
     return pltpu.make_async_copy(
-        remote.at[chunk, :, start:stop], local.at[chunk, :, start:stop], sems.at[chunk * len(bounds) + part]
+        remote.at[chunk - first, :, start:stop], local.at[chunk, :, start:stop], sems.at[chunk * len(bounds) + part]
     )
 
 
@@ -298,38 +299,40 @@
     return (group_ref[1, 0] + GROUP - 1) // GROUP
 
 
-def weigh_kernel(group_ref, left_ref, right_ref, cubes_hbm, done_ref, cubes_ref, sems, *, n_row, n_col):
+def weigh_kernel(group_ref, left_ref, right_ref, cubes_hbm, done_ref, cubes_ref, sems, *, n_row, n_col, first, last):
     seg_dev = right_ref.shape[1] // (n_row * n_col)
     done_ref[...] = jnp.zeros_like(done_ref)
-
-    def chunk_copy(chunk):
-        return pltpu.make_async_copy(cubes_ref.at[chunk], cubes_hbm.at[chunk], sems.at[chunk])
+    stop = chunk_steps(group_ref) if last is None else last // GROUP
+
+    def chunk_copy(place):
+        return pltpu.make_async_copy(cubes_ref.at[place], cubes_hbm.at[place], sems.at[place])
 
     def step(k, carry):
         for part in range(GROUP):
             chunk = k * GROUP + part
+            place = chunk - first
             left = left_ref[aligned(chunk * CHUNK, CHUNK), :]
             for col in range(n_col):
                 to = slice(col * seg_dev, (col + 1) * seg_dev)
                 high, low = cube_halves(left, right_ref[:, block_part(group_ref[0, chunk], col, n_row, seg_dev)])
-                cubes_ref[chunk, 0:CHUNK, to] = high
-                cubes_ref[chunk, CHUNK:2 * CHUNK, to] = low
-            chunk_copy(chunk).start()
+                cubes_ref[place, 0:CHUNK, to] = high
+                cubes_ref[place, CHUNK:2 * CHUNK, to] = low
+            chunk_copy(place).start()
         return carry
 
     def finish(k, carry):
         for part in range(GROUP):
-            chunk_copy(k * GROUP + part).wait()
+            chunk_copy(k * GROUP + part - first).wait()
         return carry
 
-    lax.fori_loop(0, chunk_steps(group_ref), step, 0)
-    lax.fori_loop(0, chunk_steps(group_ref), finish, 0)
+    lax.fori_loop(first // GROUP, stop, step, 0)
+    lax.fori_loop(first // GROUP, stop, finish, 0)
 
 
 def field_kernel(group_ref, length_ref, slot_ref, moment_ref, basis_ref, *refs, n_row, n_col, keep):
     if keep:
-        cubes_hbm, out_ref, table_ref, sums_ref, cubes_ref, sems = refs
-        kept = (cubes_ref, cubes_hbm, sems)
+        early_hbm, late_hbm, out_ref, table_ref, sums_ref, cubes_ref, sems = refs
+        kept = (cubes_ref, sems)
 
         bounds = part_bounds(n_col, moment_ref.shape[1] // (n_row * n_col))
 
@@ -337,17 +340,18 @@
             start, stop = bounds[piece]
             cubes_ref[chunk, :, start:stop] = jnp.zeros((2 * CHUNK, stop - start), jnp.bfloat16)
 
-        def begin(chunk, carry):
+        def begin(remote, first, chunk, carry):
             for_parts(group_ref, length_ref, chunk, bounds,
-                      lambda piece: part_copy(kept, chunk, piece, bounds).start(),
+                      lambda piece: part_copy(kept, chunk, piece, bounds, remote, first).start(),
                       lambda piece: clear(chunk, piece))
             return carry
 
-        def arrive(chunk):
+        def arrive(remote, first, chunk):
             for_parts(group_ref, length_ref, chunk, bounds,
-                      lambda piece: part_copy(kept, chunk, piece, bounds).wait())
-
-        lax.fori_loop(0, chunk_steps(group_ref) * GROUP, begin, 0)
+                      lambda piece: part_copy(kept, chunk, piece, bounds, remote, first).wait())
+
+        lax.fori_loop(0, EARLY, functools.partial(begin, early_hbm, 0), 0)
+        lax.fori_loop(EARLY, chunk_steps(group_ref) * GROUP, functools.partial(begin, late_hbm, EARLY), 0)
     else:
         left_ref, right_ref, out_ref, table_ref, sums_ref = refs
     chunk_count = sums_ref.shape[0] // 16
@@ -378,10 +382,10 @@
     def cubes_of(chunk):
         return jnp.concatenate(cube_halves(left_ref[aligned(chunk * CHUNK, CHUNK), :], block_row(right_ref, chunk)), axis=0)
 
-    def step(k, carry):
+    def step(source, k, carry):
         if keep:
             for part in range(GROUP):
-                arrive(k * GROUP + part)
+                arrive(*source, k * GROUP + part)
         for part in range(0, GROUP, 2):
             chunk = k * GROUP + part
             tables = jnp.concatenate([block_row(table_ref, chunk), block_row(table_ref, chunk + 1)], axis=0)
@@ -396,7 +400,11 @@
                 sums_ref[pl.ds(chunk + half, 16, stride=chunk_count), :] = total[0:16] + total[16:32]
         return carry
 
-    lax.fori_loop(0, chunk_steps(group_ref), step, 0)
+    if keep:
+        lax.fori_loop(0, EARLY // GROUP, functools.partial(step, (early_hbm, 0)), 0)
+        lax.fori_loop(EARLY // GROUP, chunk_steps(group_ref), functools.partial(step, (late_hbm, EARLY)), 0)
+    else:
+        lax.fori_loop(0, chunk_steps(group_ref), functools.partial(step, None), 0)
     sums = jnp.concatenate([sums_ref[0:6 * chunk_count], sums_ref[8 * chunk_count:14 * chunk_count]], axis=0)
     sums = jnp.concatenate(split3(sums), axis=1).astype(jnp.bfloat16)
     for tile in range(slot_ref.shape[1] // TILE):
@@ -517,25 +525,33 @@
         name="sides",
     )(*pieces)
     right, moment = sides[0:2]
+    def weigh(first, last, microseconds, name):
+        count = (last or chunk_count) - first
+        return stream(
+            functools.partial(weigh_kernel, n_row=n_row, n_col=n_col, first=first, last=last),
+            out_shape=(shape(roomy(4 * CHUNK * width), *cube_shape[1:], dtype=jnp.bfloat16), shape(8, 128)),
+            in_specs=[smem, vmem, vmem],
+            out_specs=(hbm, vmem),
+            scratch_shapes=[pltpu.VMEM((count,) + cube_shape[1:], jnp.bfloat16), pltpu.SemaphoreType.DMA((count,))],
+            cost_estimate=work(microseconds),
+            name=name,
+        )(group_table, left, right)
+
+    if keep:
+        early, before = weigh(0, EARLY, 2, "weigh_early")
+    else:
+        before = group_table
     image_own, image_spread = call(
         functools.partial(first_kernel, coupling),
         out_shape=(shape(1, seg_dev), shape(n_dev, 1, seg_dev)),
         scratch_shapes=scratch,
         cost_estimate=work(3),
         name="first_image",
-    )(drive_all, bundle, group_table, *sides)
+    )(drive_all, bundle, before, *sides)
     image_all = exchange(image_spread).reshape(1, segments)
     cube_scratch = [pltpu.VMEM(cube_shape, jnp.bfloat16), pltpu.SemaphoreType.DMA((3 * chunk_count,))]
     if keep:
-        cubes, after = stream(
-            functools.partial(weigh_kernel, n_row=n_row, n_col=n_col),
-            out_shape=(shape(roomy(4 * CHUNK * width), *cube_shape[1:], dtype=jnp.bfloat16), shape(8, 128)),
-            in_specs=[smem, vmem, vmem],
-            out_specs=(hbm, vmem),
-            scratch_shapes=cube_scratch,
-            cost_estimate=work(5),
-            name="weigh",
-        )(group_table, left, right)
+        late, after = weigh(EARLY, None, 4, "weigh_late")
     else:
         after = group_table
     basis, basis_own, stats, known = call(
@@ -550,14 +566,14 @@
     field = stream(
         functools.partial(field_kernel, n_row=n_row, n_col=n_col, keep=keep),
         out_shape=shape(12, points_count),
-        in_specs=[smem, smem, vmem, vmem, vmem] + ([hbm] if keep else [vmem, vmem]),
+        in_specs=[smem, smem, vmem, vmem, vmem] + ([hbm, hbm] if keep else [vmem, vmem]),
         scratch_shapes=[
             pltpu.VMEM((32, segments), jnp.bfloat16),
             pltpu.VMEM((16 * chunk_count, CHUNK), jnp.float32),
         ] + (cube_scratch if keep else []),
         cost_estimate=work(6),
         name="block_field",
-    )(group_table, range_len, slot, moment, basis, *([cubes] if keep else [left, right]))
+    )(group_table, range_len, slot, moment, basis, *([early, late] if keep else [left, right]))
     currents, iron_field = stream(
         final_kernel,
         out_shape=(shape(1, seg_dev), shape(3, points_count)),

time: 48.6 us -> 47.8 us (0.984)
  Pallas kernels: 24.5 us -> 25.6 us
  waiting for transfers between devices: 6.35 us -> 5.28 us
  starting transfers between devices: 16.2 us -> 15.6 us
    all_to_all x3, waiting for transfers between devices: 6.34 us -> 5.27 us  [exchange(): return lax.all_to_all(x, AXES, 0, 0, tiled=True)]
    pallas_call x1 -> x2, Pallas kernels: 5.79 us -> 6.86 us  [weigh(): stream(functools.partial(weigh_kernel, n_row=n_row, n_col=n_col, first=fi...]
    all_to_all x3, starting transfers between devices: 13 us -> 12.4 us  [exchange(): return lax.all_to_all(x, AXES, 0, 0, tiled=True)]
  transfers between devices with their start and end apart: 6 -> 6, of which waited for: 2 -> 2; matrix products, arithmetic and copies ran while one was open for 0% -> 1% of each run, Pallas kernels for 31% -> 34%
where the time goes in v11:
time: 47.8 us; the launch traced here: 47.6 us
  Pallas kernels  25.6 us (54%)
  starting transfers between devices  15.6 us (33%)
  waiting for transfers between devices  5.28 us (11%)
  between operations  0.87 us (2%)
    all_to_all x3, starting transfers between devices, exchange(): return lax.all_to_all(x, AXES, 0, 0, tiled=True)  12.4 us
    pallas_call x1, Pallas kernels, shards(): stream(functools.partial(field_kernel, n_row=n_row, n_col=n_col, keep=kee...  7.43 us
    pallas_call x2, Pallas kernels, weigh(): stream(functools.partial(weigh_kernel, n_row=n_row, n_col=n_col, first=fi...  6.86 us
    all_to_all x3, waiting for transfers between devices, exchange(): return lax.all_to_all(x, AXES, 0, 0, tiled=True)  5.27 us
    pallas_call x1, Pallas kernels, shards(): call(functools.partial(second_kernel, coupling), out_shape=(shape(2, segm...  3.72 us
    ppermute x3, starting transfers between devices, shards(): lax.ppermute(geometry, 'col', [(k, (k + shift) % n_col) for k in range(n_...  3.23 us
    pallas_call x1, Pallas kernels, shards(): call(functools.partial(first_kernel, coupling), out_shape=(shape(1, seg_d...  3.23 us
    pallas_call x1, Pallas kernels, shards(): pl.pallas_call(entry_kernel, out_shape=(shape(n_dev, 1, seg_dev), shape(6...  1.47 us
  transfers between devices with their start and end apart: 6, of which 2 were waited for; matrix products, arithmetic and copies ran while one was open for 1% of the time, Pallas kernels for 34%

profile of v11, /device:TPU:0, one launch (start us, length us, event | category | flops | bytes accessed | tf_op | source)
XLA Modules:
  0.0 47.6 jit_solution(15069108249315829060)
XLA Ops:
  0.7 1.5 %entry.1 = (f32[32,1,256]{2,1,0:T(1,128)}, f32[6,2048]{1,0:T(8,128)}) custom-call(f32[1,256]{1,0:T(1,128)} %bitcast.11, f32[3,2048]{1,0:T(4,128)} %centers_hbm.1, f32[3,2048]{1,0:T(4,128)} %tangents_hbm.1), custom_call_target="tpu_custom_call" | custom-call | flops 8000000000 | tf_op jit(solution)/shard_map/entry/pallas_call | solution.py:471
  2.2 2.4 %collective-permute-start.2 = (f32[6,2048]{1,0:T(8,128)}, f32[6,2048]{1,0:T(8,128)S(1)}, u32[]{:S(2)}, u32[]{:S(2)}) collective-permute-start(f32[6,2048]{1,0:T(8,128)} %get-tuple-element.26), channel_id=1, source_target_pairs={{0,24},{8,0},{16,8},{24,16},{1,25},{9,1},{17,9},{25,17},{2,26},{10... | collective-permute-start | bytes 147464 | tf_op jit(solution)/shard_map/ppermute | solution.py:496
  4.6 0.6 %collective-permute-start.1 = (f32[6,2048]{1,0:T(8,128)}, f32[6,2048]{1,0:T(8,128)S(1)}, u32[]{:S(2)}, u32[]{:S(2)}) collective-permute-start(f32[6,2048]{1,0:T(8,128)} %get-tuple-element.26), channel_id=1, source_target_pairs={{0,16},{8,24},{16,0},{24,8},{1,17},{9,25},{17,1},{25,9},{2,18},{10... | collective-permute-start | bytes 147464 | tf_op jit(solution)/shard_map/ppermute | solution.py:496
  5.2 0.2 collective-permute-start
  5.4 5.9 %all-to-all-start = ((f32[32,1,256]{2,1,0:T(1,128)}), f32[32,1,256]{2,1,0:T(1,128)S(1)}, u32[]{:S(2)}, u32[]{:S(2)}) async-start(f32[32,1,256]{2,1,0:T(1,128)} %get-tuple-element.23), calls=%async_computation | async-start | bytes 65536 | tf_op jit(solution)/shard_map/all_to_all | solution.py:469
  11.4 0.0 copy-done.2
  11.5 0.2 concatenate.7.bundle_ref.refs_0_
  11.7 1.2 %group_points.1 = (s32[1,2048]{1,0:T(1,128)S(1)}, s32[8,128]{1,0:T(8,128)S(1)}, bf16[3072,48]{1,0:T(8,128)(2,1)S(1)}) custom-call(f32[11,2048]{1,0:T(8,128)S(1)} %concatenate.7.bundle_ref.refs_0_), custom_call_target="tpu_custom_call" | custom-call | flops 3000000000 | tf_op jit(solution)/shard_map/group_points/pallas_call | solution.py:501
  12.9 0.0 collective-permute-done.2.refs_3_
  12.9 0.0 collective-permute-done.1.refs_2_
  12.9 0.0 collective-permute-done.refs_1_
  12.9 0.6 %sides.1 = (bf16[48,8192]{1,0:T(8,128)(2,1)S(1)}, f32[8,8192]{1,0:T(8,128)S(1)}, bf16[2,256,48]{2,1,0:T(8,128)(2,1)S(1)}, f32[3,256,128]{2,1,0:T(8,128)S(1)}) custom-call(f32[11,2048]{1,0:T(8,128)S(1)} %concatenate.7.bundle_ref.refs_0_, f32[6,2048]{1,0:T(8,128)S(1)} %collective-permute-done.refs_1_, f32[6,2048]{1,0:T(8,128)S(1)} %collective-permute-done.1.refs_2_, ...), custom_call_target="tpu_custom_call" | custom-call | flops 1000000000 | tf_op jit(solution)/shard_map/sides/pallas_call | solution.py:518
  13.6 0.0 copy-start
  13.6 3.0 %weigh_early.1 = (bf16[40,256,1024]{2,1,0:T(8,128)(2,1)}, f32[8,128]{1,0:T(8,128)S(1)}) custom-call(s32[8,128]{1,0:T(8,128)S(1)} %get-tuple-element.24.group_ref, bf16[3072,48]{1,0:T(8,128)(2,1)S(1)} %get-tuple-element.25.left_ref, bf16[48,8192]{1,0:T(8,128)(2,1)S(1)} %get-tuple-element.27.right_ref), custom_call_target="tpu_custom_call" | custom-call | flops 2000000000 | tf_op jit(solution)/shard_map/weigh_early/pallas_call | solution.py:530
  16.6 2.0 %all-to-all-done = f32[32,1,256]{2,1,0:T(1,128)S(1)} async-done(((f32[32,1,256]{2,1,0:T(1,128)}), f32[32,1,256]{2,1,0:T(1,128)S(1)}, u32[]{:S(2)}, u32[]{:S(2)}) %all-to-all-start) | async-done | bytes 32800 | tf_op jit(solution)/shard_map/all_to_all | solution.py:469
  18.5 3.2 %first_image.1 = (f32[1,256]{1,0:T(1,128)S(1)}, f32[32,1,256]{2,1,0:T(1,128)}) custom-call(f32[1,8192]{1,0:T(1,128)S(1)} %bitcast.7, f32[11,2048]{1,0:T(8,128)S(1)} %concatenate.7.bundle_ref.refs_0_, f32[8,128]{1,0:T(8,128)S(1)} %get-tuple-element.28.after_ref, bf16[48,8192]{1,0:T(8,128)(2,1)S(1)} %get-tuple-element.27.right_ref, ...), custom_call_target="tpu_custom_call" | custom-call | flops 3000000000 | tf_op jit(solution)/shard_map/first_image/pallas_call | solution.py:544
  21.8 3.9 %all-to-all-start.1 = ((f32[32,1,256]{2,1,0:T(1,128)}), f32[32,1,256]{2,1,0:T(1,128)S(1)}, u32[]{:S(2)}, u32[]{:S(2)}) async-start(f32[32,1,256]{2,1,0:T(1,128)} %get-tuple-element.32), calls=%async_computation.1 | async-start | bytes 65536 | tf_op jit(solution)/shard_map/all_to_all | solution.py:469
  25.6 3.9 %weigh_late.1 = (bf16[40,256,1024]{2,1,0:T(8,128)(2,1)}, f32[8,128]{1,0:T(8,128)S(1)}) custom-call(s32[8,128]{1,0:T(8,128)S(1)} %get-tuple-element.24.group_ref, bf16[3072,48]{1,0:T(8,128)(2,1)S(1)} %get-tuple-element.25.left_ref, bf16[48,8192]{1,0:T(8,128)(2,1)S(1)} %get-tuple-element.27.right_ref), custom_call_target="tpu_custom_call" | custom-call | flops 4000000000 | tf_op jit(solution)/shard_map/weigh_late/pallas_call | solution.py:530
  29.5 3.3 %all-to-all-done.1 = f32[32,1,256]{2,1,0:T(1,128)S(1)} async-done(((f32[32,1,256]{2,1,0:T(1,128)}), f32[32,1,256]{2,1,0:T(1,128)S(1)}, u32[]{:S(2)}, u32[]{:S(2)}) %all-to-all-start.1) | async-done | bytes 32800 | tf_op jit(solution)/shard_map/all_to_all | solution.py:469
  32.8 3.7 %second_image.1 = (f32[2,8192]{1,0:T(2,128)S(1)}, f32[2,256]{1,0:T(2,128)S(1)}, f32[32,1,128]{2,1,0:T(1,128)}, f32[1,128]{1,0:T(1,128)S(1)}) custom-call(f32[1,8192]{1,0:T(1,128)S(1)} %bitcast.8, f32[1,8192]{1,0:T(1,128)S(1)} %bitcast.9, f32[1,256]{1,0:T(1,128)S(1)} %get-tuple-element.33.image_own_ref, f32[11,2048]{1,0:T(8,128)S(1)} %concatenate.7.bundle_ref.refs_0_, ...), custom_call_target="tpu_custom_call" | custom-call | flops 3000000000 | tf_op jit(solution)/shard_map/second_image/pallas_call | solution.py:557
  36.5 2.6 %all-to-all-start.2 = ((f32[32,1,128]{2,1,0:T(1,128)}), f32[32,1,128]{2,1,0:T(1,128)S(1)}, u32[]{:S(2)}, u32[]{:S(2)}) async-start(f32[32,1,128]{2,1,0:T(1,128)} %get-tuple-element.35), calls=%async_computation.2 | async-start | bytes 32768 | tf_op jit(solution)/shard_map/all_to_all | solution.py:469
  39.1 7.4 %block_field.1.field_ref = f32[12,2048]{1,0:T(8,128)S(1)} custom-call(s32[8,128]{1,0:T(8,128)S(1)} %get-tuple-element.24.group_ref, s32[8]{0:T(128)S(1)} %copy-done, s32[1,2048]{1,0:T(1,128)S(1)} %get-tuple-element.38.slot_ref, f32[8,8192]{1,0:T(8,128)S(1)} %get-tuple-element.29.moment_ref, f32[2,8192]{1,0:T(2,128)S(1)} %get-tuple-element.39.basis_ref, ...), custom_call_target="tpu_custom_call" | custom-call | flops 6000000000 | tf_op jit(solution)/shard_map/block_field/pallas_call | solution.py:566
  46.6 0.0 all-to-all-done.2.stats_ref
  46.6 1.0 %combine.1 = (f32[1,256]{1,0:T(1,128)}, f32[3,2048]{1,0:T(4,128)}) custom-call(f32[32,1,128]{2,1,0:T(1,128)S(1)} %all-to-all-done.2.stats_ref, f32[1,128]{1,0:T(1,128)S(1)} %get-tuple-element.36.known_ref, f32[2,256]{1,0:T(2,128)S(1)} %get-tuple-element.37.basis_own_ref, f32[12,2048]{1,0:T(8,128)S(1)} %block_field.1.field_ref, ...), custom_call_target="tpu_custom_call" | custom-call | tf_op jit(solution)/shard_map/combine/pallas_call | solution.py:577
  (15 shorter events, 0.0 us)
Async XLA Ops:
  0.6 10.8 %copy-start.2 = (f32[3,2048]{1,0:T(4,128)S(1)}, f32[3,2048]{1,0:T(4,128)}, u32[]{:S(2)}) copy-start(f32[3,2048]{1,0:T(4,128)} %tangents_hbm.1) | copy-start | bytes 73732
  0.6 10.8 %copy-start.1 = (f32[3,2048]{1,0:T(4,128)S(1)}, f32[3,2048]{1,0:T(4,128)}, u32[]{:S(2)}) copy-start(f32[3,2048]{1,0:T(4,128)} %centers_hbm.1) | copy-start | bytes 73732
  0.7 10.7 %copy-start.5 = (f32[256]{0:T(256)S(1)}, f32[256]{0:T(256)}, u32[]{:S(2)}) copy-start(f32[256]{0:T(256)} %param.7) | copy-start | bytes 3076
  0.7 10.7 %copy-start.6 = (f32[256]{0:T(256)S(1)}, f32[256]{0:T(256)}, u32[]{:S(2)}) copy-start(f32[256]{0:T(256)} %param.8) | copy-start | bytes 3076
  0.7 10.7 %copy-start.4 = (s32[2048,1]{0,1:T(1,128)S(1)}, s32[2048,1]{0,1:T(1,128)}, u32[]{:S(2)}) copy-start(s32[2048,1]{0,1:T(1,128)} %param.12) | copy-start | bytes 24580
  0.7 10.8 %copy-start.3 = (f32[3,2048]{1,0:T(4,128)S(1)}, f32[3,2048]{1,0:T(4,128)}, u32[]{:S(2)}) copy-start(f32[3,2048]{1,0:T(4,128)} %param.11) | copy-start | bytes 73732
  2.2 10.7 %collective-permute-start.2 = (f32[6,2048]{1,0:T(8,128)}, f32[6,2048]{1,0:T(8,128)S(1)}, u32[]{:S(2)}, u32[]{:S(2)}) collective-permute-start(f32[6,2048]{1,0:T(8,128)} %get-tuple-element.26), channel_id=1, source_target_pairs={{0,24},{8,0},{16,8},{24,16},{1,25},{9,1},{17,9},{25,17},{2,26},{10... | collective-permute-start | bytes 147464 | tf_op jit(solution)/shard_map/ppermute | solution.py:496
  4.6 8.3 %collective-permute-start.1 = (f32[6,2048]{1,0:T(8,128)}, f32[6,2048]{1,0:T(8,128)S(1)}, u32[]{:S(2)}, u32[]{:S(2)}) collective-permute-start(f32[6,2048]{1,0:T(8,128)} %get-tuple-element.26), channel_id=1, source_target_pairs={{0,16},{8,24},{16,0},{24,8},{1,17},{9,25},{17,1},{25,9},{2,18},{10... | collective-permute-start | bytes 147464 | tf_op jit(solution)/shard_map/ppermute | solution.py:496
  5.2 7.7 %collective-permute-start = (f32[6,2048]{1,0:T(8,128)}, f32[6,2048]{1,0:T(8,128)S(1)}, u32[]{:S(2)}, u32[]{:S(2)}) collective-permute-start(f32[6,2048]{1,0:T(8,128)} %get-tuple-element.26), channel_id=1, source_target_pairs={{0,8},{8,16},{16,24},{24,0},{1,9},{9,17},{17,25},{25,1},{2,10},{10... | collective-permute-start | bytes 147464 | tf_op jit(solution)/shard_map/ppermute | solution.py:496
  5.4 13.1 %all-to-all-start = ((f32[32,1,256]{2,1,0:T(1,128)}), f32[32,1,256]{2,1,0:T(1,128)S(1)}, u32[]{:S(2)}, u32[]{:S(2)}) async-start(f32[32,1,256]{2,1,0:T(1,128)} %get-tuple-element.23), calls=%async_computation | async-start | bytes 65536 | tf_op jit(solution)/shard_map/all_to_all | solution.py:469
  13.6 25.5 %copy-start = (s32[8]{0:T(128)S(1)}, s32[8]{0:T(128)}, u32[]{:S(2)}) copy-start(s32[8]{0:T(128)} %length_ref.1) | copy-start | bytes 100
  21.8 11.1 %all-to-all-start.1 = ((f32[32,1,256]{2,1,0:T(1,128)}), f32[32,1,256]{2,1,0:T(1,128)S(1)}, u32[]{:S(2)}, u32[]{:S(2)}) async-start(f32[32,1,256]{2,1,0:T(1,128)} %get-tuple-element.32), calls=%async_computation.1 | async-start | bytes 65536 | tf_op jit(solution)/shard_map/all_to_all | solution.py:469
  36.5 10.0 %all-to-all-start.2 = ((f32[32,1,128]{2,1,0:T(1,128)}), f32[32,1,128]{2,1,0:T(1,128)S(1)}, u32[]{:S(2)}, u32[]{:S(2)}) async-start(f32[32,1,128]{2,1,0:T(1,128)} %get-tuple-element.35), calls=%async_computation.2 | async-start | bytes 32768 | tf_op jit(solution)/shard_map/all_to_all | solution.py:469

commit v12 on v11

--- a/solution.py
+++ b/solution.py
@@ -13,7 +13,7 @@
 AXES = ("col", "row")
 CHUNK = 128
 GROUP = 4
-EARLY = 8
+EARLY = 4
 TILE = 512
 COLUMNS = 256
 ROWS = 64

time: 47.8 us -> 48 us (level)
  no operation moved by 1% of the time
where the time goes in v12:
time: 48 us; the launch traced here: 47.8 us
  Pallas kernels  25.8 us (54%)
  starting transfers between devices  15.6 us (32%)
  waiting for transfers between devices  5.29 us (11%)
  between operations  0.87 us (2%)
    all_to_all x3, starting transfers between devices, exchange(): return lax.all_to_all(x, AXES, 0, 0, tiled=True)  12.3 us
    pallas_call x1, Pallas kernels, shards(): stream(functools.partial(field_kernel, n_row=n_row, n_col=n_col, keep=kee...  7.64 us
    pallas_call x2, Pallas kernels, weigh(): stream(functools.partial(weigh_kernel, n_row=n_row, n_col=n_col, first=fi...  6.84 us
    all_to_all x3, waiting for transfers between devices, exchange(): return lax.all_to_all(x, AXES, 0, 0, tiled=True)  5.28 us
    pallas_call x1, Pallas kernels, shards(): call(functools.partial(second_kernel, coupling), out_shape=(shape(2, segm...  3.72 us
    ppermute x3, starting transfers between devices, shards(): lax.ppermute(geometry, 'col', [(k, (k + shift) % n_col) for k in range(n_...  3.23 us
    pallas_call x1, Pallas kernels, shards(): call(functools.partial(first_kernel, coupling), out_shape=(shape(1, seg_d...  3.23 us
    pallas_call x1, Pallas kernels, shards(): pl.pallas_call(entry_kernel, out_shape=(shape(n_dev, 1, seg_dev), shape(6...  1.47 us
  transfers between devices with their start and end apart: 6, of which 2 were waited for; matrix products, arithmetic and copies ran while one was open for 1% of the time, Pallas kernels for 34%

profile of v12, /device:TPU:0, one launch (start us, length us, event | category | flops | bytes accessed | tf_op | source)
XLA Modules:
  0.0 47.8 jit_solution(9846575975973637252)
XLA Ops:
  0.7 1.5 %entry.1 = (f32[32,1,256]{2,1,0:T(1,128)}, f32[6,2048]{1,0:T(8,128)}) custom-call(f32[1,256]{1,0:T(1,128)} %bitcast.11, f32[3,2048]{1,0:T(4,128)} %centers_hbm.1, f32[3,2048]{1,0:T(4,128)} %tangents_hbm.1), custom_call_target="tpu_custom_call" | custom-call | flops 8000000000 | tf_op jit(solution)/shard_map/entry/pallas_call | solution.py:471
  2.2 2.4 %collective-permute-start.2 = (f32[6,2048]{1,0:T(8,128)}, f32[6,2048]{1,0:T(8,128)S(1)}, u32[]{:S(2)}, u32[]{:S(2)}) collective-permute-start(f32[6,2048]{1,0:T(8,128)} %get-tuple-element.26), channel_id=1, source_target_pairs={{0,24},{8,0},{16,8},{24,16},{1,25},{9,1},{17,9},{25,17},{2,26},{10... | collective-permute-start | bytes 147464 | tf_op jit(solution)/shard_map/ppermute | solution.py:496
  4.6 0.6 %collective-permute-start.1 = (f32[6,2048]{1,0:T(8,128)}, f32[6,2048]{1,0:T(8,128)S(1)}, u32[]{:S(2)}, u32[]{:S(2)}) collective-permute-start(f32[6,2048]{1,0:T(8,128)} %get-tuple-element.26), channel_id=1, source_target_pairs={{0,16},{8,24},{16,0},{24,8},{1,17},{9,25},{17,1},{25,9},{2,18},{10... | collective-permute-start | bytes 147464 | tf_op jit(solution)/shard_map/ppermute | solution.py:496
  5.2 0.2 collective-permute-start
  5.4 5.9 %all-to-all-start = ((f32[32,1,256]{2,1,0:T(1,128)}), f32[32,1,256]{2,1,0:T(1,128)S(1)}, u32[]{:S(2)}, u32[]{:S(2)}) async-start(f32[32,1,256]{2,1,0:T(1,128)} %get-tuple-element.23), calls=%async_computation | async-start | bytes 65536 | tf_op jit(solution)/shard_map/all_to_all | solution.py:469
  11.4 0.0 copy-done.2
  11.5 0.2 concatenate.7.bundle_ref.refs_0_
  11.7 1.2 %group_points.1 = (s32[1,2048]{1,0:T(1,128)S(1)}, s32[8,128]{1,0:T(8,128)S(1)}, bf16[3072,48]{1,0:T(8,128)(2,1)S(1)}) custom-call(f32[11,2048]{1,0:T(8,128)S(1)} %concatenate.7.bundle_ref.refs_0_), custom_call_target="tpu_custom_call" | custom-call | flops 3000000000 | tf_op jit(solution)/shard_map/group_points/pallas_call | solution.py:501
  12.9 0.0 collective-permute-done.2.refs_3_
  12.9 0.0 collective-permute-done.1.refs_2_
  12.9 0.0 collective-permute-done.refs_1_
  12.9 0.6 %sides.1 = (bf16[48,8192]{1,0:T(8,128)(2,1)S(1)}, f32[8,8192]{1,0:T(8,128)S(1)}, bf16[2,256,48]{2,1,0:T(8,128)(2,1)S(1)}, f32[3,256,128]{2,1,0:T(8,128)S(1)}) custom-call(f32[11,2048]{1,0:T(8,128)S(1)} %concatenate.7.bundle_ref.refs_0_, f32[6,2048]{1,0:T(8,128)S(1)} %collective-permute-done.refs_1_, f32[6,2048]{1,0:T(8,128)S(1)} %collective-permute-done.1.refs_2_, ...), custom_call_target="tpu_custom_call" | custom-call | flops 1000000000 | tf_op jit(solution)/shard_map/sides/pallas_call | solution.py:518
  13.6 0.0 copy-start
  13.6 2.3 %weigh_early.1 = (bf16[40,256,1024]{2,1,0:T(8,128)(2,1)}, f32[8,128]{1,0:T(8,128)S(1)}) custom-call(s32[8,128]{1,0:T(8,128)S(1)} %get-tuple-element.24.group_ref, bf16[3072,48]{1,0:T(8,128)(2,1)S(1)} %get-tuple-element.25.left_ref, bf16[48,8192]{1,0:T(8,128)(2,1)S(1)} %get-tuple-element.27.right_ref), custom_call_target="tpu_custom_call" | custom-call | flops 2000000000 | tf_op jit(solution)/shard_map/weigh_early/pallas_call | solution.py:530
  15.8 2.7 %all-to-all-done = f32[32,1,256]{2,1,0:T(1,128)S(1)} async-done(((f32[32,1,256]{2,1,0:T(1,128)}), f32[32,1,256]{2,1,0:T(1,128)S(1)}, u32[]{:S(2)}, u32[]{:S(2)}) %all-to-all-start) | async-done | bytes 32800 | tf_op jit(solution)/shard_map/all_to_all | solution.py:469
  18.5 3.2 %first_image.1 = (f32[1,256]{1,0:T(1,128)S(1)}, f32[32,1,256]{2,1,0:T(1,128)}) custom-call(f32[1,8192]{1,0:T(1,128)S(1)} %bitcast.7, f32[11,2048]{1,0:T(8,128)S(1)} %concatenate.7.bundle_ref.refs_0_, f32[8,128]{1,0:T(8,128)S(1)} %get-tuple-element.28.after_ref, bf16[48,8192]{1,0:T(8,128)(2,1)S(1)} %get-tuple-element.27.right_ref, ...), custom_call_target="tpu_custom_call" | custom-call | flops 3000000000 | tf_op jit(solution)/shard_map/first_image/pallas_call | solution.py:544
  21.8 3.1 %all-to-all-start.1 = ((f32[32,1,256]{2,1,0:T(1,128)}), f32[32,1,256]{2,1,0:T(1,128)S(1)}, u32[]{:S(2)}, u32[]{:S(2)}) async-start(f32[32,1,256]{2,1,0:T(1,128)} %get-tuple-element.32), calls=%async_computation.1 | async-start | bytes 65536 | tf_op jit(solution)/shard_map/all_to_all | solution.py:469
  24.9 4.6 %weigh_late.1 = (bf16[40,256,1024]{2,1,0:T(8,128)(2,1)}, f32[8,128]{1,0:T(8,128)S(1)}) custom-call(s32[8,128]{1,0:T(8,128)S(1)} %get-tuple-element.24.group_ref, bf16[3072,48]{1,0:T(8,128)(2,1)S(1)} %get-tuple-element.25.left_ref, bf16[48,8192]{1,0:T(8,128)(2,1)S(1)} %get-tuple-element.27.right_ref), custom_call_target="tpu_custom_call" | custom-call | flops 4000000000 | tf_op jit(solution)/shard_map/weigh_late/pallas_call | solution.py:530
  29.5 2.6 %all-to-all-done.1 = f32[32,1,256]{2,1,0:T(1,128)S(1)} async-done(((f32[32,1,256]{2,1,0:T(1,128)}), f32[32,1,256]{2,1,0:T(1,128)S(1)}, u32[]{:S(2)}, u32[]{:S(2)}) %all-to-all-start.1) | async-done | bytes 32800 | tf_op jit(solution)/shard_map/all_to_all | solution.py:469
  32.1 3.7 %second_image.1 = (f32[2,8192]{1,0:T(2,128)S(1)}, f32[2,256]{1,0:T(2,128)S(1)}, f32[32,1,128]{2,1,0:T(1,128)}, f32[1,128]{1,0:T(1,128)S(1)}) custom-call(f32[1,8192]{1,0:T(1,128)S(1)} %bitcast.8, f32[1,8192]{1,0:T(1,128)S(1)} %bitcast.9, f32[1,256]{1,0:T(1,128)S(1)} %get-tuple-element.33.image_own_ref, f32[11,2048]{1,0:T(8,128)S(1)} %concatenate.7.bundle_ref.refs_0_, ...), custom_call_target="tpu_custom_call" | custom-call | flops 3000000000 | tf_op jit(solution)/shard_map/second_image/pallas_call | solution.py:557
  35.8 3.3 %all-to-all-start.2 = ((f32[32,1,128]{2,1,0:T(1,128)}), f32[32,1,128]{2,1,0:T(1,128)S(1)}, u32[]{:S(2)}, u32[]{:S(2)}) async-start(f32[32,1,128]{2,1,0:T(1,128)} %get-tuple-element.35), calls=%async_computation.2 | async-start | bytes 32768 | tf_op jit(solution)/shard_map/all_to_all | solution.py:469
  39.1 7.6 %block_field.1.field_ref = f32[12,2048]{1,0:T(8,128)S(1)} custom-call(s32[8,128]{1,0:T(8,128)S(1)} %get-tuple-element.24.group_ref, s32[8]{0:T(128)S(1)} %copy-done, s32[1,2048]{1,0:T(1,128)S(1)} %get-tuple-element.38.slot_ref, f32[8,8192]{1,0:T(8,128)S(1)} %get-tuple-element.29.moment_ref, f32[2,8192]{1,0:T(2,128)S(1)} %get-tuple-element.39.basis_ref, ...), custom_call_target="tpu_custom_call" | custom-call | flops 6000000000 | tf_op jit(solution)/shard_map/block_field/pallas_call | solution.py:566
  46.7 0.0 all-to-all-done.2.stats_ref
  46.8 1.0 %combine.1 = (f32[1,256]{1,0:T(1,128)}, f32[3,2048]{1,0:T(4,128)}) custom-call(f32[32,1,128]{2,1,0:T(1,128)S(1)} %all-to-all-done.2.stats_ref, f32[1,128]{1,0:T(1,128)S(1)} %get-tuple-element.36.known_ref, f32[2,256]{1,0:T(2,128)S(1)} %get-tuple-element.37.basis_own_ref, f32[12,2048]{1,0:T(8,128)S(1)} %block_field.1.field_ref, ...), custom_call_target="tpu_custom_call" | custom-call | tf_op jit(solution)/shard_map/combine/pallas_call | solution.py:577
  (15 shorter events, 0.0 us)
Async XLA Ops:
  0.6 10.8 %copy-start.2 = (f32[3,2048]{1,0:T(4,128)S(1)}, f32[3,2048]{1,0:T(4,128)}, u32[]{:S(2)}) copy-start(f32[3,2048]{1,0:T(4,128)} %tangents_hbm.1) | copy-start | bytes 73732
  0.6 10.8 %copy-start.1 = (f32[3,2048]{1,0:T(4,128)S(1)}, f32[3,2048]{1,0:T(4,128)}, u32[]{:S(2)}) copy-start(f32[3,2048]{1,0:T(4,128)} %centers_hbm.1) | copy-start | bytes 73732
  0.7 10.7 %copy-start.5 = (f32[256]{0:T(256)S(1)}, f32[256]{0:T(256)}, u32[]{:S(2)}) copy-start(f32[256]{0:T(256)} %param.7) | copy-start | bytes 3076
  0.7 10.7 %copy-start.6 = (f32[256]{0:T(256)S(1)}, f32[256]{0:T(256)}, u32[]{:S(2)}) copy-start(f32[256]{0:T(256)} %param.8) | copy-start | bytes 3076
  0.7 10.7 %copy-start.4 = (s32[2048,1]{0,1:T(1,128)S(1)}, s32[2048,1]{0,1:T(1,128)}, u32[]{:S(2)}) copy-start(s32[2048,1]{0,1:T(1,128)} %param.12) | copy-start | bytes 24580
  0.7 10.8 %copy-start.3 = (f32[3,2048]{1,0:T(4,128)S(1)}, f32[3,2048]{1,0:T(4,128)}, u32[]{:S(2)}) copy-start(f32[3,2048]{1,0:T(4,128)} %param.11) | copy-start | bytes 73732
  2.2 10.7 %collective-permute-start.2 = (f32[6,2048]{1,0:T(8,128)}, f32[6,2048]{1,0:T(8,128)S(1)}, u32[]{:S(2)}, u32[]{:S(2)}) collective-permute-start(f32[6,2048]{1,0:T(8,128)} %get-tuple-element.26), channel_id=1, source_target_pairs={{0,24},{8,0},{16,8},{24,16},{1,25},{9,1},{17,9},{25,17},{2,26},{10... | collective-permute-start | bytes 147464 | tf_op jit(solution)/shard_map/ppermute | solution.py:496
  4.6 8.3 %collective-permute-start.1 = (f32[6,2048]{1,0:T(8,128)}, f32[6,2048]{1,0:T(8,128)S(1)}, u32[]{:S(2)}, u32[]{:S(2)}) collective-permute-start(f32[6,2048]{1,0:T(8,128)} %get-tuple-element.26), channel_id=1, source_target_pairs={{0,16},{8,24},{16,0},{24,8},{1,17},{9,25},{17,1},{25,9},{2,18},{10... | collective-permute-start | bytes 147464 | tf_op jit(solution)/shard_map/ppermute | solution.py:496
  5.2 7.7 %collective-permute-start = (f32[6,2048]{1,0:T(8,128)}, f32[6,2048]{1,0:T(8,128)S(1)}, u32[]{:S(2)}, u32[]{:S(2)}) collective-permute-start(f32[6,2048]{1,0:T(8,128)} %get-tuple-element.26), channel_id=1, source_target_pairs={{0,8},{8,16},{16,24},{24,0},{1,9},{9,17},{17,25},{25,1},{2,10},{10... | collective-permute-start | bytes 147464 | tf_op jit(solution)/shard_map/ppermute | solution.py:496
  5.4 13.1 %all-to-all-start = ((f32[32,1,256]{2,1,0:T(1,128)}), f32[32,1,256]{2,1,0:T(1,128)S(1)}, u32[]{:S(2)}, u32[]{:S(2)}) async-start(f32[32,1,256]{2,1,0:T(1,128)} %get-tuple-element.23), calls=%async_computation | async-start | bytes 65536 | tf_op jit(solution)/shard_map/all_to_all | solution.py:469
  13.6 25.5 %copy-start = (s32[8]{0:T(128)S(1)}, s32[8]{0:T(128)}, u32[]{:S(2)}) copy-start(s32[8]{0:T(128)} %length_ref.1) | copy-start | bytes 100
  21.8 10.3 %all-to-all-start.1 = ((f32[32,1,256]{2,1,0:T(1,128)}), f32[32,1,256]{2,1,0:T(1,128)S(1)}, u32[]{:S(2)}, u32[]{:S(2)}) async-start(f32[32,1,256]{2,1,0:T(1,128)} %get-tuple-element.32), calls=%async_computation.1 | async-start | bytes 65536 | tf_op jit(solution)/shard_map/all_to_all | solution.py:469
  35.8 10.9 %all-to-all-start.2 = ((f32[32,1,128]{2,1,0:T(1,128)}), f32[32,1,128]{2,1,0:T(1,128)S(1)}, u32[]{:S(2)}, u32[]{:S(2)}) async-start(f32[32,1,128]{2,1,0:T(1,128)} %get-tuple-element.35), calls=%async_computation.2 | async-start | bytes 32768 | tf_op jit(solution)/shard_map/all_to_all | solution.py:469

commit v13 on v11

--- a/solution.py
+++ b/solution.py
@@ -140,7 +140,7 @@
                 acc_ref[rows] = total
         return carry
 
-    lax.fori_loop(0, vec_ref.shape[1] // TILE, step, 0, unroll=4)
+    lax.fori_loop(0, vec_ref.shape[1] // TILE, step, 0, unroll=8)
     return jnp.sum(acc_ref[...].T, axis=0, keepdims=True)
 
 

time: 47.8 us -> 47.3 us (0.990)
  Pallas kernels: 25.6 us -> 24.9 us
where the time goes in v13:
time: 47.3 us; the launch traced here: 46.9 us
  Pallas kernels  24.9 us (53%)
  starting transfers between devices  15.6 us (33%)
  waiting for transfers between devices  5.28 us (11%)
  between operations  0.87 us (2%)
    all_to_all x3, starting transfers between devices, exchange(): return lax.all_to_all(x, AXES, 0, 0, tiled=True)  12.4 us
    pallas_call x1, Pallas kernels, shards(): stream(functools.partial(field_kernel, n_row=n_row, n_col=n_col, keep=kee...  7.35 us
    pallas_call x2, Pallas kernels, weigh(): stream(functools.partial(weigh_kernel, n_row=n_row, n_col=n_col, first=fi...  6.85 us
    all_to_all x3, waiting for transfers between devices, exchange(): return lax.all_to_all(x, AXES, 0, 0, tiled=True)  5.27 us
    pallas_call x1, Pallas kernels, shards(): call(functools.partial(second_kernel, coupling), out_shape=(shape(2, segm...  3.41 us
    ppermute x3, starting transfers between devices, shards(): lax.ppermute(geometry, 'col', [(k, (k + shift) % n_col) for k in range(n_...  3.23 us
    pallas_call x1, Pallas kernels, shards(): call(functools.partial(first_kernel, coupling), out_shape=(shape(1, seg_d...  2.91 us
    pallas_call x1, Pallas kernels, shards(): pl.pallas_call(entry_kernel, out_shape=(shape(n_dev, 1, seg_dev), shape(6...  1.47 us
  transfers between devices with their start and end apart: 6, of which 2 were waited for; matrix products, arithmetic and copies ran while one was open for 1% of the time, Pallas kernels for 34%

profile of v13, /device:TPU:0, one launch (start us, length us, event | category | flops | bytes accessed | tf_op | source)
XLA Modules:
  0.0 46.9 jit_solution(1451545746589385620)
XLA Ops:
  0.6 0.0 copy-start.2
  0.7 1.5 %entry.1 = (f32[32,1,256]{2,1,0:T(1,128)}, f32[6,2048]{1,0:T(8,128)}) custom-call(f32[1,256]{1,0:T(1,128)} %bitcast.11, f32[3,2048]{1,0:T(4,128)} %centers_hbm.1, f32[3,2048]{1,0:T(4,128)} %tangents_hbm.1), custom_call_target="tpu_custom_call" | custom-call | flops 8000000000 | tf_op jit(solution)/shard_map/entry/pallas_call | solution.py:471
  2.2 2.4 %collective-permute-start.2 = (f32[6,2048]{1,0:T(8,128)}, f32[6,2048]{1,0:T(8,128)S(1)}, u32[]{:S(2)}, u32[]{:S(2)}) collective-permute-start(f32[6,2048]{1,0:T(8,128)} %get-tuple-element.26), channel_id=1, source_target_pairs={{0,24},{8,0},{16,8},{24,16},{1,25},{9,1},{17,9},{25,17},{2,26},{10... | collective-permute-start | bytes 147464 | tf_op jit(solution)/shard_map/ppermute | solution.py:496
  4.6 0.6 %collective-permute-start.1 = (f32[6,2048]{1,0:T(8,128)}, f32[6,2048]{1,0:T(8,128)S(1)}, u32[]{:S(2)}, u32[]{:S(2)}) collective-permute-start(f32[6,2048]{1,0:T(8,128)} %get-tuple-element.26), channel_id=1, source_target_pairs={{0,16},{8,24},{16,0},{24,8},{1,17},{9,25},{17,1},{25,9},{2,18},{10... | collective-permute-start | bytes 147464 | tf_op jit(solution)/shard_map/ppermute | solution.py:496
  5.2 0.2 collective-permute-start
  5.4 5.9 %all-to-all-start = ((f32[32,1,256]{2,1,0:T(1,128)}), f32[32,1,256]{2,1,0:T(1,128)S(1)}, u32[]{:S(2)}, u32[]{:S(2)}) async-start(f32[32,1,256]{2,1,0:T(1,128)} %get-tuple-element.23), calls=%async_computation | async-start | bytes 65536 | tf_op jit(solution)/shard_map/all_to_all | solution.py:469
  11.5 0.2 concatenate.7.bundle_ref.refs_0_
  11.7 1.2 %group_points.1 = (s32[1,2048]{1,0:T(1,128)S(1)}, s32[8,128]{1,0:T(8,128)S(1)}, bf16[3072,48]{1,0:T(8,128)(2,1)S(1)}) custom-call(f32[11,2048]{1,0:T(8,128)S(1)} %concatenate.7.bundle_ref.refs_0_), custom_call_target="tpu_custom_call" | custom-call | flops 3000000000 | tf_op jit(solution)/shard_map/group_points/pallas_call | solution.py:501
  12.9 0.0 collective-permute-done.2.refs_3_
  12.9 0.0 collective-permute-done.1.refs_2_
  12.9 0.0 collective-permute-done.refs_1_
  12.9 0.6 %sides.1 = (bf16[48,8192]{1,0:T(8,128)(2,1)S(1)}, f32[8,8192]{1,0:T(8,128)S(1)}, bf16[2,256,48]{2,1,0:T(8,128)(2,1)S(1)}, f32[3,256,128]{2,1,0:T(8,128)S(1)}) custom-call(f32[11,2048]{1,0:T(8,128)S(1)} %concatenate.7.bundle_ref.refs_0_, f32[6,2048]{1,0:T(8,128)S(1)} %collective-permute-done.refs_1_, f32[6,2048]{1,0:T(8,128)S(1)} %collective-permute-done.1.refs_2_, ...), custom_call_target="tpu_custom_call" | custom-call | flops 1000000000 | tf_op jit(solution)/shard_map/sides/pallas_call | solution.py:518
  13.6 0.0 copy-start
  13.6 3.0 %weigh_early.1 = (bf16[40,256,1024]{2,1,0:T(8,128)(2,1)}, f32[8,128]{1,0:T(8,128)S(1)}) custom-call(s32[8,128]{1,0:T(8,128)S(1)} %get-tuple-element.24.group_ref, bf16[3072,48]{1,0:T(8,128)(2,1)S(1)} %get-tuple-element.25.left_ref, bf16[48,8192]{1,0:T(8,128)(2,1)S(1)} %get-tuple-element.27.right_ref), custom_call_target="tpu_custom_call" | custom-call | flops 2000000000 | tf_op jit(solution)/shard_map/weigh_early/pallas_call | solution.py:530
  16.6 2.0 %all-to-all-done = f32[32,1,256]{2,1,0:T(1,128)S(1)} async-done(((f32[32,1,256]{2,1,0:T(1,128)}), f32[32,1,256]{2,1,0:T(1,128)S(1)}, u32[]{:S(2)}, u32[]{:S(2)}) %all-to-all-start) | async-done | bytes 32800 | tf_op jit(solution)/shard_map/all_to_all | solution.py:469
  18.5 2.9 %first_image.1 = (f32[1,256]{1,0:T(1,128)S(1)}, f32[32,1,256]{2,1,0:T(1,128)}) custom-call(f32[1,8192]{1,0:T(1,128)S(1)} %bitcast.7, f32[11,2048]{1,0:T(8,128)S(1)} %concatenate.7.bundle_ref.refs_0_, f32[8,128]{1,0:T(8,128)S(1)} %get-tuple-element.28.after_ref, bf16[48,8192]{1,0:T(8,128)(2,1)S(1)} %get-tuple-element.27.right_ref, ...), custom_call_target="tpu_custom_call" | custom-call | flops 3000000000 | tf_op jit(solution)/shard_map/first_image/pallas_call | solution.py:544
  21.5 3.9 %all-to-all-start.1 = ((f32[32,1,256]{2,1,0:T(1,128)}), f32[32,1,256]{2,1,0:T(1,128)S(1)}, u32[]{:S(2)}, u32[]{:S(2)}) async-start(f32[32,1,256]{2,1,0:T(1,128)} %get-tuple-element.32), calls=%async_computation.1 | async-start | bytes 65536 | tf_op jit(solution)/shard_map/all_to_all | solution.py:469
  25.3 3.9 %weigh_late.1 = (bf16[40,256,1024]{2,1,0:T(8,128)(2,1)}, f32[8,128]{1,0:T(8,128)S(1)}) custom-call(s32[8,128]{1,0:T(8,128)S(1)} %get-tuple-element.24.group_ref, bf16[3072,48]{1,0:T(8,128)(2,1)S(1)} %get-tuple-element.25.left_ref, bf16[48,8192]{1,0:T(8,128)(2,1)S(1)} %get-tuple-element.27.right_ref), custom_call_target="tpu_custom_call" | custom-call | flops 4000000000 | tf_op jit(solution)/shard_map/weigh_late/pallas_call | solution.py:530
  29.2 3.3 %all-to-all-done.1 = f32[32,1,256]{2,1,0:T(1,128)S(1)} async-done(((f32[32,1,256]{2,1,0:T(1,128)}), f32[32,1,256]{2,1,0:T(1,128)S(1)}, u32[]{:S(2)}, u32[]{:S(2)}) %all-to-all-start.1) | async-done | bytes 32800 | tf_op jit(solution)/shard_map/all_to_all | solution.py:469
  32.5 3.4 %second_image.1 = (f32[2,8192]{1,0:T(2,128)S(1)}, f32[2,256]{1,0:T(2,128)S(1)}, f32[32,1,128]{2,1,0:T(1,128)}, f32[1,128]{1,0:T(1,128)S(1)}) custom-call(f32[1,8192]{1,0:T(1,128)S(1)} %bitcast.8, f32[1,8192]{1,0:T(1,128)S(1)} %bitcast.9, f32[1,256]{1,0:T(1,128)S(1)} %get-tuple-element.33.image_own_ref, f32[11,2048]{1,0:T(8,128)S(1)} %concatenate.7.bundle_ref.refs_0_, ...), custom_call_target="tpu_custom_call" | custom-call | flops 3000000000 | tf_op jit(solution)/shard_map/second_image/pallas_call | solution.py:557
  35.9 2.6 %all-to-all-start.2 = ((f32[32,1,128]{2,1,0:T(1,128)}), f32[32,1,128]{2,1,0:T(1,128)S(1)}, u32[]{:S(2)}, u32[]{:S(2)}) async-start(f32[32,1,128]{2,1,0:T(1,128)} %get-tuple-element.35), calls=%async_computation.2 | async-start | bytes 32768 | tf_op jit(solution)/shard_map/all_to_all | solution.py:469
  38.5 7.4 %block_field.1.field_ref = f32[12,2048]{1,0:T(8,128)S(1)} custom-call(s32[8,128]{1,0:T(8,128)S(1)} %get-tuple-element.24.group_ref, s32[8]{0:T(128)S(1)} %copy-done, s32[1,2048]{1,0:T(1,128)S(1)} %get-tuple-element.38.slot_ref, f32[8,8192]{1,0:T(8,128)S(1)} %get-tuple-element.29.moment_ref, f32[2,8192]{1,0:T(2,128)S(1)} %get-tuple-element.39.basis_ref, ...), custom_call_target="tpu_custom_call" | custom-call | flops 6000000000 | tf_op jit(solution)/shard_map/block_field/pallas_call | solution.py:566
  45.9 0.0 all-to-all-done.2.stats_ref
  45.9 1.0 %combine.1 = (f32[1,256]{1,0:T(1,128)}, f32[3,2048]{1,0:T(4,128)}) custom-call(f32[32,1,128]{2,1,0:T(1,128)S(1)} %all-to-all-done.2.stats_ref, f32[1,128]{1,0:T(1,128)S(1)} %get-tuple-element.36.known_ref, f32[2,256]{1,0:T(2,128)S(1)} %get-tuple-element.37.basis_own_ref, f32[12,2048]{1,0:T(8,128)S(1)} %block_field.1.field_ref, ...), custom_call_target="tpu_custom_call" | custom-call | tf_op jit(solution)/shard_map/combine/pallas_call | solution.py:577
  (15 shorter events, 0.0 us)
Async XLA Ops:
  0.6 10.8 %copy-start.2 = (f32[3,2048]{1,0:T(4,128)S(1)}, f32[3,2048]{1,0:T(4,128)}, u32[]{:S(2)}) copy-start(f32[3,2048]{1,0:T(4,128)} %tangents_hbm.1) | copy-start | bytes 73732
  0.6 10.8 %copy-start.1 = (f32[3,2048]{1,0:T(4,128)S(1)}, f32[3,2048]{1,0:T(4,128)}, u32[]{:S(2)}) copy-start(f32[3,2048]{1,0:T(4,128)} %centers_hbm.1) | copy-start | bytes 73732
  0.7 10.7 %copy-start.5 = (f32[256]{0:T(256)S(1)}, f32[256]{0:T(256)}, u32[]{:S(2)}) copy-start(f32[256]{0:T(256)} %param.7) | copy-start | bytes 3076
  0.7 10.7 %copy-start.6 = (f32[256]{0:T(256)S(1)}, f32[256]{0:T(256)}, u32[]{:S(2)}) copy-start(f32[256]{0:T(256)} %param.8) | copy-start | bytes 3076
  0.7 10.7 %copy-start.4 = (s32[2048,1]{0,1:T(1,128)S(1)}, s32[2048,1]{0,1:T(1,128)}, u32[]{:S(2)}) copy-start(s32[2048,1]{0,1:T(1,128)} %param.12) | copy-start | bytes 24580
  0.7 10.8 %copy-start.3 = (f32[3,2048]{1,0:T(4,128)S(1)}, f32[3,2048]{1,0:T(4,128)}, u32[]{:S(2)}) copy-start(f32[3,2048]{1,0:T(4,128)} %param.11) | copy-start | bytes 73732
  2.2 10.7 %collective-permute-start.2 = (f32[6,2048]{1,0:T(8,128)}, f32[6,2048]{1,0:T(8,128)S(1)}, u32[]{:S(2)}, u32[]{:S(2)}) collective-permute-start(f32[6,2048]{1,0:T(8,128)} %get-tuple-element.26), channel_id=1, source_target_pairs={{0,24},{8,0},{16,8},{24,16},{1,25},{9,1},{17,9},{25,17},{2,26},{10... | collective-permute-start | bytes 147464 | tf_op jit(solution)/shard_map/ppermute | solution.py:496
  4.6 8.3 %collective-permute-start.1 = (f32[6,2048]{1,0:T(8,128)}, f32[6,2048]{1,0:T(8,128)S(1)}, u32[]{:S(2)}, u32[]{:S(2)}) collective-permute-start(f32[6,2048]{1,0:T(8,128)} %get-tuple-element.26), channel_id=1, source_target_pairs={{0,16},{8,24},{16,0},{24,8},{1,17},{9,25},{17,1},{25,9},{2,18},{10... | collective-permute-start | bytes 147464 | tf_op jit(solution)/shard_map/ppermute | solution.py:496
  5.2 7.7 %collective-permute-start = (f32[6,2048]{1,0:T(8,128)}, f32[6,2048]{1,0:T(8,128)S(1)}, u32[]{:S(2)}, u32[]{:S(2)}) collective-permute-start(f32[6,2048]{1,0:T(8,128)} %get-tuple-element.26), channel_id=1, source_target_pairs={{0,8},{8,16},{16,24},{24,0},{1,9},{9,17},{17,25},{25,1},{2,10},{10... | collective-permute-start | bytes 147464 | tf_op jit(solution)/shard_map/ppermute | solution.py:496
  5.4 13.1 %all-to-all-start = ((f32[32,1,256]{2,1,0:T(1,128)}), f32[32,1,256]{2,1,0:T(1,128)S(1)}, u32[]{:S(2)}, u32[]{:S(2)}) async-start(f32[32,1,256]{2,1,0:T(1,128)} %get-tuple-element.23), calls=%async_computation | async-start | bytes 65536 | tf_op jit(solution)/shard_map/all_to_all | solution.py:469
  13.6 24.9 %copy-start = (s32[8]{0:T(128)S(1)}, s32[8]{0:T(128)}, u32[]{:S(2)}) copy-start(s32[8]{0:T(128)} %length_ref.1) | copy-start | bytes 100
  21.5 11.1 %all-to-all-start.1 = ((f32[32,1,256]{2,1,0:T(1,128)}), f32[32,1,256]{2,1,0:T(1,128)S(1)}, u32[]{:S(2)}, u32[]{:S(2)}) async-start(f32[32,1,256]{2,1,0:T(1,128)} %get-tuple-element.32), calls=%async_computation.1 | async-start | bytes 65536 | tf_op jit(solution)/shard_map/all_to_all | solution.py:469
  35.9 9.9 %all-to-all-start.2 = ((f32[32,1,128]{2,1,0:T(1,128)}), f32[32,1,128]{2,1,0:T(1,128)S(1)}, u32[]{:S(2)}, u32[]{:S(2)}) async-start(f32[32,1,128]{2,1,0:T(1,128)} %get-tuple-element.35), calls=%async_computation.2 | async-start | bytes 32768 | tf_op jit(solution)/shard_map/all_to_all | solution.py:469
